TPU v7x, 32 devices: a whole 2x2x4 slice. The times are simulated.
32 devices in a mesh: region: 8 (over y, x, core), industry: 4 (over z).
Axes of the slice: x: 2, y: 2, z: 4, core: 2. Of those that a mesh axis runs over, the one named last changes fastest.
Arguments:
- position: bfloat16 [8, 1536, 16, 1024], P(None, 'region', None, 'industry'), may hold values from 0.049804688 to 0.94921875
- dual_lower: bfloat16 [8, 1536, 16, 1024], P(None, 'region', None, 'industry'), may hold values from 0.099609375 to 10
- dual_upper: bfloat16 [8, 1536, 16, 1024], P(None, 'region', None, 'industry'), may hold values from 0.099609375 to 10
- upper_bound: int32 [1536, 16, 1024], P('region', None, 'industry'), may hold values from 2 to 63
- suppressed: int32 [1536, 16, 1024], P('region', None, 'industry'), may hold values from 0 to 1
- attack_region: int32 [8], replicated, may hold values from 0 to 1535
- attack_column: int32 [8], replicated, may hold values from 0 to 16383
- dual_row: float32 [8, 1536, 16], P(None, 'region'), may hold values from -3 to 3
- dual_col: float32 [8, 16, 1024], P(None, None, 'industry'), may hold values from -3 to 3
Outputs:
- cell_step: bfloat16 [8, 1536, 16, 1024], P(None, 'region', None, 'industry')
- row_step: float32 [8, 1536, 16], P(None, 'region')
- col_step: float32 [8, 16, 1024], P(None, None, 'industry')
All inputs are finite; a program needn't handle non-finite values.
Results may differ from a plain program's by a relative error of at most 0.001.
Values sent between devices are 32-bit elements; how exact they have to be, the bound alone decides.
No kernel may reach another device: no remote copies, remote signals or barrier semaphores. Data moves between devices by JAX's collectives and lax.ppermute only.
A program may use at most 128 MiB of HBM per device.

v0:
```python
import jax
import jax.numpy as jnp
from jax import lax
from jax.sharding import PartitionSpec as P

ITERS = 3


weight_attack = 8.0
barrier = 0.5
shift_diag = 1.0


def row_margin(partial_value):
    return lax.psum(partial_value, "industry")


def col_margin(partial_value):
    return lax.psum(partial_value, "region")


def couple(scaling, part_row, part_col):
    left = row_margin(jnp.sum(scaling * part_col[:, None, :, :], axis=3))
    right = col_margin(jnp.sum(scaling * part_row[..., None], axis=1))
    return (left, right)


def local_pair(first_row, second_row, first_col, second_col):
    row_flag = (lax.axis_index("industry") == 0).astype(jnp.float32)
    col_flag = (lax.axis_index("region") == 0).astype(jnp.float32)
    return row_flag * jnp.sum(first_row * second_row, axis=(1, 2)) + col_flag * jnp.sum(
        first_col * second_col, axis=(1, 2)
    )


def inner_pair(first_row, second_row, first_col, second_col):
    return lax.psum(
        local_pair(first_row, second_row, first_col, second_col), ("region", "industry")
    )


def local(
    position,
    dual_lower,
    dual_upper,
    upper_bound,
    suppressed,
    attack_region,
    attack_column,
    dual_row,
    dual_col,
):
    rows_local = upper_bound.shape[0]
    sizes_count = upper_bound.shape[1]
    inds_local = upper_bound.shape[2]
    inds_total = inds_local * lax.axis_size("industry")
    region_ids = lax.axis_index("region") * rows_local + jnp.arange(rows_local, dtype=jnp.int32)
    column_ids = (
        jnp.arange(sizes_count, dtype=jnp.int32)[:, None] * inds_total
        + lax.axis_index("industry") * inds_local
        + jnp.arange(inds_local, dtype=jnp.int32)[None, :]
    )
    attacked = (region_ids[None, :, None, None] == attack_region[:, None, None, None]) & (
        column_ids[None, None] == attack_column[:, None, None, None]
    )
    active = jnp.maximum(suppressed[None], attacked.astype(jnp.int32)).astype(jnp.float32)
    upper = upper_bound.astype(jnp.float32)[None]
    value = position.astype(jnp.float32) * upper
    slack = upper - value
    scaling = active / (
        dual_lower.astype(jnp.float32) / value + dual_upper.astype(jnp.float32) / slack
    )
    gradient = (
        jnp.where(attacked, jnp.float32(weight_attack), jnp.float32(0.0))
        - dual_row[..., None]
        - dual_col[:, None]
        + barrier * (1.0 / value - 1.0 / slack)
    )
    margin_term = active * (0.5 * upper - value) + scaling * gradient
    res_row, diag_row = row_margin((jnp.sum(margin_term, axis=3), jnp.sum(scaling, axis=3)))
    res_col, diag_col = col_margin((jnp.sum(margin_term, axis=1), jnp.sum(scaling, axis=1)))
    diag_row = diag_row + shift_diag
    diag_col = diag_col + shift_diag

    def precondition(vec_row, vec_col):
        base_row, base_col = (vec_row / diag_row, vec_col / diag_col)
        once_row, once_col = couple(scaling, base_row, base_col)
        once_row, once_col = (once_row / diag_row, once_col / diag_col)
        twice_row, twice_col = couple(scaling, once_row, once_col)
        twice_row, twice_col = (twice_row / diag_row, twice_col / diag_col)
        pre_row = base_row - once_row + twice_row
        pre_col = base_col - once_col + twice_col
        rz_value = inner_pair(vec_row, pre_row, vec_col, pre_col)
        return (pre_row, pre_col, rz_value)

    pre_row, pre_col, rz_now = precondition(res_row, res_col)
    dir_row, dir_col = (pre_row, pre_col)
    sol_row = jnp.zeros_like(res_row)
    sol_col = jnp.zeros_like(res_col)
    for iteration in range(ITERS):
        image_row, image_col = couple(scaling, dir_row, dir_col)
        image_row = diag_row * dir_row + image_row
        image_col = diag_col * dir_col + image_col
        curvature_sum = inner_pair(dir_row, image_row, dir_col, image_col)
        step_len = (rz_now / curvature_sum)[:, None, None]
        sol_row = sol_row + step_len * dir_row
        sol_col = sol_col + step_len * dir_col
        res_row = res_row - step_len * image_row
        res_col = res_col - step_len * image_col
        if iteration + 1 < ITERS:
            pre_row, pre_col, rz_next = precondition(res_row, res_col)
            step_ratio = (rz_next / rz_now)[:, None, None]
            dir_row = pre_row + step_ratio * dir_row
            dir_col = pre_col + step_ratio * dir_col
            rz_now = rz_next
    cell_step = (scaling * (sol_row[..., None] + sol_col[:, None] - gradient)).astype(jnp.bfloat16)
    return (cell_step, sol_row, sol_col)


def solution(mesh):
    placed = (
        P(None, "region", None, "industry"),
        P(None, "region", None, "industry"),
        P(None, "region", None, "industry"),
        P("region", None, "industry"),
        P("region", None, "industry"),
        P(),
        P(),
        P(None, "region", None),
        P(None, None, "industry"),
    )
    return jax.shard_map(
        local,
        mesh=mesh,
        in_specs=placed,
        out_specs=(
            P(None, "region", None, "industry"),
            P(None, "region", None),
            P(None, None, "industry"),
        ),
        check_vma=False,
    )
```

profile of v0, /device:TPU:0, one launch (start us, length us, event | category | flops | bytes accessed | tf_op | source)
XLA Modules:
  0.0 1469.8 jit_solution(369653928913397408)
XLA Ops:
  18.0 32.5 %fusion.22 = (f32[8,192,16]{2,1,0:T(8,128)}, f32[8,16,256]{2,1,0:T(8,128)}, f32[8,192,16,256]{3,2,1,0:T(8,128)}) fusion(bf16[8,192,16,256]{3,2,1,0:T(8,128)(2,1)} %param.11, f32[192,16,256]{2,1,0:T(8,128)} %convert_element_type.41, bf16[8,192,16,256]{3,2,1,0:T(8,128)(2,1)} %param.9, bf16[8,192,16,256]{3,2,1,0:T(8,128)(2,1)} %param.10, ...), kind=kLoop, calls=%fused_computation.90 | loop fusion | flops 94314496 | bytes 69469696 | tf_op jit(solution)/shard_map/reduce_sum | solution.py:80
  50.5 32.9 %fusion.21 = (f32[8,192,16]{2,1,0:T(8,128)}, f32[8,16,256]{2,1,0:T(8,128)}) fusion(f32[8,192,16,256]{3,2,1,0:T(8,128)} %get-tuple-element.54, f32[8,16,256]{2,1,0:T(8,128)S(1)} %copy-done.10, f32[8,192,16]{2,1,0:T(8,128)S(1)} %copy.23, f32[192,16,256]{2,1,0:T(8,128)S(1)} %copy-done.1, bf16[8,192,16,256]{3,2,1,0:T(8,128)(2,1)} %param.9, ...), kind=kLoop, calls=%fused_computation.89 | loop fusion | flops 132063232 | bytes 47678976 | tf_op jit(solution)/shard_map/reduce_sum | solution.py:80
  84.2 55.7 %all-reduce.60.cloned.1.call-done = (f32[8,16,256]{2,1,0:T(8,128)}, f32[8,16,256]{2,1,0:T(8,128)}) async-done(((f32[8,16,256]{2,1,0:T(8,128)}, f32[8,16,256]{2,1,0:T(8,128)}), (f32[8,16,256]{2,1,0:T(8,128)}, f32[8,16,256]{2,1,0:T(8,128)})) %all-reduce.60.cloned.1.call-update) | async-done | bytes 262160 | tf_op jit(solution)/shard_map/psum | solution.py:19
  140.9 70.4 %all-reduce.62.cloned.1.call-done = (f32[8,192,16]{2,1,0:T(8,128)}, f32[8,192,16]{2,1,0:T(8,128)}) async-done(((f32[8,192,16]{2,1,0:T(8,128)}, f32[8,192,16]{2,1,0:T(8,128)}), (f32[8,192,16]{2,1,0:T(8,128)}, f32[8,192,16]{2,1,0:T(8,128)})) %all-reduce.62.cloned.1.call-update) | async-done | bytes 196624 | tf_op jit(solution)/shard_map/psum | solution.py:15
  212.9 13.0 multiply_reduce_fusion.16
  226.5 51.5 %all-reduce.26.cloned.1.call-done = f32[8,16,256]{2,1,0:T(8,128)} async-done(((f32[8,16,256]{2,1,0:T(8,128)}), f32[8,16,256]{2,1,0:T(8,128)}) %all-reduce.26.cloned.1.call-update) | async-done | bytes 131088 | tf_op jit(solution)/shard_map/psum | solution.py:19
  279.0 44.9 %all-reduce.24.cloned.1.call-done = f32[8,192,16]{2,1,0:T(8,128)} async-done(((f32[8,192,16]{2,1,0:T(8,128)}), f32[8,192,16]{2,1,0:T(8,128)}) %all-reduce.24.cloned.1.call-update) | async-done | bytes 98320 | tf_op jit(solution)/shard_map/psum | solution.py:15
  338.8 51.8 %all-reduce.30.cloned.1.call-done = f32[8,16,256]{2,1,0:T(8,128)} async-done(((f32[8,16,256]{2,1,0:T(8,128)}), f32[8,16,256]{2,1,0:T(8,128)}) %all-reduce.30.cloned.1.call-update) | async-done | bytes 131088 | tf_op jit(solution)/shard_map/psum | solution.py:19
  391.6 45.0 %all-reduce.28.cloned.1.call-done = f32[8,192,16]{2,1,0:T(8,128)} async-done(((f32[8,192,16]{2,1,0:T(8,128)}), f32[8,192,16]{2,1,0:T(8,128)}) %all-reduce.28.cloned.1.call-update) | async-done | bytes 98320 | tf_op jit(solution)/shard_map/psum | solution.py:15
  451.7 51.6 %all-reduce.34.cloned.1.call-done = f32[8,16,256]{2,1,0:T(8,128)} async-done(((f32[8,16,256]{2,1,0:T(8,128)}), f32[8,16,256]{2,1,0:T(8,128)}) %all-reduce.34.cloned.1.call-update) | async-done | bytes 131088 | tf_op jit(solution)/shard_map/psum | solution.py:19
  504.3 45.0 %all-reduce.32.cloned.1.call-done = f32[8,192,16]{2,1,0:T(8,128)} async-done(((f32[8,192,16]{2,1,0:T(8,128)}), f32[8,192,16]{2,1,0:T(8,128)}) %all-reduce.32.cloned.1.call-update) | async-done | bytes 98320 | tf_op jit(solution)/shard_map/psum | solution.py:15
  550.8 40.0 %all-reduce = (f32[8]{0:T(128)S(1)}, f32[8]{0:T(128)S(1)}) all-reduce(f32[8]{0:T(128)S(1)} %get-tuple-element.56, f32[8]{0:T(128)S(1)} %get-tuple-element.55), channel_id=1, replica_groups=mesh['region'=8,'industry'=4] {'region','industry'}, use_global_device_ids=true, to_apply=%region_18.19 | all-reduce | flops 16 | bytes 128 | tf_op jit(solution)/shard_map/psum | solution.py:37
  607.4 51.6 %all-reduce.38.cloned.1.call-done = f32[8,16,256]{2,1,0:T(8,128)} async-done(((f32[8,16,256]{2,1,0:T(8,128)}), f32[8,16,256]{2,1,0:T(8,128)}) %all-reduce.38.cloned.1.call-update) | async-done | bytes 131088 | tf_op jit(solution)/shard_map/psum | solution.py:19
  660.7 44.4 %all-reduce.36.cloned.1.call-done = f32[8,192,16]{2,1,0:T(8,128)} async-done(((f32[8,192,16]{2,1,0:T(8,128)}), f32[8,192,16]{2,1,0:T(8,128)}) %all-reduce.36.cloned.1.call-update) | async-done | bytes 98320 | tf_op jit(solution)/shard_map/psum | solution.py:15
  706.4 13.0 multiply_reduce_fusion.9
  720.0 51.8 %all-reduce.42.cloned.1.call-done = f32[8,16,256]{2,1,0:T(8,128)} async-done(((f32[8,16,256]{2,1,0:T(8,128)}), f32[8,16,256]{2,1,0:T(8,128)}) %all-reduce.42.cloned.1.call-update) | async-done | bytes 131088 | tf_op jit(solution)/shard_map/psum | solution.py:19
  773.5 44.2 %all-reduce.40.cloned.1.call-done = f32[8,192,16]{2,1,0:T(8,128)} async-done(((f32[8,192,16]{2,1,0:T(8,128)}), f32[8,192,16]{2,1,0:T(8,128)}) %all-reduce.40.cloned.1.call-update) | async-done | bytes 98320 | tf_op jit(solution)/shard_map/psum | solution.py:15
  819.9 39.8 %psum.212 = f32[8]{0:T(128)S(1)} all-reduce(f32[8]{0:T(128)S(1)} %multiply_add_fusion.13), channel_id=1, replica_groups=mesh['region'=8,'industry'=4] {'region','industry'}, use_global_device_ids=true, to_apply=%region_36.37 | all-reduce | flops 8 | bytes 64 | tf_op jit(solution)/shard_map/psum | solution.py:37
  876.1 51.7 %all-reduce.46.cloned.1.call-done = f32[8,16,256]{2,1,0:T(8,128)} async-done(((f32[8,16,256]{2,1,0:T(8,128)}), f32[8,16,256]{2,1,0:T(8,128)}) %all-reduce.46.cloned.1.call-update) | async-done | bytes 131088 | tf_op jit(solution)/shard_map/psum | solution.py:19
  928.9 44.9 %all-reduce.44.cloned.1.call-done = f32[8,192,16]{2,1,0:T(8,128)} async-done(((f32[8,192,16]{2,1,0:T(8,128)}), f32[8,192,16]{2,1,0:T(8,128)}) %all-reduce.44.cloned.1.call-update) | async-done | bytes 98320 | tf_op jit(solution)/shard_map/psum | solution.py:15
  975.2 39.8 %psum.215 = f32[8]{0:T(128)} all-reduce(f32[8]{0:T(128)S(1)} %multiply_add_fusion.12), channel_id=1, replica_groups=mesh['region'=8,'industry'=4] {'region','industry'}, use_global_device_ids=true, to_apply=%region_43.44 | all-reduce | flops 8 | bytes 64 | tf_op jit(solution)/shard_map/psum | solution.py:37
  1019.7 13.0 multiply_reduce_fusion.4
  1033.3 51.9 %all-reduce.50.cloned.1.call-done = f32[8,16,256]{2,1,0:T(8,128)} async-done(((f32[8,16,256]{2,1,0:T(8,128)}), f32[8,16,256]{2,1,0:T(8,128)}) %all-reduce.50.cloned.1.call-update) | async-done | bytes 131088 | tf_op jit(solution)/shard_map/psum | solution.py:19
  1086.8 43.7 %all-reduce.48.cloned.1.call-done = f32[8,192,16]{2,1,0:T(8,128)} async-done(((f32[8,192,16]{2,1,0:T(8,128)}), f32[8,192,16]{2,1,0:T(8,128)}) %all-reduce.48.cloned.1.call-update) | async-done | bytes 98320 | tf_op jit(solution)/shard_map/psum | solution.py:15
  1131.7 13.0 multiply_reduce_fusion.3
  1145.4 51.8 %all-reduce.54.cloned.1.call-done = f32[8,16,256]{2,1,0:T(8,128)} async-done(((f32[8,16,256]{2,1,0:T(8,128)}), f32[8,16,256]{2,1,0:T(8,128)}) %all-reduce.54.cloned.1.call-update) | async-done | bytes 131088 | tf_op jit(solution)/shard_map/psum | solution.py:19
  1198.4 44.2 %all-reduce.52.cloned.1.call-done = f32[8,192,16]{2,1,0:T(8,128)} async-done(((f32[8,192,16]{2,1,0:T(8,128)}), f32[8,192,16]{2,1,0:T(8,128)}) %all-reduce.52.cloned.1.call-update) | async-done | bytes 98320 | tf_op jit(solution)/shard_map/psum | solution.py:15
  1245.4 40.0 %psum.220 = f32[8]{0:T(128)S(1)} all-reduce(f32[8]{0:T(128)S(1)} %multiply_add_fusion.11), channel_id=1, replica_groups=mesh['region'=8,'industry'=4] {'region','industry'}, use_global_device_ids=true, to_apply=%region_54.55 | all-reduce | flops 8 | bytes 64 | tf_op jit(solution)/shard_map/psum | solution.py:37
  1300.8 51.7 %all-reduce.58.cloned.1.call-done = f32[8,16,256]{2,1,0:T(8,128)} async-done(((f32[8,16,256]{2,1,0:T(8,128)}), f32[8,16,256]{2,1,0:T(8,128)}) %all-reduce.58.cloned.1.call-update) | async-done | bytes 131088 | tf_op jit(solution)/shard_map/psum | solution.py:19
  1353.6 44.7 %all-reduce.56.cloned.1.call-done = f32[8,192,16]{2,1,0:T(8,128)} async-done(((f32[8,192,16]{2,1,0:T(8,128)}), f32[8,192,16]{2,1,0:T(8,128)}) %all-reduce.56.cloned.1.call-update) | async-done | bytes 98320 | tf_op jit(solution)/shard_map/psum | solution.py:15
  1399.8 39.8 %psum.223 = f32[8]{0:T(128)S(1)} all-reduce(f32[8]{0:T(128)S(1)} %multiply_add_fusion.10), channel_id=1, replica_groups=mesh['region'=8,'industry'=4] {'region','industry'}, use_global_device_ids=true, to_apply=%region_61.62 | all-reduce | flops 8 | bytes 64 | tf_op jit(solution)/shard_map/psum | solution.py:37
  1442.4 20.5 %multiply_convert_fusion = bf16[8,192,16,256]{3,2,1,0:T(8,128)(2,1)} fusion(f32[8,192,16,256]{3,2,1,0:T(8,128)} %get-tuple-element.54, f32[8,16,256]{2,1,0:T(8,128)S(1)} %multiply_add_fusion.5, f32[8,192,16]{2,1,0:T(8,128)S(1)} %multiply_add_fusion, f32[192,16,256]{2,1,0:T(8,128)} %convert_element_type.41, bf16[8,192,16,256]{3,2,1,0:T(8,128)(2,1)} %param.9, ...), kind=kLoop, calls=%fused_computation.10 | loop fusion | flops 100663296 | bytes 53970432 | tf_op jit(solution)/shard_map/convert_element_type | solution.py:116
  (126 shorter events, 125.4 us)
Async XLA Ops:
  7.2 132.7 %all-reduce.60.cloned.1.call-start = ((), (), s32[]{:S(2)}) async-start(), calls=%async_computation.18 | async-start | bytes 524288 | tf_op jit(solution)/shard_map/psum | solution.py:19
  16.4 34.1 %copy-start.4 = (f32[8,192,16]{2,1,0:T(8,128)}, f32[8,192,16]{2,1,0:T(8,128)S(1)}, u32[]{:S(2)}) copy-start(f32[8,192,16]{2,1,0:T(8,128)S(1)} %copy.23) | copy-start | bytes 294916
  17.9 32.5 %copy-start.12 = (pred[8,16,256]{2,1,0:T(8,128)(4,1)}, pred[8,16,256]{2,1,0:T(8,128)(4,1)S(1)}, u32[]{:S(2)}) copy-start(pred[8,16,256]{2,1,0:T(8,128)(4,1)S(1)} %broadcast_compare_fusion) | copy-start | bytes 98308
  17.9 32.5 %copy-start.1 = (f32[192,16,256]{2,1,0:T(8,128)S(1)}, f32[192,16,256]{2,1,0:T(8,128)}, u32[]{:S(2)}) copy-start(f32[192,16,256]{2,1,0:T(8,128)} %convert_element_type.41) | copy-start | bytes 9437188
  18.0 32.5 %copy-start.10 = (f32[8,16,256]{2,1,0:T(8,128)S(1)}, f32[8,16,256]{2,1,0:T(8,128)}, u32[]{:S(2)}) copy-start(f32[8,16,256]{2,1,0:T(8,128)} %param.17) | copy-start | bytes 393220
  83.4 127.9 %all-reduce.62.cloned.1.call-start = ((), (), s32[]{:S(2)}) async-start(), calls=%async_computation.19 | async-start | bytes 3145728 | tf_op jit(solution)/shard_map/psum | solution.py:15
  84.1 193.9 %all-reduce.26.cloned.1.call-start = ((), (), s32[]{:S(2)}) async-start(), calls=%async_computation.1 | async-start | bytes 262144 | tf_op jit(solution)/shard_map/psum | solution.py:19
  139.9 138.1 %copy-start.2 = (f32[8,16,256]{2,1,0:T(8,128)S(1)}, f32[8,16,256]{2,1,0:T(8,128)}, u32[]{:S(2)}) copy-start(f32[8,16,256]{2,1,0:T(8,128)} %get-tuple-element.35) | copy-start | bytes 393220
  211.3 112.6 %copy-start = (f32[8,192,16]{2,1,0:T(8,128)S(1)}, f32[8,192,16]{2,1,0:T(8,128)}, u32[]{:S(2)}) copy-start(f32[8,192,16]{2,1,0:T(8,128)} %get-tuple-element.37) | copy-start | bytes 294916
  212.9 177.7 %copy-start.8 = (f32[8,16,256]{2,1,0:T(8,128)S(1)}, f32[8,16,256]{2,1,0:T(8,128)}, u32[]{:S(2)}) copy-start(f32[8,16,256]{2,1,0:T(8,128)} %get-tuple-element.34) | copy-start | bytes 393220
  212.9 223.7 %copy-start.3 = (f32[8,192,16]{2,1,0:T(8,128)S(1)}, f32[8,192,16]{2,1,0:T(8,128)}, u32[]{:S(2)}) copy-start(f32[8,192,16]{2,1,0:T(8,128)} %get-tuple-element.36) | copy-start | bytes 294916
  225.9 98.0 %all-reduce.24.cloned.1.call-start = ((), (), s32[]{:S(2)}) async-start(), calls=%async_computation | async-start | bytes 1572864 | tf_op jit(solution)/shard_map/psum | solution.py:15
  226.5 164.1 %all-reduce.30.cloned.1.call-start = ((), (), s32[]{:S(2)}) async-start(), calls=%async_computation.3 | async-start | bytes 262144 | tf_op jit(solution)/shard_map/psum | solution.py:19
  323.9 112.7 %copy-start.6 = (f32[8,192,16]{2,1,0:T(8,128)S(1)}, f32[8,192,16]{2,1,0:T(8,128)}, u32[]{:S(2)}) copy-start(f32[8,192,16]{2,1,0:T(8,128)} %all-reduce.24.cloned.1.call-done) | copy-start | bytes 294916
  338.2 98.4 %all-reduce.28.cloned.1.call-start = ((), (), s32[]{:S(2)}) async-start(), calls=%async_computation.2 | async-start | bytes 1572864 | tf_op jit(solution)/shard_map/psum | solution.py:15
  338.8 164.5 %all-reduce.34.cloned.1.call-start = ((), (), s32[]{:S(2)}) async-start(), calls=%async_computation.5 | async-start | bytes 262144 | tf_op jit(solution)/shard_map/psum | solution.py:19
  450.9 98.4 %all-reduce.32.cloned.1.call-start = ((), (), s32[]{:S(2)}) async-start(), calls=%async_computation.4 | async-start | bytes 1572864 | tf_op jit(solution)/shard_map/psum | solution.py:15
  451.6 207.5 %all-reduce.38.cloned.1.call-start = ((), (), s32[]{:S(2)}) async-start(), calls=%async_computation.7 | async-start | bytes 262144 | tf_op jit(solution)/shard_map/psum | solution.py:19
  593.8 177.9 %copy-start.9 = (f32[8,16,256]{2,1,0:T(8,128)S(1)}, f32[8,16,256]{2,1,0:T(8,128)}, u32[]{:S(2)}) copy-start(f32[8,16,256]{2,1,0:T(8,128)} %get-tuple-element.51) | copy-start | bytes 393220
  606.8 98.3 %all-reduce.36.cloned.1.call-start = ((), (), s32[]{:S(2)}) async-start(), calls=%async_computation.6 | async-start | bytes 1572864 | tf_op jit(solution)/shard_map/psum | solution.py:15
  607.4 164.4 %all-reduce.42.cloned.1.call-start = ((), (), s32[]{:S(2)}) async-start(), calls=%async_computation.9 | async-start | bytes 262144 | tf_op jit(solution)/shard_map/psum | solution.py:19
  705.1 112.6 %copy-start.5 = (f32[8,192,16]{2,1,0:T(8,128)S(1)}, f32[8,192,16]{2,1,0:T(8,128)}, u32[]{:S(2)}) copy-start(f32[8,192,16]{2,1,0:T(8,128)} %all-reduce.36.cloned.1.call-done) | copy-start | bytes 294916
  719.4 98.3 %all-reduce.40.cloned.1.call-start = ((), (), s32[]{:S(2)}) async-start(), calls=%async_computation.8 | async-start | bytes 1572864 | tf_op jit(solution)/shard_map/psum | solution.py:15
  719.9 207.9 %all-reduce.46.cloned.1.call-start = ((), (), s32[]{:S(2)}) async-start(), calls=%async_computation.11 | async-start | bytes 262144 | tf_op jit(solution)/shard_map/psum | solution.py:19
  875.5 98.3 %all-reduce.44.cloned.1.call-start = ((), (), s32[]{:S(2)}) async-start(), calls=%async_computation.10 | async-start | bytes 1572864 | tf_op jit(solution)/shard_map/psum | solution.py:15
  876.1 209.1 %all-reduce.50.cloned.1.call-start = ((), (), s32[]{:S(2)}) async-start(), calls=%async_computation.13 | async-start | bytes 262144 | tf_op jit(solution)/shard_map/psum | solution.py:19
  1019.7 265.7 %copy-start.14 = (f32[8]{0:T(128)S(1)}, f32[8]{0:T(128)}, u32[]{:S(2)}) copy-start(f32[8]{0:T(128)} %copy-done.13) | copy-start | bytes 100
  1032.7 97.8 %all-reduce.48.cloned.1.call-start = ((), (), s32[]{:S(2)}) async-start(), calls=%async_computation.12 | async-start | bytes 1572864 | tf_op jit(solution)/shard_map/psum | solution.py:15
  1033.3 163.9 %all-reduce.54.cloned.1.call-start = ((), (), s32[]{:S(2)}) async-start(), calls=%async_computation.15 | async-start | bytes 262144 | tf_op jit(solution)/shard_map/psum | solution.py:19
  1144.8 97.8 %all-reduce.52.cloned.1.call-start = ((), (), s32[]{:S(2)}) async-start(), calls=%async_computation.14 | async-start | bytes 1572864 | tf_op jit(solution)/shard_map/psum | solution.py:15
  1145.4 207.2 %all-reduce.58.cloned.1.call-start = ((), (), s32[]{:S(2)}) async-start(), calls=%async_computation.17 | async-start | bytes 262144 | tf_op jit(solution)/shard_map/psum | solution.py:19
  1300.2 98.2 %all-reduce.56.cloned.1.call-start = ((), (), s32[]{:S(2)}) async-start(), calls=%async_computation.16 | async-start | bytes 1572864 | tf_op jit(solution)/shard_map/psum | solution.py:15
  (4 other events, 23.9 us)
Sparse Core Ops, SparseCore 0:
  83.5 56.3 all-reduce.59
  142.4 68.8 all-reduce.61
  226.0 51.9 all-reduce.25
  280.8 43.0 all-reduce.23
  338.3 52.2 all-reduce.29
  393.5 43.0 all-reduce.27
  451.0 52.2 all-reduce.33
  506.2 43.0 all-reduce.31
  606.9 52.1 all-reduce.37
  662.0 43.0 all-reduce.35
  719.5 52.2 all-reduce.41
  774.6 43.0 all-reduce.39
  875.6 52.1 all-reduce.45
  930.8 43.0 all-reduce.43
  1032.8 52.3 all-reduce.49
  1087.4 43.0 all-reduce.47
  1144.9 52.2 all-reduce.53
  1199.6 43.0 all-reduce.51
  1300.3 52.1 all-reduce.57
  1355.3 43.0 all-reduce.55
where the time goes:
time: 1470 us
  waiting for transfers between devices  998 us (68%)
  other arithmetic  253 us (17%)
  blocking collectives  199 us (14%)
    psum x10, waiting for transfers between devices, col_margin(): return lax.psum(partial_value, 'region')  521 us
    psum x10, waiting for transfers between devices, row_margin(): return lax.psum(partial_value, 'industry')  471 us
    psum x5, blocking collectives, inner_pair(): lax.psum(local_pair(first_row, second_row, first_col, second_col), ('regi...  199 us
    reduce_sum x6, other arithmetic, couple(): left = row_margin(jnp.sum(scaling * part_col[:, None, :, :], axis=3))  77.6 us
    reduce_sum x3, other arithmetic, couple(): right = col_margin(jnp.sum(scaling * part_row[..., None], axis=1))  38.9 us
    reduce_sum x1, other arithmetic, local(): jnp.sum(margin_term, axis=3)  32.9 us
    reduce_sum x1, other arithmetic, local(): jnp.sum(scaling, axis=3)  32.5 us
  transfers between devices with their start and end apart: 20, of which 20 were waited for; matrix products, arithmetic and copies ran while one was open for 1% of the time, Pallas kernels for 0%

commit v1 on v0

v1 whole, which is shorter than its diff:
```python
import functools

import jax
import jax.numpy as jnp
from jax import lax
from jax.experimental import pallas as pl
from jax.experimental.pallas import tpu as pltpu
from jax.sharding import PartitionSpec as P

WEIGHT_ATTACK = 8.0
SHIFT_DIAG = 1.0
BLOCK = 8
VMEM_SPEC = pl.BlockSpec(memory_space=pltpu.VMEM)
SMEM_SPEC = pl.BlockSpec(memory_space=pltpu.SMEM)
ANY_SPEC = pl.BlockSpec(memory_space=pl.ANY)
F32 = jnp.float32


def up8(count):
    return -(-count // 8) * 8


def inverse(x):
    rough = pl.reciprocal(x, approx=True)
    return rough * (2.0 - x * rough)


def piece_at(full_ref, index, piece):
    return full_ref[pl.ds(pl.multiple_of(index * piece, 8), piece), :]


def direct(count):
    return count <= 8


def parts(count):
    return count if direct(count) else 1


def put_pieces(full_ref, piece_refs, me, piece):
    count = len(piece_refs)
    if count == 1:
        full_ref[...] = piece_refs[0][...]
        return
    for d, ref in enumerate(piece_refs):
        owner = lax.rem(me + (count - d), count)
        full_ref[pl.ds(pl.multiple_of(owner * piece, 8), piece), :] = ref[...]


def take_pieces(full_refs, piece_refs, me, piece):
    count = len(piece_refs)
    for d, ref in enumerate(piece_refs):
        for j, full in enumerate(full_refs):
            if count == 1:
                ref[:, j] = full[...].reshape(ref.shape[0], ref.shape[2], 128)
            else:
                ref[j] = piece_at(full, lax.rem(me + d, count), piece)


def sweep(scaling_ref, row_ref, col_ref, row_out, col_out, rows, inds):
    col_out[...] = jnp.zeros_like(col_out)
    if row_out.shape[0] > rows:
        row_out[...] = jnp.zeros_like(row_out)

    def step(block, _):
        r0 = pl.multiple_of(block * BLOCK, BLOCK)
        row_wide = jnp.broadcast_to(row_ref[pl.ds(r0, BLOCK), :][:, None, :], (BLOCK, 8, 128))
        row_acc = jnp.zeros((BLOCK, 8, 128), F32)
        for i0 in range(0, inds, 8):
            tile = scaling_ref[pl.ds(r0, BLOCK), i0 : i0 + 8, :]
            row_acc = row_acc + tile * col_ref[i0 : i0 + 8, :][None]
            col_out[i0 : i0 + 8, :] += jnp.sum(tile * row_wide, axis=0)
        row_out[pl.ds(r0, BLOCK), :] = jnp.sum(row_acc, axis=1)
        return 0

    lax.fori_loop(0, rows // BLOCK, step, 0)


def prepare_kernel(
    rows, sizes, inds, probs, nreg, nind, row_piece, col_piece,
    place_ref, flag_ref, region_ref, column_ref,
    pos_hbm, low_hbm, high_hbm, upper_hbm, supp_hbm, drow_ref, dcol_ref,
    *rest,
):
    scaling_ref, barrier_hbm = rest[:2]
    nrow, ncol = parts(nind), parts(nreg)
    row_outs = rest[2 : 2 + nrow]
    col_outs = rest[2 + nrow : 2 + nrow + ncol]
    (tile_s, tile_m, up_s, act_s, row_m, row_s, col_m, col_mt, col_s, col_e) = rest[2 + nrow + ncol :]
    my_reg, my_ind = place_ref[0], place_ref[1]
    half = inds // 128
    col_m[...] = jnp.zeros_like(col_m)
    col_s[...] = jnp.zeros_like(col_s)
    col_e[...] = jnp.zeros_like(col_e)
    row_m[...] = jnp.zeros_like(row_m)
    row_s[...] = jnp.zeros_like(row_s)

    def body(pos_ref, low_ref, high_ref, upper_ref, supp_ref, barrier_ref):
        block = pl.program_id(0)
        r0 = pl.multiple_of(block * BLOCK, BLOCK)
        up_s[...] = upper_ref[...].astype(F32)
        act_s[...] = supp_ref[...].astype(F32)

        def problem(k, _, attacked):
            total = jnp.zeros((sizes, inds), F32)
            for r in range(BLOCK):
                upper = up_s[r]
                active = act_s[r]
                if attacked:
                    own = (region_ref[k] == my_reg * rows + r0 + r).astype(jnp.int32)
                    column = lax.broadcasted_iota(jnp.int32, (sizes, inds), 0) * (inds * nind)
                    column = column + lax.broadcasted_iota(jnp.int32, (sizes, inds), 1) + my_ind * inds
                    hit = column == jnp.where(own == 1, column_ref[k], -1)
                    active = jnp.where(hit, jnp.ones_like(active), active)
                value = pos_ref[k, r].astype(F32) * upper
                slack = upper - value
                den = low_ref[k, r].astype(F32) * slack + high_ref[k, r].astype(F32) * value
                ratio = active * inverse(den)
                scaling = value * slack * ratio
                middle = 0.5 * upper - value
                barrier = middle * ratio
                if attacked:
                    barrier = barrier + jnp.where(hit, WEIGHT_ATTACK * scaling, jnp.zeros_like(scaling))
                margin = middle * active + barrier
                barrier_ref[k, r] = barrier
                place = pl.ds(pl.multiple_of(k * sizes, sizes), sizes)
                tile_s[r, place, :] = scaling
                folded = margin[:, :128]
                for part in range(1, half):
                    folded = folded + margin[:, part * 128 : (part + 1) * 128]
                tile_m[r, place, :] = folded
                total = total + margin
            place = pl.ds(pl.multiple_of(k * sizes, sizes), sizes)
            col_m[place, :] += total
            return 0

        hits = flag_ref[block]

        @pl.when(hits == 0)
        def _():
            lax.fori_loop(0, probs, functools.partial(problem, attacked=False), 0)

        @pl.when(hits != 0)
        def _():
            lax.fori_loop(0, probs, functools.partial(problem, attacked=True), 0)

        def turn(r, _):
            scaling_ref[r0 + r] = tile_s[r].T
            row_m[pl.ds(r0 + r, 1), :] = jnp.sum(tile_m[r].T, axis=0, keepdims=True)
            return 0

        lax.fori_loop(0, BLOCK, turn, 0)

        row_wide = jnp.broadcast_to(drow_ref[pl.ds(r0, BLOCK), :][:, None, :], (BLOCK, 8, 128))
        sum_acc = jnp.zeros((BLOCK, 8, 128), F32)
        dual_acc = jnp.zeros((BLOCK, 8, 128), F32)
        for i0 in range(0, inds, 8):
            tile = scaling_ref[pl.ds(r0, BLOCK), i0 : i0 + 8, :]
            sum_acc = sum_acc + tile
            dual_acc = dual_acc + tile * dcol_ref[i0 : i0 + 8, :][None]
            col_s[i0 : i0 + 8, :] += jnp.sum(tile, axis=0)
            col_e[i0 : i0 + 8, :] += jnp.sum(tile * row_wide, axis=0)
        sums = jnp.sum(sum_acc, axis=1)
        here = pl.ds(r0, BLOCK)
        row_s[here, :] = sums
        row_m[here, :] = row_m[here, :] - drow_ref[here, :] * sums - jnp.sum(dual_acc, axis=1)

    cells = pl.BlockSpec((probs, BLOCK, sizes, inds), lambda b: (0, b, 0, 0))
    shared = pl.BlockSpec((BLOCK, sizes, inds), lambda b: (b, 0, 0))
    pltpu.emit_pipeline(
        body,
        grid=(rows // BLOCK,),
        in_specs=[cells, cells, cells, shared, shared],
        out_specs=[cells],
    )(pos_hbm, low_hbm, high_hbm, upper_hbm, supp_hbm, barrier_hbm)

    if col_mt.shape[0] > inds:
        col_mt[...] = jnp.zeros_like(col_mt)
    col_mt[:inds, :] = col_m[...].T - dcol_ref[:inds, :] * col_s[:inds, :] - col_e[:inds, :]
    take_pieces((row_m, row_s), row_outs, my_ind, row_piece)
    take_pieces((col_mt, col_s), col_outs, my_reg, col_piece)


def couple_kernel(rows, inds, nreg, nind, row_piece, col_piece, place_ref, scaling_ref, *rest):
    nrow, ncol = parts(nind), parts(nreg)
    row_ins, rest = rest[:nrow], rest[nrow:]
    col_ins, rest = rest[:ncol], rest[ncol:]
    row_full, col_full = rest[:2]
    row_outs, rest = rest[2 : 2 + nrow], rest[2 + nrow :]
    col_outs, rest = rest[:ncol], rest[ncol:]
    row_part, col_part = rest
    my_reg, my_ind = place_ref[0], place_ref[1]
    put_pieces(row_full, row_ins, my_ind, row_piece)
    put_pieces(col_full, col_ins, my_reg, col_piece)
    sweep(scaling_ref, row_full, col_full, row_part, col_part, rows, inds)
    take_pieces((row_part,), row_outs, my_ind, row_piece)
    take_pieces((col_part,), col_outs, my_reg, col_piece)


def products_kernel(
    rows, inds, nreg, nind, row_piece, col_piece, iters,
    place_ref, scaling_ref, row_diag_ref, col_diag_ref, *rest,
):
    nrow, ncol = parts(nind), parts(nreg)
    row_ins, rest = rest[:nrow], rest[nrow:]
    col_ins, rest = rest[:ncol], rest[ncol:]
    row_old, rest = rest[:2], rest[2:]
    col_old, rest = rest[:2], rest[2:]
    count = 3 * iters
    row_own, rest = rest[:count], rest[count:]
    col_own, rest = rest[:count], rest[count:]
    out_ref, row_full, col_full, row_z, col_z = rest
    my_reg, my_ind = place_ref[0], place_ref[1]
    put_pieces(row_full, row_ins, my_ind, row_piece)
    put_pieces(col_full, col_ins, my_reg, col_piece)
    row_z[...] = row_old[0][...] - row_old[1][...] + row_full[...]
    col_z[...] = col_old[0][...] - col_old[1][...] + col_full[...]

    def step(block, acc):
        r0 = pl.multiple_of(block * BLOCK, BLOCK)
        row_acc = jnp.zeros((BLOCK, 8, 128), F32)
        for i0 in range(0, inds, 8):
            row_acc = row_acc + scaling_ref[pl.ds(r0, BLOCK), i0 : i0 + 8, :] * col_z[i0 : i0 + 8, :][None]
        return acc + jnp.sum(row_acc, axis=1) * row_z[pl.ds(r0, BLOCK), :]

    cross = lax.fori_loop(0, rows // BLOCK, step, jnp.zeros((BLOCK, 128), F32))
    cross = 2.0 * jnp.sum(cross, axis=0, keepdims=True)

    out_ref[...] = jnp.zeros_like(out_ref)
    row_p = [ref[...] for ref in row_own]
    col_p = [ref[...] for ref in col_own]
    row_zs = [row_p[3 * j] - row_p[3 * j + 1] + row_p[3 * j + 2] for j in range(iters)]
    col_zs = [col_p[3 * j] - col_p[3 * j + 1] + col_p[3 * j + 2] for j in range(iters)]
    slot = 0
    row_diag, col_diag = row_diag_ref[...], col_diag_ref[...]

    def dot(j, row_v, col_v):
        return jnp.sum(row_zs[j] * row_v, axis=0, keepdims=True) + jnp.sum(col_zs[j] * col_v, axis=0, keepdims=True)

    row_first, col_first = row_diag * row_p[0], col_diag * col_p[0]
    for j in range(iters):
        out_ref[slot : slot + 1, :] = dot(j, row_first, col_first)
        slot += 1
    for m in range(iters):
        if m + 1 < iters:
            row_n = row_diag * (row_p[3 * m] + row_p[3 * m + 3])
            col_n = col_diag * (col_p[3 * m] + col_p[3 * m + 3])
        else:
            row_n = row_diag * row_zs[m]
            col_n = col_diag * col_zs[m]
        for j in range(m, iters):
            product = dot(j, row_n, col_n)
            if m + 1 == iters:
                product = product + cross
            out_ref[slot : slot + 1, :] = product
            slot += 1


def ordered_kernel(slot, place_ref, *rest):
    ins, out_ref, slots = rest[:-2], rest[-2], rest[-1]
    ordered_sum(out_ref, ins, slots, place_ref[slot])


def ordered_sum(out_ref, ins, slots, me):
    count = len(ins)
    for d, ref in enumerate(ins):
        slots[lax.rem(me + (count - d), count)] = ref[...]
    total = slots[0]
    for j in range(1, count):
        total = total + slots[j]
    out_ref[...] = total


def finish_kernel(
    rows, sizes, inds, probs, nreg, nind, row_piece, col_piece, iters,
    place_ref, scaling_ref, barrier_hbm, drow_ref, dcol_ref, *rest,
):
    nrow, ncol = parts(nind), parts(nreg)
    sums, rest = rest[:nrow], rest[nrow:]
    row_ins, rest = rest[:nrow], rest[nrow:]
    col_ins, rest = rest[:ncol], rest[ncol:]
    count = 3 * iters - 1
    row_old, rest = rest[:count], rest[count:]
    col_old, rest = rest[:count], rest[count:]
    cell_hbm, row_ref, col_ref, row_full, col_full, row_add, col_add, slots, total_ref = rest
    my_reg, my_ind = place_ref[0], place_ref[1]
    put_pieces(row_full, row_ins, my_ind, row_piece)
    put_pieces(col_full, col_ins, my_reg, col_piece)
    ordered_sum(total_ref, sums, slots, my_ind)
    total = total_ref[...]
    lane = lax.broadcasted_iota(jnp.int32, (128, 128), 0) // sizes
    other = lax.broadcasted_iota(jnp.int32, (128, 128), 1) // sizes
    same = (lane == other).astype(F32)
    total = jnp.dot(total, same, preferred_element_type=F32, precision=lax.Precision.HIGHEST)
    line = [total[j : j + 1, :] for j in range(9)]
    g0, g1, g2, h00, h10, h20, h11, h21, h22 = line
    l1, l2 = h10 / h00, h20 / h00
    d1 = h11 - l1 * h10
    t21 = h21 - l2 * h10
    m21 = t21 / d1
    d2 = h22 - l2 * h20 - m21 * t21
    y1 = g1 - l1 * g0
    y2 = g2 - l2 * g0 - m21 * y1
    c2 = y2 / d2
    c1 = y1 / d1 - m21 * c2
    c0 = g0 / h00 - l1 * c1 - l2 * c2
    coef = (c0, c1, c2)

    def combine(old, last):
        parts = [ref[...] for ref in old] + [last[...]]
        acc = None
        for j in range(iters):
            z = parts[3 * j] - parts[3 * j + 1] + parts[3 * j + 2]
            term = coef[j] * z
            acc = term if acc is None else acc + term
        return acc

    row_y = combine(row_old, row_full)
    col_y = combine(col_old, col_full)
    row_ref[...] = row_y
    col_ref[...] = col_y
    row_add[...] = row_y + drow_ref[...]
    col_add[...] = col_y + dcol_ref[...]

    def body(barrier_ref, cell_ref):
        r0 = pl.program_id(0) * BLOCK

        def one(r, _):
            moved = (col_add[:inds, :] + row_add[pl.ds(r0 + r, 1), :]) * scaling_ref[r0 + r]
            moved = moved.T
            for k in range(probs):
                cell_ref[k, r] = (moved[k * sizes : (k + 1) * sizes, :] - barrier_ref[k, r]).astype(jnp.bfloat16)
            return 0

        lax.fori_loop(0, BLOCK, one, 0)

    cells = pl.BlockSpec((probs, BLOCK, sizes, inds), lambda b: (0, b, 0, 0))
    pltpu.emit_pipeline(
        body, grid=(rows // BLOCK,), in_specs=[cells], out_specs=[cells]
    )(barrier_hbm, cell_hbm)


def shift(x, axis, d, count):
    return lax.ppermute(x, axis, [(j, (j + d) % count) for j in range(count)])


def scatter_sum(pieces, axis, count):
    if not direct(count):
        return lax.psum_scatter(pieces[0], axis, scatter_dimension=0)
    total = pieces[0]
    arrived = [shift(pieces[d], axis, d, count) for d in range(1, count)]
    for part in arrived:
        total = total + part
    return total


def gather(piece, axis, count):
    if not direct(count):
        return [lax.all_gather(piece, axis, tiled=True)]
    return [piece] + [shift(piece, axis, d, count) for d in range(1, count)]


def sum_scalars(part, place, axis, count, slot):
    if not direct(count):
        return lax.psum(part, axis)
    pieces = gather(part, axis, count)
    return pl.pallas_call(
        functools.partial(ordered_kernel, slot),
        out_shape=jax.ShapeDtypeStruct(part.shape, F32),
        in_specs=[SMEM_SPEC] + [VMEM_SPEC] * count,
        out_specs=VMEM_SPEC,
        scratch_shapes=[pltpu.VMEM((count,) + part.shape, F32)],
        compiler_params=pltpu.CompilerParams(vmem_limit_bytes=4 * 1024 * 1024),
        name="regions",
    )(place, *pieces)


def local(
    nreg, nind, iters,
    position, dual_lower, dual_upper, upper_bound, suppressed,
    attack_region, attack_column, dual_row, dual_col,
):
    probs, rows, sizes, inds = position.shape
    row_piece, col_piece = up8(-(-rows // nind)), up8(-(-inds // nreg))
    row_len, col_len = row_piece * nind, col_piece * nreg
    my_reg, my_ind = lax.axis_index("region"), lax.axis_index("industry")
    place = jnp.stack([my_reg, my_ind]).astype(jnp.int32)
    blocks = rows // BLOCK
    first = my_reg * rows + BLOCK * jnp.arange(blocks, dtype=jnp.int32)
    near = (attack_region[None, :] >= first[:, None]) & (attack_region[None, :] < first[:, None] + BLOCK)
    flags = jnp.any(near, axis=1).astype(jnp.int32)
    drow = dual_row.transpose(1, 0, 2).reshape(rows, probs * sizes)
    dcol = dual_col.reshape(probs * sizes, inds).T
    drow = jnp.pad(drow, ((0, row_len - rows), (0, 0)))
    dcol = jnp.pad(dcol, ((0, col_len - inds), (0, 0)))

    def shape(*dims):
        return jax.ShapeDtypeStruct(dims, F32)

    def params(mib):
        return pltpu.CompilerParams(vmem_limit_bytes=mib * 1024 * 1024)

    nrow, ncol = parts(nind), parts(nreg)

    def pieces(count, piece, *inner):
        if direct(count):
            return [shape(*inner, piece, 128)] * count
        return [shape(count, *inner, piece, 128)]

    sizes_all = (rows, inds, nreg, nind, row_piece, col_piece)
    outs = pl.pallas_call(
        functools.partial(prepare_kernel, rows, sizes, inds, probs, nreg, nind, row_piece, col_piece),
        out_shape=[pltpu.VMEM((rows, inds, 128), F32), shape(probs, rows, sizes, inds)]
        + pieces(nind, row_piece, 2)
        + pieces(nreg, col_piece, 2),
        in_specs=[SMEM_SPEC] * 4 + [ANY_SPEC] * 5 + [VMEM_SPEC] * 2,
        out_specs=[VMEM_SPEC, ANY_SPEC] + [VMEM_SPEC] * (nrow + ncol),
        scratch_shapes=[
            pltpu.VMEM((BLOCK, 128, inds), F32),
            pltpu.VMEM((BLOCK, 128, 128), F32),
            pltpu.VMEM((BLOCK, sizes, inds), F32),
            pltpu.VMEM((BLOCK, sizes, inds), F32),
            pltpu.VMEM((row_len, 128), F32),
            pltpu.VMEM((row_len, 128), F32),
            pltpu.VMEM((128, inds), F32),
            pltpu.VMEM((col_len, 128), F32),
            pltpu.VMEM((col_len, 128), F32),
            pltpu.VMEM((col_len, 128), F32),
        ],
        compiler_params=params(14),
        name="prepare",
    )(place, flags, attack_region, attack_column, position, dual_lower, dual_upper, upper_bound, suppressed, drow, dcol)
    scaling, barrier = outs[:2]
    row_pieces, col_pieces = outs[2 : 2 + nrow], outs[2 + nrow :]

    def keep(x):
        return pltpu.with_memory_space_constraint(x, pltpu.VMEM)

    row_both = scatter_sum(row_pieces, "industry", nind)
    col_both = scatter_sum(col_pieces, "region", nreg)
    row_diag, col_diag = row_both[1] + SHIFT_DIAG, col_both[1] + SHIFT_DIAG
    row_now, col_now = row_both[0] / row_diag, col_both[0] / col_diag
    row_own, col_own = [row_now], [col_now]
    row_all, col_all = [], []
    couple = pl.pallas_call(
        functools.partial(couple_kernel, *sizes_all),
        out_shape=[shape(row_len, 128), shape(col_len, 128)]
        + pieces(nind, row_piece, 1)
        + pieces(nreg, col_piece, 1),
        in_specs=[SMEM_SPEC] + [VMEM_SPEC] * (1 + nrow + ncol),
        out_specs=[VMEM_SPEC] * (2 + nrow + ncol),
        scratch_shapes=[pltpu.VMEM((row_len, 128), F32), pltpu.VMEM((col_len, 128), F32)],
        compiler_params=params(8),
        name="couple",
    )
    for _ in range(3 * iters - 1):
        row_in, col_in = gather(row_now, "industry", nind), gather(col_now, "region", nreg)
        outs = couple(place, keep(scaling), *row_in, *col_in)
        row_all.append(outs[0])
        col_all.append(outs[1])
        row_now = scatter_sum(outs[2 : 2 + nrow], "industry", nind)[0] / row_diag
        col_now = scatter_sum(outs[2 + nrow :], "region", nreg)[0] / col_diag
        row_own.append(row_now)
        col_own.append(col_now)
    row_in, col_in = gather(row_now, "industry", nind), gather(col_now, "region", nreg)
    part = pl.pallas_call(
        functools.partial(products_kernel, *sizes_all, iters),
        out_shape=shape(16, 128),
        in_specs=[SMEM_SPEC] + [VMEM_SPEC] * (3 + nrow + ncol + 4 + 6 * iters),
        out_specs=VMEM_SPEC,
        scratch_shapes=[
            pltpu.VMEM((row_len, 128), F32),
            pltpu.VMEM((col_len, 128), F32),
            pltpu.VMEM((row_len, 128), F32),
            pltpu.VMEM((col_len, 128), F32),
        ],
        compiler_params=params(8),
        name="products",
    )(
        place, keep(scaling), row_diag, col_diag, *row_in, *col_in,
        *row_all[-2:], *col_all[-2:], *row_own, *col_own,
    )
    part = sum_scalars(part, place, "region", nreg, 0)
    sums = gather(part, "industry", nind) if direct(nind) else [lax.psum(part, "industry")]
    cell, row_y, col_y = pl.pallas_call(
        functools.partial(finish_kernel, rows, sizes, inds, probs, nreg, nind, row_piece, col_piece, iters),
        out_shape=[
            jax.ShapeDtypeStruct((probs, rows, sizes, inds), jnp.bfloat16),
            shape(row_len, 128),
            shape(col_len, 128),
        ],
        in_specs=[SMEM_SPEC, VMEM_SPEC, ANY_SPEC]
        + [VMEM_SPEC] * (2 + 2 * nrow + ncol + 2 * (3 * iters - 1)),
        out_specs=[ANY_SPEC, VMEM_SPEC, VMEM_SPEC],
        scratch_shapes=[
            pltpu.VMEM((row_len, 128), F32),
            pltpu.VMEM((col_len, 128), F32),
            pltpu.VMEM((row_len, 128), F32),
            pltpu.VMEM((col_len, 128), F32),
            pltpu.VMEM((nind, 16, 128), F32),
            pltpu.VMEM((16, 128), F32),
        ],
        compiler_params=params(12),
        name="finish",
    )(place, keep(scaling), barrier, drow, dcol, *sums, *row_in, *col_in, *row_all, *col_all)
    row_step = row_y[:rows].reshape(rows, probs, sizes).transpose(1, 0, 2)
    col_step = col_y[:inds].T.reshape(probs, sizes, inds)
    return cell, row_step, col_step


def solution(mesh):
    nreg, nind = mesh.shape["region"], mesh.shape["industry"]
    cells = P(None, "region", None, "industry")
    table = P("region", None, "industry")
    row, col = P(None, "region", None), P(None, None, "industry")
    return jax.shard_map(
        functools.partial(local, nreg, nind, 3),
        mesh=mesh,
        in_specs=(cells, cells, cells, table, table, P(), P(), row, col),
        out_specs=(cells, row, col),
        check_vma=False,
    )
```

time: 1470 us -> 425 us (0.29)
  waiting for transfers between devices: 998 us -> 47 us
  other arithmetic: 253 us -> 11.3 us
  starting transfers between devices: 0.8 us -> 205 us
  blocking collectives: 199 us -> 0 us
  Pallas kernels: 0 us -> 133 us
  local copies, waits for them, and re-layouts: 3.21 us -> 25.1 us
    psum x20 -> x0, waiting for transfers between devices: 993 us -> none  [the longest x10 521 us: col_margin(): return lax.psum(partial_value, 'region')]
    ppermute x0 -> x190, starting transfers between devices: none -> 205 us  [shift(): return lax.ppermute(x, axis, [(j, (j + d) % count) for j in range(count)])]
    psum x5 -> x0, blocking collectives: 199 us -> none  [inner_pair(): lax.psum(local_pair(first_row, second_row, first_col, second_col), ('regi...]
    reduce_sum x21 -> x0, other arithmetic: 197 us -> none  [the longest x6 77.6 us: couple(): left = row_margin(jnp.sum(scaling * part_col[:, None, :, :], axis=3))]
    pallas_call x0 -> x12, Pallas kernels: none -> 133 us  [the longest x1 64.1 us: local(): pl.pallas_call(functools.partial(prepare_kernel, rows, sizes, inds, probs...]
    ppermute x0 -> x190, waiting for transfers between devices: none -> 47 us  [shift(): return lax.ppermute(x, axis, [(j, (j + d) % count) for j in range(count)])]
    convert_element_type x2 -> x1, other arithmetic: 24.5 us -> 0.01 us  [local(): flags = jnp.any(near, axis=1).astype(jnp.int32)]
    unnamed x34 -> x22, local copies, waits for them, and re-layouts: 3.21 us -> 21.6 us
  transfers between devices with their start and end apart: 20 -> 190, of which waited for: 20 -> 30; matrix products, arithmetic and copies ran while one was open for 1% -> 2% of each run, Pallas kernels for 0% -> 0%
where the time goes in v1:
time: 425 us; the launch traced here: 423 us
  starting transfers between devices  205 us (48%)
  Pallas kernels  133 us (31%)
  waiting for transfers between devices  47 us (11%)
  local copies, waits for them, and re-layouts  25.1 us (6%)
  other arithmetic  11.3 us (3%)
    ppermute x190, starting transfers between devices, shift(): return lax.ppermute(x, axis, [(j, (j + d) % count) for j in range(count)])  205 us
    pallas_call x1, Pallas kernels, local(): pl.pallas_call(functools.partial(prepare_kernel, rows, sizes, inds, probs...  64.1 us
    ppermute x190, waiting for transfers between devices, shift(): return lax.ppermute(x, axis, [(j, (j + d) % count) for j in range(count)])  47 us
    pallas_call x8, Pallas kernels, local(): outs = couple(place, keep(scaling), *row_in, *col_in)  34.3 us
    pallas_call x1, Pallas kernels, local(): pl.pallas_call(functools.partial(finish_kernel, rows, sizes, inds, probs,...  31.2 us
    unnamed x22, local copies, waits for them, and re-layouts  21.6 us
  transfers between devices with their start and end apart: 190, of which 30 were waited for; matrix products, arithmetic and copies ran while one was open for 2% of the time, Pallas kernels for 0%

profile of v1, /device:TPU:0, one launch (start us, length us, event | category | flops | bytes accessed | tf_op | source)
XLA Modules:
  0.0 423.3 jit_solution(612082781048080570)
XLA Ops:
  8.6 64.1 %prepare.1 = (f32[192,256,128]{2,1,0:T(8,128)S(1)}, f32[8,192,16,256]{3,2,1,0:T(8,128)}, f32[2,48,128]{2,1,0:T(8,128)S(1)}, f32[2,48,128]{2,1,0:T(8,128)S(1)}, f...) custom-call(s32[2]{0:T(128)S(1)} %pad_add_fusion.place_ref, ...), custom_call_target="tpu_custom_call" | custom-call | tf_op jit(solution)/shard_map/prepare/pallas_call | solution.py:411
  72.7 8.3 %copy-done = f32[192,256,128]{2,1,0:T(8,128)} copy-done((f32[192,256,128]{2,1,0:T(8,128)}, f32[192,256,128]{2,1,0:T(8,128)S(1)}, u32[]{:S(2)}) %copy-start) | copy-done | bytes 25165848
  81.1 2.8 collective-permute-start.4
  91.8 2.6 collective-permute-start.1
  104.8 2.5 collective-permute-done.14.rest_6_
  108.9 8.1 %copy-done.1 = f32[192,256,128]{2,1,0:T(8,128)S(1)} copy-done((f32[192,256,128]{2,1,0:T(8,128)S(1)}, f32[192,256,128]{2,1,0:T(8,128)}, u32[]{:S(2)}) %copy-start.1) | copy-done | bytes 25165848
  117.0 4.3 %couple.8 = (f32[192,128]{1,0:T(8,128)S(1)}, f32[256,128]{1,0:T(8,128)S(1)}, f32[1,48,128]{2,1,0:T(8,128)S(1)}, f32[1,48,128]{2,1,0:T(8,128)S(1)}, f32[1,48,128]...) custom-call(s32[2]{0:T(128)S(1)} %pad_add_fusion.place_ref, ...), custom_call_target="tpu_custom_call" | custom-call | tf_op jit(solution)/shard_map/couple/pallas_call | solution.py:458
  129.1 2.5 collective-permute-start.20
  141.6 2.7 collective-permute-start.34
  148.3 4.3 %couple.9 = (f32[192,128]{1,0:T(8,128)S(1)}, f32[256,128]{1,0:T(8,128)S(1)}, f32[1,48,128]{2,1,0:T(8,128)S(1)}, f32[1,48,128]{2,1,0:T(8,128)S(1)}, f32[1,48,128]...) custom-call(s32[2]{0:T(128)S(1)} %pad_add_fusion.place_ref, ...), custom_call_target="tpu_custom_call" | custom-call | tf_op jit(solution)/shard_map/couple/pallas_call | solution.py:458
  173.4 2.5 collective-permute-start.54
  180.1 4.3 %couple.10 = (f32[192,128]{1,0:T(8,128)S(1)}, f32[256,128]{1,0:T(8,128)S(1)}, f32[1,48,128]{2,1,0:T(8,128)S(1)}, f32[1,48,128]{2,1,0:T(8,128)S(1)}, f32[1,48,128...) custom-call(s32[2]{0:T(128)S(1)} %pad_add_fusion.place_ref, ...), custom_call_target="tpu_custom_call" | custom-call | tf_op jit(solution)/shard_map/couple/pallas_call | solution.py:458
  192.1 2.8 collective-permute-start.60
  204.8 2.9 collective-permute-start.74
  211.7 4.3 %couple.11 = (f32[192,128]{1,0:T(8,128)S(1)}, f32[256,128]{1,0:T(8,128)S(1)}, f32[1,48,128]{2,1,0:T(8,128)S(1)}, f32[1,48,128]{2,1,0:T(8,128)S(1)}, f32[1,48,128...) custom-call(s32[2]{0:T(128)S(1)} %pad_add_fusion.place_ref, ...), custom_call_target="tpu_custom_call" | custom-call | tf_op jit(solution)/shard_map/couple/pallas_call | solution.py:458
  237.0 2.5 collective-permute-start.94
  243.6 4.3 %couple.12 = (f32[192,128]{1,0:T(8,128)S(1)}, f32[256,128]{1,0:T(8,128)S(1)}, f32[1,48,128]{2,1,0:T(8,128)S(1)}, f32[1,48,128]{2,1,0:T(8,128)S(1)}, f32[1,48,128...) custom-call(s32[2]{0:T(128)S(1)} %pad_add_fusion.place_ref, ...), custom_call_target="tpu_custom_call" | custom-call | tf_op jit(solution)/shard_map/couple/pallas_call | solution.py:458
  255.7 2.8 collective-permute-start.100
  268.4 2.9 collective-permute-start.114
  275.3 4.3 %couple.13 = (f32[192,128]{1,0:T(8,128)S(1)}, f32[256,128]{1,0:T(8,128)S(1)}, f32[1,48,128]{2,1,0:T(8,128)S(1)}, f32[1,48,128]{2,1,0:T(8,128)S(1)}, f32[1,48,128...) custom-call(s32[2]{0:T(128)S(1)} %pad_add_fusion.place_ref, ...), custom_call_target="tpu_custom_call" | custom-call | tf_op jit(solution)/shard_map/couple/pallas_call | solution.py:458
  287.3 2.4 collective-permute-start.120
  300.4 2.5 collective-permute-start.134
  307.0 4.3 %couple.14 = (f32[192,128]{1,0:T(8,128)S(1)}, f32[256,128]{1,0:T(8,128)S(1)}, f32[1,48,128]{2,1,0:T(8,128)S(1)}, f32[1,48,128]{2,1,0:T(8,128)S(1)}, f32[1,48,128...) custom-call(s32[2]{0:T(128)S(1)} %pad_add_fusion.place_ref, ...), custom_call_target="tpu_custom_call" | custom-call | tf_op jit(solution)/shard_map/couple/pallas_call | solution.py:458
  319.1 2.8 collective-permute-start.140
  331.8 2.9 collective-permute-start.154
  338.7 4.3 %couple.15 = (f32[192,128]{1,0:T(8,128)S(1)}, f32[256,128]{1,0:T(8,128)S(1)}, f32[1,48,128]{2,1,0:T(8,128)S(1)}, f32[1,48,128]{2,1,0:T(8,128)S(1)}, f32[1,48,128...) custom-call(s32[2]{0:T(128)S(1)} %pad_add_fusion.place_ref, ...), custom_call_target="tpu_custom_call" | custom-call | tf_op jit(solution)/shard_map/couple/pallas_call | solution.py:458
  350.8 2.4 collective-permute-start.160
  361.4 2.9 collective-permute-start.165
  365.9 3.3 collective-permute-done.164.rest_2_.rest_6_
  370.1 2.9 products.1.rest_0_
  376.6 2.9 collective-permute-start.181
  390.5 31.2 %finish.1 = (bf16[8,192,16,256]{3,2,1,0:T(8,128)(2,1)}, f32[192,128]{1,0:T(8,128)S(1)}, f32[256,128]{1,0:T(8,128)S(1)}) custom-call(s32[2]{0:T(128)S(1)} %pad_add_fusion.place_ref, f32[192,256,128]{2,1,0:T(8,128)S(1)} %copy-done.2, f32[8,192,16,256]{3,2,1,0:T(8,128)} %get-tuple-element.133.barrier_hbm, f32[192,128]{1,0:T(8,128)S(1)} %copy.22.drow_ref, ...), custom_call_target="tpu_custom_call" | custom-call | tf_op jit(solution)/shard_map/finish/pallas_call | solution.py:485
  (412 shorter events, 221.2 us)
Async XLA Ops:
  86.7 7.6 %collective-permute-start.7 = (f32[2,32,128]{2,1,0:T(8,128)S(1)}, f32[2,32,128]{2,1,0:T(8,128)S(1)}, u32[]{:S(2)}, u32[]{:S(2)}) collective-permute-start(f32[2,32,128]{2,1,0:T(8,128)S(1)} %get-tuple-element.143), channel_id=1, source_target_pairs={{0,20},{4,24},{8,28},{12,0},{16,4},{20,8},{24,12},{28,16},{1,21},{... | collective-permute-start | bytes 98312 | tf_op jit(solution)/shard_map/ppermute | solution.py:344
  86.7 9.0 %collective-permute-start.8 = (f32[2,32,128]{2,1,0:T(8,128)S(1)}, f32[2,32,128]{2,1,0:T(8,128)S(1)}, u32[]{:S(2)}, u32[]{:S(2)}) collective-permute-start(f32[2,32,128]{2,1,0:T(8,128)S(1)} %get-tuple-element.144), channel_id=1, source_target_pairs={{0,24},{4,28},{8,0},{12,4},{16,8},{20,12},{24,16},{28,20},{1,25},{... | collective-permute-start | bytes 98312 | tf_op jit(solution)/shard_map/ppermute | solution.py:344
  87.9 7.8 %collective-permute-start.9 = (f32[2,32,128]{2,1,0:T(8,128)S(1)}, f32[2,32,128]{2,1,0:T(8,128)S(1)}, u32[]{:S(2)}, u32[]{:S(2)}) collective-permute-start(f32[2,32,128]{2,1,0:T(8,128)S(1)} %get-tuple-element.145), channel_id=1, source_target_pairs={{0,28},{4,0},{8,4},{12,8},{16,12},{20,16},{24,20},{28,24},{1,29},{... | collective-permute-start | bytes 98312 | tf_op jit(solution)/shard_map/ppermute | solution.py:344
  99.5 9.4 %collective-permute-start.12 = (f32[48,128]{1,0:T(8,128)S(1)}, f32[48,128]{1,0:T(8,128)S(1)}, u32[]{:S(2)}, u32[]{:S(2)}) collective-permute-start(f32[48,128]{1,0:T(8,128)S(1)} %fusion.rest_0_.rest_16_), channel_id=1, source_target_pairs={{0,3},{1,0},{2,1},{3,2},{4,7},{5,4},{6,5},{7,6},{8,11},{9,8},{10,9... | collective-permute-start | bytes 73736 | tf_op jit(solution)/shard_map/ppermute | solution.py:344
  123.8 7.8 %collective-permute-start.29 = (f32[1,32,128]{2,1,0:T(8,128)S(1)}, f32[1,32,128]{2,1,0:T(8,128)S(1)}, u32[]{:S(2)}, u32[]{:S(2)}) collective-permute-start(f32[1,32,128]{2,1,0:T(8,128)S(1)} %get-tuple-element.154), channel_id=1, source_target_pairs={{0,16},{4,20},{8,24},{12,28},{16,0},{20,4},{24,8},{28,12},{1,17},{... | collective-permute-start | bytes 49160 | tf_op jit(solution)/shard_map/ppermute | solution.py:344
  125.4 8.5 %collective-permute-start.31 = (f32[1,32,128]{2,1,0:T(8,128)S(1)}, f32[1,32,128]{2,1,0:T(8,128)S(1)}, u32[]{:S(2)}, u32[]{:S(2)}) collective-permute-start(f32[1,32,128]{2,1,0:T(8,128)S(1)} %get-tuple-element.156), channel_id=1, source_target_pairs={{0,24},{4,28},{8,0},{12,4},{16,8},{20,12},{24,16},{28,20},{1,25},{... | collective-permute-start | bytes 49160 | tf_op jit(solution)/shard_map/ppermute | solution.py:344
  138.9 9.4 %collective-permute-start.25 = (f32[48,128]{1,0:T(8,128)S(1)}, f32[48,128]{1,0:T(8,128)S(1)}, u32[]{:S(2)}, u32[]{:S(2)}) collective-permute-start(f32[48,128]{1,0:T(8,128)S(1)} %bitcast_divide_fusion.7.rest_0_.rest_17_), channel_id=1, source_target_pairs={{0,3},{1,0},{2,1},{3,2},{4,7},{5,4},{6,5},{7,6},{8,11},{9,8},{10,9... | collective-permute-start | bytes 73736 | tf_op jit(solution)/shard_map/ppermute | solution.py:344
  140.5 7.8 %collective-permute-start.24 = (f32[48,128]{1,0:T(8,128)S(1)}, f32[48,128]{1,0:T(8,128)S(1)}, u32[]{:S(2)}, u32[]{:S(2)}) collective-permute-start(f32[48,128]{1,0:T(8,128)S(1)} %bitcast_divide_fusion.7.rest_0_.rest_17_), channel_id=1, source_target_pairs={{0,2},{1,3},{2,0},{3,1},{4,6},{5,7},{6,4},{7,5},{8,10},{9,11},{10,... | collective-permute-start | bytes 73736 | tf_op jit(solution)/shard_map/ppermute | solution.py:344
  157.1 7.6 %collective-permute-start.50 = (f32[1,32,128]{2,1,0:T(8,128)S(1)}, f32[1,32,128]{2,1,0:T(8,128)S(1)}, u32[]{:S(2)}, u32[]{:S(2)}) collective-permute-start(f32[1,32,128]{2,1,0:T(8,128)S(1)} %get-tuple-element.167), channel_id=1, source_target_pairs={{0,20},{4,24},{8,28},{12,0},{16,4},{20,8},{24,12},{28,16},{1,21},{... | collective-permute-start | bytes 49160 | tf_op jit(solution)/shard_map/ppermute | solution.py:344
  157.1 8.1 %collective-permute-start.51 = (f32[1,32,128]{2,1,0:T(8,128)S(1)}, f32[1,32,128]{2,1,0:T(8,128)S(1)}, u32[]{:S(2)}, u32[]{:S(2)}) collective-permute-start(f32[1,32,128]{2,1,0:T(8,128)S(1)} %get-tuple-element.168), channel_id=1, source_target_pairs={{0,24},{4,28},{8,0},{12,4},{16,8},{20,12},{24,16},{28,20},{1,25},{... | collective-permute-start | bytes 49160 | tf_op jit(solution)/shard_map/ppermute | solution.py:344
  170.4 9.7 %collective-permute-start.45 = (f32[48,128]{1,0:T(8,128)S(1)}, f32[48,128]{1,0:T(8,128)S(1)}, u32[]{:S(2)}, u32[]{:S(2)}) collective-permute-start(f32[48,128]{1,0:T(8,128)S(1)} %bitcast_divide_fusion.6.rest_0_.rest_18_), channel_id=1, source_target_pairs={{0,3},{1,0},{2,1},{3,2},{4,7},{5,4},{6,5},{7,6},{8,11},{9,8},{10,9... | collective-permute-start | bytes 73736 | tf_op jit(solution)/shard_map/ppermute | solution.py:344
  172.4 7.6 %collective-permute-start.44 = (f32[48,128]{1,0:T(8,128)S(1)}, f32[48,128]{1,0:T(8,128)S(1)}, u32[]{:S(2)}, u32[]{:S(2)}) collective-permute-start(f32[48,128]{1,0:T(8,128)S(1)} %bitcast_divide_fusion.6.rest_0_.rest_18_), channel_id=1, source_target_pairs={{0,2},{1,3},{2,0},{3,1},{4,6},{5,7},{6,4},{7,5},{8,10},{9,11},{10,... | collective-permute-start | bytes 73736 | tf_op jit(solution)/shard_map/ppermute | solution.py:344
  187.2 7.8 %collective-permute-start.69 = (f32[1,32,128]{2,1,0:T(8,128)S(1)}, f32[1,32,128]{2,1,0:T(8,128)S(1)}, u32[]{:S(2)}, u32[]{:S(2)}) collective-permute-start(f32[1,32,128]{2,1,0:T(8,128)S(1)} %get-tuple-element.178), channel_id=1, source_target_pairs={{0,16},{4,20},{8,24},{12,28},{16,0},{20,4},{24,8},{28,12},{1,17},{... | collective-permute-start | bytes 49160 | tf_op jit(solution)/shard_map/ppermute | solution.py:344
  188.5 8.9 %collective-permute-start.71 = (f32[1,32,128]{2,1,0:T(8,128)S(1)}, f32[1,32,128]{2,1,0:T(8,128)S(1)}, u32[]{:S(2)}, u32[]{:S(2)}) collective-permute-start(f32[1,32,128]{2,1,0:T(8,128)S(1)} %get-tuple-element.180), channel_id=1, source_target_pairs={{0,24},{4,28},{8,0},{12,4},{16,8},{20,12},{24,16},{28,20},{1,25},{... | collective-permute-start | bytes 49160 | tf_op jit(solution)/shard_map/ppermute | solution.py:344
  202.3 9.4 %collective-permute-start.65 = (f32[48,128]{1,0:T(8,128)S(1)}, f32[48,128]{1,0:T(8,128)S(1)}, u32[]{:S(2)}, u32[]{:S(2)}) collective-permute-start(f32[48,128]{1,0:T(8,128)S(1)} %bitcast_divide_fusion.5.rest_0_.rest_19_), channel_id=1, source_target_pairs={{0,3},{1,0},{2,1},{3,2},{4,7},{5,4},{6,5},{7,6},{8,11},{9,8},{10,9... | collective-permute-start | bytes 73736 | tf_op jit(solution)/shard_map/ppermute | solution.py:344
  203.9 7.8 %collective-permute-start.64 = (f32[48,128]{1,0:T(8,128)S(1)}, f32[48,128]{1,0:T(8,128)S(1)}, u32[]{:S(2)}, u32[]{:S(2)}) collective-permute-start(f32[48,128]{1,0:T(8,128)S(1)} %bitcast_divide_fusion.5.rest_0_.rest_19_), channel_id=1, source_target_pairs={{0,2},{1,3},{2,0},{3,1},{4,6},{5,7},{6,4},{7,5},{8,10},{9,11},{10,... | collective-permute-start | bytes 73736 | tf_op jit(solution)/shard_map/ppermute | solution.py:344
  220.5 8.1 %collective-permute-start.91 = (f32[1,32,128]{2,1,0:T(8,128)S(1)}, f32[1,32,128]{2,1,0:T(8,128)S(1)}, u32[]{:S(2)}, u32[]{:S(2)}) collective-permute-start(f32[1,32,128]{2,1,0:T(8,128)S(1)} %get-tuple-element.192), channel_id=1, source_target_pairs={{0,24},{4,28},{8,0},{12,4},{16,8},{20,12},{24,16},{28,20},{1,25},{... | collective-permute-start | bytes 49160 | tf_op jit(solution)/shard_map/ppermute | solution.py:344
  233.8 9.8 %collective-permute-start.85 = (f32[48,128]{1,0:T(8,128)S(1)}, f32[48,128]{1,0:T(8,128)S(1)}, u32[]{:S(2)}, u32[]{:S(2)}) collective-permute-start(f32[48,128]{1,0:T(8,128)S(1)} %bitcast_divide_fusion.4.rest_0_.rest_20_), channel_id=1, source_target_pairs={{0,3},{1,0},{2,1},{3,2},{4,7},{5,4},{6,5},{7,6},{8,11},{9,8},{10,9... | collective-permute-start | bytes 73736 | tf_op jit(solution)/shard_map/ppermute | solution.py:344
  236.0 7.6 %collective-permute-start.84 = (f32[48,128]{1,0:T(8,128)S(1)}, f32[48,128]{1,0:T(8,128)S(1)}, u32[]{:S(2)}, u32[]{:S(2)}) collective-permute-start(f32[48,128]{1,0:T(8,128)S(1)} %bitcast_divide_fusion.4.rest_0_.rest_20_), channel_id=1, source_target_pairs={{0,2},{1,3},{2,0},{3,1},{4,6},{5,7},{6,4},{7,5},{8,10},{9,11},{10,... | collective-permute-start | bytes 73736 | tf_op jit(solution)/shard_map/ppermute | solution.py:344
  250.7 7.8 %collective-permute-start.109 = (f32[1,32,128]{2,1,0:T(8,128)S(1)}, f32[1,32,128]{2,1,0:T(8,128)S(1)}, u32[]{:S(2)}, u32[]{:S(2)}) collective-permute-start(f32[1,32,128]{2,1,0:T(8,128)S(1)} %get-tuple-element.202), channel_id=1, source_target_pairs={{0,16},{4,20},{8,24},{12,28},{16,0},{20,4},{24,8},{28,12},{1,17},{... | collective-permute-start | bytes 49160 | tf_op jit(solution)/shard_map/ppermute | solution.py:344
  252.1 8.9 %collective-permute-start.111 = (f32[1,32,128]{2,1,0:T(8,128)S(1)}, f32[1,32,128]{2,1,0:T(8,128)S(1)}, u32[]{:S(2)}, u32[]{:S(2)}) collective-permute-start(f32[1,32,128]{2,1,0:T(8,128)S(1)} %get-tuple-element.204), channel_id=1, source_target_pairs={{0,24},{4,28},{8,0},{12,4},{16,8},{20,12},{24,16},{28,20},{1,25},{... | collective-permute-start | bytes 49160 | tf_op jit(solution)/shard_map/ppermute | solution.py:344
  265.9 9.4 %collective-permute-start.105 = (f32[48,128]{1,0:T(8,128)S(1)}, f32[48,128]{1,0:T(8,128)S(1)}, u32[]{:S(2)}, u32[]{:S(2)}) collective-permute-start(f32[48,128]{1,0:T(8,128)S(1)} %bitcast_divide_fusion.3.rest_0_.rest_21_), channel_id=1, source_target_pairs={{0,3},{1,0},{2,1},{3,2},{4,7},{5,4},{6,5},{7,6},{8,11},{9,8},{10,9... | collective-permute-start | bytes 73736 | tf_op jit(solution)/shard_map/ppermute | solution.py:344
  267.5 7.8 %collective-permute-start.104 = (f32[48,128]{1,0:T(8,128)S(1)}, f32[48,128]{1,0:T(8,128)S(1)}, u32[]{:S(2)}, u32[]{:S(2)}) collective-permute-start(f32[48,128]{1,0:T(8,128)S(1)} %bitcast_divide_fusion.3.rest_0_.rest_21_), channel_id=1, source_target_pairs={{0,2},{1,3},{2,0},{3,1},{4,6},{5,7},{6,4},{7,5},{8,10},{9,11},{10,... | collective-permute-start | bytes 73736 | tf_op jit(solution)/shard_map/ppermute | solution.py:344
  284.1 8.1 %collective-permute-start.131 = (f32[1,32,128]{2,1,0:T(8,128)S(1)}, f32[1,32,128]{2,1,0:T(8,128)S(1)}, u32[]{:S(2)}, u32[]{:S(2)}) collective-permute-start(f32[1,32,128]{2,1,0:T(8,128)S(1)} %get-tuple-element.216), channel_id=1, source_target_pairs={{0,24},{4,28},{8,0},{12,4},{16,8},{20,12},{24,16},{28,20},{1,25},{... | collective-permute-start | bytes 49160 | tf_op jit(solution)/shard_map/ppermute | solution.py:344
  297.4 9.7 %collective-permute-start.125 = (f32[48,128]{1,0:T(8,128)S(1)}, f32[48,128]{1,0:T(8,128)S(1)}, u32[]{:S(2)}, u32[]{:S(2)}) collective-permute-start(f32[48,128]{1,0:T(8,128)S(1)} %bitcast_divide_fusion.2.rest_0_.rest_22_), channel_id=1, source_target_pairs={{0,3},{1,0},{2,1},{3,2},{4,7},{5,4},{6,5},{7,6},{8,11},{9,8},{10,9... | collective-permute-start | bytes 73736 | tf_op jit(solution)/shard_map/ppermute | solution.py:344
  299.4 7.6 %collective-permute-start.124 = (f32[48,128]{1,0:T(8,128)S(1)}, f32[48,128]{1,0:T(8,128)S(1)}, u32[]{:S(2)}, u32[]{:S(2)}) collective-permute-start(f32[48,128]{1,0:T(8,128)S(1)} %bitcast_divide_fusion.2.rest_0_.rest_22_), channel_id=1, source_target_pairs={{0,2},{1,3},{2,0},{3,1},{4,6},{5,7},{6,4},{7,5},{8,10},{9,11},{10,... | collective-permute-start | bytes 73736 | tf_op jit(solution)/shard_map/ppermute | solution.py:344
  314.1 7.8 %collective-permute-start.149 = (f32[1,32,128]{2,1,0:T(8,128)S(1)}, f32[1,32,128]{2,1,0:T(8,128)S(1)}, u32[]{:S(2)}, u32[]{:S(2)}) collective-permute-start(f32[1,32,128]{2,1,0:T(8,128)S(1)} %get-tuple-element.226), channel_id=1, source_target_pairs={{0,16},{4,20},{8,24},{12,28},{16,0},{20,4},{24,8},{28,12},{1,17},{... | collective-permute-start | bytes 49160 | tf_op jit(solution)/shard_map/ppermute | solution.py:344
  315.5 8.9 %collective-permute-start.151 = (f32[1,32,128]{2,1,0:T(8,128)S(1)}, f32[1,32,128]{2,1,0:T(8,128)S(1)}, u32[]{:S(2)}, u32[]{:S(2)}) collective-permute-start(f32[1,32,128]{2,1,0:T(8,128)S(1)} %get-tuple-element.228), channel_id=1, source_target_pairs={{0,24},{4,28},{8,0},{12,4},{16,8},{20,12},{24,16},{28,20},{1,25},{... | collective-permute-start | bytes 49160 | tf_op jit(solution)/shard_map/ppermute | solution.py:344
  329.3 9.4 %collective-permute-start.145 = (f32[48,128]{1,0:T(8,128)S(1)}, f32[48,128]{1,0:T(8,128)S(1)}, u32[]{:S(2)}, u32[]{:S(2)}) collective-permute-start(f32[48,128]{1,0:T(8,128)S(1)} %bitcast_divide_fusion.1.rest_0_.rest_23_), channel_id=1, source_target_pairs={{0,3},{1,0},{2,1},{3,2},{4,7},{5,4},{6,5},{7,6},{8,11},{9,8},{10,9... | collective-permute-start | bytes 73736 | tf_op jit(solution)/shard_map/ppermute | solution.py:344
  330.9 7.8 %collective-permute-start.144 = (f32[48,128]{1,0:T(8,128)S(1)}, f32[48,128]{1,0:T(8,128)S(1)}, u32[]{:S(2)}, u32[]{:S(2)}) collective-permute-start(f32[48,128]{1,0:T(8,128)S(1)} %bitcast_divide_fusion.1.rest_0_.rest_23_), channel_id=1, source_target_pairs={{0,2},{1,3},{2,0},{3,1},{4,6},{5,7},{6,4},{7,5},{8,10},{9,11},{10,... | collective-permute-start | bytes 73736 | tf_op jit(solution)/shard_map/ppermute | solution.py:344
  347.5 7.7 %collective-permute-start.170 = (f32[1,32,128]{2,1,0:T(8,128)S(1)}, f32[1,32,128]{2,1,0:T(8,128)S(1)}, u32[]{:S(2)}, u32[]{:S(2)}) collective-permute-start(f32[1,32,128]{2,1,0:T(8,128)S(1)} %get-tuple-element.239), channel_id=1, source_target_pairs={{0,20},{4,24},{8,28},{12,0},{16,4},{20,8},{24,12},{28,16},{1,21},{... | collective-permute-start | bytes 49160 | tf_op jit(solution)/shard_map/ppermute | solution.py:344
  347.5 8.2 %collective-permute-start.171 = (f32[1,32,128]{2,1,0:T(8,128)S(1)}, f32[1,32,128]{2,1,0:T(8,128)S(1)}, u32[]{:S(2)}, u32[]{:S(2)}) collective-permute-start(f32[1,32,128]{2,1,0:T(8,128)S(1)} %get-tuple-element.240), channel_id=1, source_target_pairs={{0,24},{4,28},{8,0},{12,4},{16,8},{20,12},{24,16},{28,20},{1,25},{... | collective-permute-start | bytes 49160 | tf_op jit(solution)/shard_map/ppermute | solution.py:344
  (169 other events, 1037.5 us)

commit v2 on v0

v2 whole, which is shorter than its diff:
```python
import functools

import jax
import jax.numpy as jnp
from jax import lax
from jax.experimental import pallas as pl
from jax.experimental.pallas import tpu as pltpu
from jax.sharding import PartitionSpec as P

WEIGHT_ATTACK = 8.0
SHIFT_DIAG = 1.0
BLOCK = 8
LANES = 128
VMEM_MIB = 12
VMEM_SPEC = pl.BlockSpec(memory_space=pltpu.VMEM)
SMEM_SPEC = pl.BlockSpec(memory_space=pltpu.SMEM)
ANY_SPEC = pl.BlockSpec(memory_space=pl.ANY)
F32 = jnp.float32


def shape(*dims):
    return jax.ShapeDtypeStruct(dims, F32)


def params():
    return pltpu.CompilerParams(vmem_limit_bytes=VMEM_MIB * 1024 * 1024)


def inverse(x):
    rough = pl.reciprocal(x, approx=True)
    return rough * (2.0 - x * rough)


def widen(rows):
    return jnp.broadcast_to(rows[:, None, :], (BLOCK, 8, LANES))


def prepare_kernel(
    rows, sizes, inds, probs, nind,
    place_ref, flag_ref, region_ref, column_ref,
    pos_hbm, low_hbm, high_hbm, upper_hbm, supp_hbm, drow_ref, dcol_ref,
    scaling_ref, barrier_hbm, row_ref, col_ref,
    tile_s, tile_m, up_s, act_s, col_m, col_e,
):
    my_reg, my_ind = place_ref[0], place_ref[1]
    blocks = rows // BLOCK
    half = inds // LANES
    col_m[...] = jnp.zeros_like(col_m)
    col_e[...] = jnp.zeros_like(col_e)
    col_ref[...] = jnp.zeros_like(col_ref)

    def turn(slot, before, r):
        scaling_ref[before * BLOCK + r] = tile_s[slot, r].T

    def sums(slot, before):
        r0 = pl.multiple_of(before * BLOCK, BLOCK)
        here = pl.ds(r0, BLOCK)
        drow = drow_ref[here, :]
        row_wide = widen(drow)
        sum_acc = jnp.zeros((BLOCK, 8, LANES), F32)
        dual_acc = jnp.zeros((BLOCK, 8, LANES), F32)
        for i0 in range(0, inds, 8):
            tile = scaling_ref[here, i0 : i0 + 8, :]
            sum_acc = sum_acc + tile
            dual_acc = dual_acc + tile * dcol_ref[i0 : i0 + 8, :][None]
            col_ref[1, i0 : i0 + 8, :] += jnp.sum(tile, axis=0)
            col_e[i0 : i0 + 8, :] += jnp.sum(tile * row_wide, axis=0)
        total = jnp.sum(sum_acc, axis=1)
        margin = lax.dot_general(
            jnp.ones((8, LANES), F32),
            tile_m[slot].reshape(BLOCK * LANES, LANES),
            (((1,), (1,)), ((), ())),
            precision=lax.Precision.HIGHEST,
            preferred_element_type=F32,
        )
        margin = jnp.concatenate([margin[:1, r * LANES : (r + 1) * LANES] for r in range(BLOCK)], axis=0)
        row_ref[1, here, :] = total
        row_ref[0, here, :] = margin - drow * total - jnp.sum(dual_acc, axis=1)

    def body(pos_ref, low_ref, high_ref, upper_ref, supp_ref, barrier_ref):
        block = pl.program_id(0)
        slot = lax.rem(block, 2)
        other = 1 - slot
        before = jnp.maximum(block - 1, 0)
        r0 = block * BLOCK
        up_s[...] = upper_ref[...].astype(F32)
        act_s[...] = supp_ref[...].astype(F32)

        def problem(k, _, attacked):
            turn(other, before, k)
            total = jnp.zeros((sizes, inds), F32)
            place = pl.ds(pl.multiple_of(k * sizes, sizes), sizes)
            for r in range(BLOCK):
                upper = up_s[r]
                active = act_s[r]
                if attacked:
                    own = (region_ref[k] == my_reg * rows + r0 + r).astype(jnp.int32)
                    column = lax.broadcasted_iota(jnp.int32, (sizes, inds), 0) * (inds * nind)
                    column = column + lax.broadcasted_iota(jnp.int32, (sizes, inds), 1) + my_ind * inds
                    hit = column == jnp.where(own == 1, column_ref[k], -1)
                    active = jnp.where(hit, jnp.ones_like(active), active)
                value = pos_ref[k, r].astype(F32) * upper
                slack = upper - value
                den = low_ref[k, r].astype(F32) * slack + high_ref[k, r].astype(F32) * value
                ratio = active * inverse(den)
                scaling = value * slack * ratio
                middle = 0.5 * upper - value
                barrier = middle * ratio
                if attacked:
                    barrier = barrier + jnp.where(hit, WEIGHT_ATTACK * scaling, jnp.zeros_like(scaling))
                margin = middle * active + barrier
                barrier_ref[k, r] = barrier
                tile_s[slot, r, place, :] = scaling
                folded = margin[:, :LANES]
                for part in range(1, half):
                    folded = folded + margin[:, part * LANES : (part + 1) * LANES]
                tile_m[slot, r, place, :] = folded
                total = total + margin
            col_m[place, :] += total
            return 0

        hits = flag_ref[block]

        @pl.when(hits == 0)
        def _():
            lax.fori_loop(0, probs, functools.partial(problem, attacked=False), 0)

        @pl.when(hits != 0)
        def _():
            lax.fori_loop(0, probs, functools.partial(problem, attacked=True), 0)

        @pl.when(block > 0)
        def _():
            sums(other, before)

    cells = pl.BlockSpec((probs, BLOCK, sizes, inds), lambda b: (0, b, 0, 0))
    shared = pl.BlockSpec((BLOCK, sizes, inds), lambda b: (b, 0, 0))
    pltpu.emit_pipeline(
        body, grid=(blocks,), in_specs=[cells, cells, cells, shared, shared], out_specs=[cells]
    )(pos_hbm, low_hbm, high_hbm, upper_hbm, supp_hbm, barrier_hbm)
    last = blocks - 1
    for r in range(BLOCK):
        turn(last % 2, last, r)
    sums(last % 2, last)
    col_ref[0] = col_m[...].T - dcol_ref[...] * col_ref[1] - col_e[...]


def add_up(refs):
    values = [ref[...] for ref in refs]
    while len(values) > 1:
        values = [values[j] + values[j + 1] for j in range(0, len(values), 2)]
    return values[0]


def join_kernel(nrow, ncol, *refs):
    ins, outs = refs[: nrow + ncol], refs[nrow + ncol :]
    outs = list(outs)
    if nrow:
        outs.pop(0)[...] = add_up(ins[:nrow])
    if ncol:
        outs.pop(0)[...] = add_up(ins[nrow:])


def begin_kernel(nrow, ncol, *refs):
    row_diag, col_diag, row_now, col_now = refs[nrow + ncol :]
    for ins, diag, now in ((refs[:nrow], row_diag, row_now), (refs[nrow : nrow + ncol], col_diag, col_now)):
        both = add_up(ins)
        width = both[1] + SHIFT_DIAG
        diag[...] = width
        now[...] = both[0] / width


def couple_kernel(nrow, ncol, scaled, scaling_ref, row_diag, col_diag, *refs):
    row_now, col_now, row_out, col_out = refs[nrow + ncol :]
    rows, inds, _ = scaling_ref.shape
    if scaled:
        row_now[...] = add_up(refs[:nrow]) / row_diag[...]
        col_now[...] = add_up(refs[nrow : nrow + ncol]) / col_diag[...]
    else:
        row_now[...] = refs[0][...]
        col_now[...] = refs[1][...]
    col_out[...] = jnp.zeros_like(col_out)

    def step(block, _):
        here = pl.ds(pl.multiple_of(block * BLOCK, BLOCK), BLOCK)
        row_wide = widen(row_now[here, :])
        acc = jnp.zeros((BLOCK, 8, LANES), F32)
        for i0 in range(0, inds, 8):
            tile = scaling_ref[here, i0 : i0 + 8, :]
            acc = acc + tile * col_now[i0 : i0 + 8, :][None]
            col_out[i0 : i0 + 8, :] += jnp.sum(tile * row_wide, axis=0)
        row_out[here, :] = jnp.sum(acc, axis=1)
        return 0

    lax.fori_loop(0, rows // BLOCK, step, 0)


def products_kernel(iters, nreg, nind, nrow, ncol, scaling_ref, row_diag_ref, col_diag_ref, *rest):
    row_ins, col_ins, rest = rest[:nrow], rest[nrow : nrow + ncol], rest[nrow + ncol :]
    count = 3 * iters - 1
    row_old, col_old = rest[:count], rest[count : 2 * count]
    row_now, col_now, out_ref, row_z, col_z = rest[2 * count :]
    row_now[...] = add_up(row_ins) / row_diag_ref[...]
    col_now[...] = add_up(col_ins) / col_diag_ref[...]
    row_p = [ref[...] for ref in row_old] + [row_now[...]]
    col_p = [ref[...] for ref in col_old] + [col_now[...]]
    rows, inds, _ = scaling_ref.shape
    row_zs = [row_p[3 * j] - row_p[3 * j + 1] + row_p[3 * j + 2] for j in range(iters)]
    col_zs = [col_p[3 * j] - col_p[3 * j + 1] + col_p[3 * j + 2] for j in range(iters)]
    row_z[...] = row_zs[-1]
    col_z[...] = col_zs[-1]

    def step(block, acc):
        here = pl.ds(pl.multiple_of(block * BLOCK, BLOCK), BLOCK)
        part = jnp.zeros((BLOCK, 8, LANES), F32)
        for i0 in range(0, inds, 8):
            part = part + scaling_ref[here, i0 : i0 + 8, :] * col_z[i0 : i0 + 8, :][None]
        return acc + jnp.sum(part, axis=1) * row_z[here, :]

    cross = lax.fori_loop(0, rows // BLOCK, step, jnp.zeros((BLOCK, LANES), F32))
    cross = 2.0 * jnp.sum(cross, axis=0, keepdims=True)
    row_diag, col_diag = row_diag_ref[...], col_diag_ref[...]

    def dot(j, row_v, col_v):
        row_sum = jnp.sum(row_zs[j] * row_v, axis=0, keepdims=True)
        col_sum = jnp.sum(col_zs[j] * col_v, axis=0, keepdims=True)
        return row_sum * (1.0 / nind) + col_sum * (1.0 / nreg)

    out_ref[...] = jnp.zeros_like(out_ref)
    slot = 0
    row_n, col_n = row_diag * row_p[0], col_diag * col_p[0]
    for j in range(iters):
        out_ref[slot : slot + 1, :] = dot(j, row_n, col_n)
        slot += 1
    for m in range(iters):
        last = m + 1 == iters
        row_n = row_diag * (row_zs[m] if last else row_p[3 * m] + row_p[3 * m + 3])
        col_n = col_diag * (col_zs[m] if last else col_p[3 * m] + col_p[3 * m + 3])
        for j in range(m, iters):
            product = dot(j, row_n, col_n)
            out_ref[slot : slot + 1, :] = product + cross if last else product
            slot += 1


def finish_kernel(
    rows, sizes, inds, probs, iters, sums_ref, scaling_ref, barrier_hbm, drow_ref, dcol_ref, *rest
):
    count = 3 * iters
    row_p, col_p = rest[:count], rest[count : 2 * count]
    cell_hbm, row_ref, col_ref, row_add, col_add = rest[2 * count :]
    lane = lax.broadcasted_iota(jnp.int32, (LANES, LANES), 0) // sizes
    other = lax.broadcasted_iota(jnp.int32, (LANES, LANES), 1) // sizes
    same = (lane == other).astype(F32)
    total = jnp.dot(sums_ref[...], same, preferred_element_type=F32, precision=lax.Precision.HIGHEST)
    g0, g1, g2, h00, h10, h20, h11, h21, h22 = [total[j : j + 1, :] for j in range(9)]
    l1, l2 = h10 / h00, h20 / h00
    d1 = h11 - l1 * h10
    t21 = h21 - l2 * h10
    m21 = t21 / d1
    d2 = h22 - l2 * h20 - m21 * t21
    y1 = g1 - l1 * g0
    y2 = g2 - l2 * g0 - m21 * y1
    c2 = y2 / d2
    c1 = y1 / d1 - m21 * c2
    c0 = g0 / h00 - l1 * c1 - l2 * c2

    def combine(refs):
        acc = None
        for j, coef in enumerate((c0, c1, c2)):
            term = coef * (refs[3 * j][...] - refs[3 * j + 1][...] + refs[3 * j + 2][...])
            acc = term if acc is None else acc + term
        return acc

    row_y = combine(row_p)
    col_y = combine(col_p)
    row_ref[...] = row_y
    col_ref[...] = col_y
    row_add[...] = row_y + drow_ref[...]
    col_add[...] = col_y + dcol_ref[...]

    def body(barrier_ref, cell_ref):
        r0 = pl.program_id(0) * BLOCK
        for r in range(BLOCK):
            moved = (col_add[...] + row_add[pl.ds(r0 + r, 1), :]) * scaling_ref[r0 + r]
            moved = moved.T
            for k in range(probs):
                cell_ref[k, r] = (moved[k * sizes : (k + 1) * sizes, :] - barrier_ref[k, r]).astype(jnp.bfloat16)

    cells = pl.BlockSpec((probs, BLOCK, sizes, inds), lambda b: (0, b, 0, 0))
    pltpu.emit_pipeline(body, grid=(rows // BLOCK,), in_specs=[cells], out_specs=[cells])(barrier_hbm, cell_hbm)


def stages(count, most):
    bits = [1 << j for j in range(count.bit_length() - 1)]
    if most == 1:
        return [[bit] for bit in bits]
    return [bits[:1]] + [bits[j : j + most] for j in range(1, len(bits), most)]


def exchange(x, axis, count, bits):
    flips = [0]
    for bit in bits:
        flips = flips + [flip | bit for flip in flips]
    return [x] + [lax.ppermute(x, axis, [(j, j ^ flip) for j in range(count)]) for flip in flips[1:]]


def vmem_call(kernel, outs, name, scratch=()):
    def call(*args):
        return pl.pallas_call(
            kernel,
            out_shape=outs,
            in_specs=[VMEM_SPEC] * len(args),
            out_specs=[VMEM_SPEC] * len(outs),
            scratch_shapes=list(scratch),
            compiler_params=params(),
            name=name,
        )(*args)

    return call


def both_sums(row, col, nreg, nind):
    row_stages, col_stages = stages(nind, 1), stages(nreg, 2)
    row_parts, col_parts = [row], [col]
    for j in range(max(len(row_stages), len(col_stages))):
        with_row, with_col = j < len(row_stages), j < len(col_stages)
        if j:
            ins = (row_parts if with_row else []) + (col_parts if with_col else [])
            outs = [row.shape] * with_row + [col.shape] * with_col
            kernel = functools.partial(
                join_kernel, len(row_parts) if with_row else 0, len(col_parts) if with_col else 0
            )
            summed = list(vmem_call(kernel, [shape(*dims) for dims in outs], "join")(*ins))
            if with_row:
                row = summed.pop(0)
            if with_col:
                col = summed.pop(0)
        if with_row:
            row_parts = exchange(row, "industry", nind, row_stages[j])
        if with_col:
            col_parts = exchange(col, "region", nreg, col_stages[j])
    return row_parts, col_parts


def total_over(x, axis, count):
    for bits in stages(count, 1):
        own, other = exchange(x, axis, count, bits)
        x = own + other
    return x


def local(
    nreg, nind, iters,
    position, dual_lower, dual_upper, upper_bound, suppressed,
    attack_region, attack_column, dual_row, dual_col,
):
    probs, rows, sizes, inds = position.shape
    my_reg, my_ind = lax.axis_index("region"), lax.axis_index("industry")
    place = jnp.stack([my_reg, my_ind]).astype(jnp.int32)
    blocks = rows // BLOCK
    first = my_reg * rows + BLOCK * jnp.arange(blocks, dtype=jnp.int32)
    near = (attack_region[None, :] >= first[:, None]) & (attack_region[None, :] < first[:, None] + BLOCK)
    flags = jnp.any(near, axis=1).astype(jnp.int32)
    drow = dual_row.transpose(1, 0, 2).reshape(rows, LANES)
    dcol = dual_col.reshape(LANES, inds).T

    def in_hbm(x):
        return pltpu.with_memory_space_constraint(x, pltpu.HBM)

    def keep(x):
        return pltpu.with_memory_space_constraint(x, pltpu.VMEM)

    scaling, barrier, row_both, col_both = pl.pallas_call(
        functools.partial(prepare_kernel, rows, sizes, inds, probs, nind),
        out_shape=[
            pltpu.VMEM((rows, inds, LANES), F32),
            shape(probs, rows, sizes, inds),
            shape(2, rows, LANES),
            shape(2, inds, LANES),
        ],
        in_specs=[SMEM_SPEC] * 4 + [ANY_SPEC] * 5 + [VMEM_SPEC] * 2,
        out_specs=[VMEM_SPEC, ANY_SPEC, VMEM_SPEC, VMEM_SPEC],
        scratch_shapes=[
            pltpu.VMEM((2, BLOCK, LANES, inds), F32),
            pltpu.VMEM((2, BLOCK, LANES, LANES), F32),
            pltpu.VMEM((BLOCK, sizes, inds), F32),
            pltpu.VMEM((BLOCK, sizes, inds), F32),
            pltpu.VMEM((LANES, inds), F32),
            pltpu.VMEM((inds, LANES), F32),
        ],
        compiler_params=params(),
        name="prepare",
    )(
        place, flags, attack_region, attack_column,
        *map(in_hbm, (position, dual_lower, dual_upper, upper_bound, suppressed)), drow, dcol,
    )
    scaling = keep(scaling)
    margins = [shape(rows, LANES), shape(inds, LANES)]
    row_parts, col_parts = both_sums(row_both, col_both, nreg, nind)
    kernel = functools.partial(begin_kernel, len(row_parts), len(col_parts))
    row_diag, col_diag, row_now, col_now = vmem_call(kernel, margins * 2, "begin")(*row_parts, *col_parts)
    row_parts, col_parts = [row_now], [col_now]
    row_p, col_p = [], []
    for j in range(3 * iters - 1):
        kernel = functools.partial(couple_kernel, len(row_parts), len(col_parts), j > 0)
        row_now, col_now, row_out, col_out = vmem_call(kernel, margins * 2, "couple")(
            scaling, row_diag, col_diag, *row_parts, *col_parts
        )
        row_p.append(row_now)
        col_p.append(col_now)
        row_parts, col_parts = both_sums(row_out, col_out, nreg, nind)
    kernel = functools.partial(products_kernel, iters, nreg, nind, len(row_parts), len(col_parts))
    scratch = [pltpu.VMEM((rows, LANES), F32), pltpu.VMEM((inds, LANES), F32)]
    row_now, col_now, part = vmem_call(kernel, margins + [shape(16, LANES)], "products", scratch)(
        scaling, row_diag, col_diag, *row_parts, *col_parts, *row_p, *col_p
    )
    row_p.append(row_now)
    col_p.append(col_now)
    sums = total_over(total_over(part, "region", nreg), "industry", nind)
    cell, row_y, col_y = pl.pallas_call(
        functools.partial(finish_kernel, rows, sizes, inds, probs, iters),
        out_shape=[
            jax.ShapeDtypeStruct((probs, rows, sizes, inds), jnp.bfloat16),
            shape(rows, LANES),
            shape(inds, LANES),
        ],
        in_specs=[VMEM_SPEC] * 2 + [ANY_SPEC] + [VMEM_SPEC] * (2 + 6 * iters),
        out_specs=[ANY_SPEC, VMEM_SPEC, VMEM_SPEC],
        scratch_shapes=[pltpu.VMEM((rows, LANES), F32), pltpu.VMEM((inds, LANES), F32)],
        compiler_params=params(),
        name="finish",
    )(sums, scaling, barrier, drow, dcol, *row_p, *col_p)
    row_step = row_y.reshape(rows, probs, sizes).transpose(1, 0, 2)
    col_step = col_y.T.reshape(probs, sizes, inds)
    return cell, row_step, col_step


def solution(mesh):
    nreg, nind = mesh.shape["region"], mesh.shape["industry"]
    cells = P(None, "region", None, "industry")
    table = P("region", None, "industry")
    row, col = P(None, "region", None), P(None, None, "industry")
    return jax.shard_map(
        functools.partial(local, nreg, nind, 3),
        mesh=mesh,
        in_specs=(cells, cells, cells, table, table, P(), P(), row, col),
        out_specs=(cells, row, col),
        check_vma=False,
    )
```

time: 1470 us -> 275 us (0.19)
  waiting for transfers between devices: 998 us -> 96.6 us
  other arithmetic: 253 us -> 0.85 us
  blocking collectives: 199 us -> 0 us
  Pallas kernels: 0 us -> 104 us
  starting transfers between devices: 0.8 us -> 66.5 us
    psum x20 -> x0, waiting for transfers between devices: 993 us -> none  [the longest x10 521 us: col_margin(): return lax.psum(partial_value, 'region')]
    psum x5 -> x0, blocking collectives: 199 us -> none  [inner_pair(): lax.psum(local_pair(first_row, second_row, first_col, second_col), ('regi...]
    reduce_sum x21 -> x0, other arithmetic: 197 us -> none  [the longest x6 77.6 us: couple(): left = row_margin(jnp.sum(scaling * part_col[:, None, :, :], axis=3))]
    pallas_call x0 -> x21, Pallas kernels: none -> 104 us  [the longest x1 45.4 us: local(): pl.pallas_call(functools.partial(prepare_kernel, rows, sizes, inds, probs...]
    ppermute x0 -> x59, waiting for transfers between devices: none -> 96.6 us  [exchange(): lax.ppermute(x, axis, [(j, j ^ flip) for j in range(count)])]
    ppermute x0 -> x59, starting transfers between devices: none -> 66.5 us  [exchange(): lax.ppermute(x, axis, [(j, j ^ flip) for j in range(count)])]
    convert_element_type x2 -> x1, other arithmetic: 24.5 us -> 0.01 us  [local(): flags = jnp.any(near, axis=1).astype(jnp.int32)]
    div x17 -> x0, other arithmetic: 18.9 us -> none  [the longest x6 9.6 us: precondition(): base_row, base_col = (vec_row / diag_row, vec_col / diag_col)]
  transfers between devices with their start and end apart: 20 -> 59, of which waited for: 20 -> 24; matrix products, arithmetic and copies ran while one was open for 1% -> 0% of each run, Pallas kernels for 0% -> 0%
where the time goes in v2:
time: 275 us; the launch traced here: 274 us
  Pallas kernels  104 us (38%)
  waiting for transfers between devices  96.6 us (35%)
  starting transfers between devices  66.5 us (24%)
  local copies, waits for them, and re-layouts  4.81 us (2%)
    ppermute x59, waiting for transfers between devices, exchange(): lax.ppermute(x, axis, [(j, j ^ flip) for j in range(count)])  96.6 us
    ppermute x59, starting transfers between devices, exchange(): lax.ppermute(x, axis, [(j, j ^ flip) for j in range(count)])  66.5 us
    pallas_call x1, Pallas kernels, local(): pl.pallas_call(functools.partial(prepare_kernel, rows, sizes, inds, probs...  45.4 us
    pallas_call x19, Pallas kernels, call(): pl.pallas_call(kernel, out_shape=outs, in_specs=[VMEM_SPEC] * len(args),...  35.1 us
    pallas_call x1, Pallas kernels, local(): pl.pallas_call(functools.partial(finish_kernel, rows, sizes, inds, probs,...  23.9 us
  transfers between devices with their start and end apart: 59, of which 24 were waited for; matrix products, arithmetic and copies ran while one was open for 0% of the time, Pallas kernels for 0%

profile of v2, /device:TPU:0, one launch (start us, length us, event | category | flops | bytes accessed | tf_op | source)
XLA Modules:
  0.0 274.1 jit_solution(763900079623759383)
XLA Ops:
  4.8 45.4 %prepare.1 = (f32[192,256,128]{2,1,0:T(8,128)S(1)}, f32[8,192,16,256]{3,2,1,0:T(8,128)}, f32[2,192,128]{2,1,0:T(8,128)S(1)}, f32[2,256,128]{2,1,0:T(8,128)S(1)}) custom-call(s32[2]{0:T(128)S(1)} %pad_add_fusion.place_ref, s32[24]{0:T(128)S(1)} %convert_element_type.3.flag_ref, s32[8]{0:T(128)S(1)} %copy-done, s32[8]{0:T(128)S(1)} %copy-done.1, ...), custom_call_target="tpu_custom_call" | custom-call | tf_op jit(solution)/shard_map/prepare/pallas_call | solution.py:373
  53.3 5.5 %collective-permute-done.refs_1_ = f32[2,192,128]{2,1,0:T(8,128)S(1)} collective-permute-done((f32[2,192,128]{2,1,0:T(8,128)S(1)}, f32[2,192,128]{2,1,0:T(8,128)S(1)}, u32[]{:S(2)}, u32[]{:S(2)}) %collective-permute-start) | collective-permute-done | bytes 196640 | tf_op jit(solution)/shard_map/ppermute | solution.py:304
  65.2 8.2 %collective-permute-done.2.refs_1_ = f32[2,192,128]{2,1,0:T(8,128)S(1)} collective-permute-done((f32[2,192,128]{2,1,0:T(8,128)S(1)}, f32[2,192,128]{2,1,0:T(8,128)S(1)}, u32[]{:S(2)}, u32[]{:S(2)}) %collective-permute-start.2) | collective-permute-done | bytes 196640 | tf_op jit(solution)/shard_map/ppermute | solution.py:304
  73.6 4.0 %couple.8 = (f32[192,128]{1,0:T(8,128)S(1)}, f32[256,128]{1,0:T(8,128)S(1)}, f32[192,128]{1,0:T(8,128)S(1)}, f32[256,128]{1,0:T(8,128)S(1)}) custom-call(f32[192,256,128]{2,1,0:T(8,128)S(1)} %get-tuple-element.67.scaling_ref, f32[192,128]{1,0:T(8,128)S(1)} %get-tuple-element.72.row_diag.row_diag_ref, f32[256,128]{1,0:T(8,128)S(1)} %get-tuple-element.73.col_diag.col_diag_ref, ...), custom_call_target="tpu_custom_call" | custom-call | tf_op jit(solution)/shard_map/couple/pallas_call | solution.py:309
  79.4 3.6 %collective-permute-done.6.refs_1_ = f32[192,128]{1,0:T(8,128)S(1)} collective-permute-done((f32[192,128]{1,0:T(8,128)S(1)}, f32[192,128]{1,0:T(8,128)S(1)}, u32[]{:S(2)}, u32[]{:S(2)}) %collective-permute-start.6) | collective-permute-done | bytes 98336 | tf_op jit(solution)/shard_map/ppermute | solution.py:304
  89.1 2.9 %collective-permute-done.8.refs_1_ = f32[192,128]{1,0:T(8,128)S(1)} collective-permute-done((f32[192,128]{1,0:T(8,128)S(1)}, f32[192,128]{1,0:T(8,128)S(1)}, u32[]{:S(2)}, u32[]{:S(2)}) %collective-permute-start.8) | collective-permute-done | bytes 98336 | tf_op jit(solution)/shard_map/ppermute | solution.py:304
  92.1 4.0 %couple.9 = (f32[192,128]{1,0:T(8,128)S(1)}, f32[256,128]{1,0:T(8,128)S(1)}, f32[192,128]{1,0:T(8,128)S(1)}, f32[256,128]{1,0:T(8,128)S(1)}) custom-call(f32[192,256,128]{2,1,0:T(8,128)S(1)} %get-tuple-element.67.scaling_ref, f32[192,128]{1,0:T(8,128)S(1)} %get-tuple-element.72.row_diag.row_diag_ref, f32[256,128]{1,0:T(8,128)S(1)} %get-tuple-element.73.col_diag.col_diag_ref, ...), custom_call_target="tpu_custom_call" | custom-call | tf_op jit(solution)/shard_map/couple/pallas_call | solution.py:309
  98.0 3.4 %collective-permute-done.12.refs_1_ = f32[192,128]{1,0:T(8,128)S(1)} collective-permute-done((f32[192,128]{1,0:T(8,128)S(1)}, f32[192,128]{1,0:T(8,128)S(1)}, u32[]{:S(2)}, u32[]{:S(2)}) %collective-permute-start.12) | collective-permute-done | bytes 98336 | tf_op jit(solution)/shard_map/ppermute | solution.py:304
  101.5 3.3 %collective-permute-start.17 = (f32[256,128]{1,0:T(8,128)S(1)}, f32[256,128]{1,0:T(8,128)S(1)}, u32[]{:S(2)}, u32[]{:S(2)}) collective-permute-start(f32[256,128]{1,0:T(8,128)S(1)} %get-tuple-element.83.refs_2_), channel_id=1, source_target_pairs={{0,24},{4,28},{8,16},{12,20},{16,8},{20,12},{24,0},{28,4},{1,25},{... | collective-permute-start | bytes 393224 | tf_op jit(solution)/shard_map/ppermute | solution.py:304
  105.5 2.9 %collective-permute-start.14 = (f32[192,128]{1,0:T(8,128)S(1)}, f32[192,128]{1,0:T(8,128)S(1)}, u32[]{:S(2)}, u32[]{:S(2)}) collective-permute-start(f32[192,128]{1,0:T(8,128)S(1)} %get-tuple-element.82.refs_0_), channel_id=1, source_target_pairs={{0,2},{1,3},{2,0},{3,1},{4,6},{5,7},{6,4},{7,5},{8,10},{9,11},{10,... | collective-permute-start | bytes 294920 | tf_op jit(solution)/shard_map/ppermute | solution.py:304
  108.4 4.1 %collective-permute-done.14.refs_1_ = f32[192,128]{1,0:T(8,128)S(1)} collective-permute-done((f32[192,128]{1,0:T(8,128)S(1)}, f32[192,128]{1,0:T(8,128)S(1)}, u32[]{:S(2)}, u32[]{:S(2)}) %collective-permute-start.14) | collective-permute-done | bytes 98336 | tf_op jit(solution)/shard_map/ppermute | solution.py:304
  112.4 4.0 %couple.10 = (f32[192,128]{1,0:T(8,128)S(1)}, f32[256,128]{1,0:T(8,128)S(1)}, f32[192,128]{1,0:T(8,128)S(1)}, f32[256,128]{1,0:T(8,128)S(1)}) custom-call(f32[192,256,128]{2,1,0:T(8,128)S(1)} %get-tuple-element.67.scaling_ref, f32[192,128]{1,0:T(8,128)S(1)} %get-tuple-element.72.row_diag.row_diag_ref, ...), custom_call_target="tpu_custom_call" | custom-call | tf_op jit(solution)/shard_map/couple/pallas_call | solution.py:309
  117.4 4.4 %collective-permute-done.18.refs_1_ = f32[192,128]{1,0:T(8,128)S(1)} collective-permute-done((f32[192,128]{1,0:T(8,128)S(1)}, f32[192,128]{1,0:T(8,128)S(1)}, u32[]{:S(2)}, u32[]{:S(2)}) %collective-permute-start.18) | collective-permute-done | bytes 98336 | tf_op jit(solution)/shard_map/ppermute | solution.py:304
  127.7 4.2 %collective-permute-done.20.refs_1_ = f32[192,128]{1,0:T(8,128)S(1)} collective-permute-done((f32[192,128]{1,0:T(8,128)S(1)}, f32[192,128]{1,0:T(8,128)S(1)}, u32[]{:S(2)}, u32[]{:S(2)}) %collective-permute-start.20) | collective-permute-done | bytes 98336 | tf_op jit(solution)/shard_map/ppermute | solution.py:304
  132.0 4.0 %couple.11 = (f32[192,128]{1,0:T(8,128)S(1)}, f32[256,128]{1,0:T(8,128)S(1)}, f32[192,128]{1,0:T(8,128)S(1)}, f32[256,128]{1,0:T(8,128)S(1)}) custom-call(f32[192,256,128]{2,1,0:T(8,128)S(1)} %get-tuple-element.67.scaling_ref, f32[192,128]{1,0:T(8,128)S(1)} %get-tuple-element.72.row_diag.row_diag_ref, ...), custom_call_target="tpu_custom_call" | custom-call | tf_op jit(solution)/shard_map/couple/pallas_call | solution.py:309
  136.7 4.6 %collective-permute-done.24.refs_1_ = f32[192,128]{1,0:T(8,128)S(1)} collective-permute-done((f32[192,128]{1,0:T(8,128)S(1)}, f32[192,128]{1,0:T(8,128)S(1)}, u32[]{:S(2)}, u32[]{:S(2)}) %collective-permute-start.24) | collective-permute-done | bytes 98336 | tf_op jit(solution)/shard_map/ppermute | solution.py:304
  147.1 4.4 %collective-permute-done.26.refs_1_ = f32[192,128]{1,0:T(8,128)S(1)} collective-permute-done((f32[192,128]{1,0:T(8,128)S(1)}, f32[192,128]{1,0:T(8,128)S(1)}, u32[]{:S(2)}, u32[]{:S(2)}) %collective-permute-start.26) | collective-permute-done | bytes 98336 | tf_op jit(solution)/shard_map/ppermute | solution.py:304
  151.5 4.0 %couple.12 = (f32[192,128]{1,0:T(8,128)S(1)}, f32[256,128]{1,0:T(8,128)S(1)}, f32[192,128]{1,0:T(8,128)S(1)}, f32[256,128]{1,0:T(8,128)S(1)}) custom-call(f32[192,256,128]{2,1,0:T(8,128)S(1)} %get-tuple-element.67.scaling_ref, f32[192,128]{1,0:T(8,128)S(1)} %get-tuple-element.72.row_diag.row_diag_ref, ...), custom_call_target="tpu_custom_call" | custom-call | tf_op jit(solution)/shard_map/couple/pallas_call | solution.py:309
  156.1 4.7 %collective-permute-done.30.refs_1_ = f32[192,128]{1,0:T(8,128)S(1)} collective-permute-done((f32[192,128]{1,0:T(8,128)S(1)}, f32[192,128]{1,0:T(8,128)S(1)}, u32[]{:S(2)}, u32[]{:S(2)}) %collective-permute-start.30) | collective-permute-done | bytes 98336 | tf_op jit(solution)/shard_map/ppermute | solution.py:304
  166.5 4.5 %collective-permute-done.32.refs_1_ = f32[192,128]{1,0:T(8,128)S(1)} collective-permute-done((f32[192,128]{1,0:T(8,128)S(1)}, f32[192,128]{1,0:T(8,128)S(1)}, u32[]{:S(2)}, u32[]{:S(2)}) %collective-permute-start.32) | collective-permute-done | bytes 98336 | tf_op jit(solution)/shard_map/ppermute | solution.py:304
  171.0 4.0 %couple.13 = (f32[192,128]{1,0:T(8,128)S(1)}, f32[256,128]{1,0:T(8,128)S(1)}, f32[192,128]{1,0:T(8,128)S(1)}, f32[256,128]{1,0:T(8,128)S(1)}) custom-call(f32[192,256,128]{2,1,0:T(8,128)S(1)} %get-tuple-element.67.scaling_ref, f32[192,128]{1,0:T(8,128)S(1)} %get-tuple-element.72.row_diag.row_diag_ref, ...), custom_call_target="tpu_custom_call" | custom-call | tf_op jit(solution)/shard_map/couple/pallas_call | solution.py:309
  175.5 4.9 %collective-permute-done.36.refs_1_ = f32[192,128]{1,0:T(8,128)S(1)} collective-permute-done((f32[192,128]{1,0:T(8,128)S(1)}, f32[192,128]{1,0:T(8,128)S(1)}, u32[]{:S(2)}, u32[]{:S(2)}) %collective-permute-start.36) | collective-permute-done | bytes 98336 | tf_op jit(solution)/shard_map/ppermute | solution.py:304
  185.8 4.7 %collective-permute-done.38.refs_1_ = f32[192,128]{1,0:T(8,128)S(1)} collective-permute-done((f32[192,128]{1,0:T(8,128)S(1)}, f32[192,128]{1,0:T(8,128)S(1)}, u32[]{:S(2)}, u32[]{:S(2)}) %collective-permute-start.38) | collective-permute-done | bytes 98336 | tf_op jit(solution)/shard_map/ppermute | solution.py:304
  190.5 4.0 %couple.14 = (f32[192,128]{1,0:T(8,128)S(1)}, f32[256,128]{1,0:T(8,128)S(1)}, f32[192,128]{1,0:T(8,128)S(1)}, f32[256,128]{1,0:T(8,128)S(1)}) custom-call(f32[192,256,128]{2,1,0:T(8,128)S(1)} %get-tuple-element.67.scaling_ref, f32[192,128]{1,0:T(8,128)S(1)} %get-tuple-element.72.row_diag.row_diag_ref, ...), custom_call_target="tpu_custom_call" | custom-call | tf_op jit(solution)/shard_map/couple/pallas_call | solution.py:309
  194.8 5.0 %collective-permute-done.42.refs_1_ = f32[192,128]{1,0:T(8,128)S(1)} collective-permute-done((f32[192,128]{1,0:T(8,128)S(1)}, f32[192,128]{1,0:T(8,128)S(1)}, u32[]{:S(2)}, u32[]{:S(2)}) %collective-permute-start.42) | collective-permute-done | bytes 98336 | tf_op jit(solution)/shard_map/ppermute | solution.py:304
  205.2 4.8 %collective-permute-done.44.refs_1_ = f32[192,128]{1,0:T(8,128)S(1)} collective-permute-done((f32[192,128]{1,0:T(8,128)S(1)}, f32[192,128]{1,0:T(8,128)S(1)}, u32[]{:S(2)}, u32[]{:S(2)}) %collective-permute-start.44) | collective-permute-done | bytes 98336 | tf_op jit(solution)/shard_map/ppermute | solution.py:304
  210.0 4.0 %couple.15 = (f32[192,128]{1,0:T(8,128)S(1)}, f32[256,128]{1,0:T(8,128)S(1)}, f32[192,128]{1,0:T(8,128)S(1)}, f32[256,128]{1,0:T(8,128)S(1)}) custom-call(f32[192,256,128]{2,1,0:T(8,128)S(1)} %get-tuple-element.67.scaling_ref, f32[192,128]{1,0:T(8,128)S(1)} %get-tuple-element.72.row_diag.row_diag_ref, ...), custom_call_target="tpu_custom_call" | custom-call | tf_op jit(solution)/shard_map/couple/pallas_call | solution.py:309
  214.2 5.1 %collective-permute-done.48.refs_1_ = f32[192,128]{1,0:T(8,128)S(1)} collective-permute-done((f32[192,128]{1,0:T(8,128)S(1)}, f32[192,128]{1,0:T(8,128)S(1)}, u32[]{:S(2)}, u32[]{:S(2)}) %collective-permute-start.48) | collective-permute-done | bytes 98336 | tf_op jit(solution)/shard_map/ppermute | solution.py:304
  224.6 4.9 %collective-permute-done.50.rest_1_ = f32[192,128]{1,0:T(8,128)S(1)} collective-permute-done((f32[192,128]{1,0:T(8,128)S(1)}, f32[192,128]{1,0:T(8,128)S(1)}, u32[]{:S(2)}, u32[]{:S(2)}) %collective-permute-start.50) | collective-permute-done | bytes 98336 | tf_op jit(solution)/shard_map/ppermute | solution.py:304
  240.5 3.6 %collective-permute-done.57 = f32[16,128]{1,0:T(8,128)S(1)} collective-permute-done((f32[16,128]{1,0:T(8,128)S(1)}, f32[16,128]{1,0:T(8,128)S(1)}, u32[]{:S(2)}, u32[]{:S(2)}) %collective-permute-start.57) | collective-permute-done | bytes 8224 | tf_op jit(solution)/shard_map/ppermute | solution.py:304
  245.4 3.3 %collective-permute-done.58 = f32[16,128]{1,0:T(8,128)S(1)} collective-permute-done((f32[16,128]{1,0:T(8,128)S(1)}, f32[16,128]{1,0:T(8,128)S(1)}, u32[]{:S(2)}, u32[]{:S(2)}) %collective-permute-start.58) | collective-permute-done | bytes 8224 | tf_op jit(solution)/shard_map/ppermute | solution.py:304
  248.7 23.9 %finish.1 = (bf16[8,192,16,256]{3,2,1,0:T(8,128)(2,1)}, f32[192,128]{1,0:T(8,128)S(1)}, f32[256,128]{1,0:T(8,128)S(1)}) custom-call(f32[16,128]{1,0:T(8,128)S(1)} %add.43.sums_ref, f32[192,256,128]{2,1,0:T(8,128)S(1)} %get-tuple-element.67.scaling_ref, f32[8,192,16,256]{3,2,1,0:T(8,128)} %get-tuple-element.125.barrier_hbm, f32[192,128]{1,0:T(8,128)S(1)} %copy.22.drow_ref, ...), custom_call_target="tpu_custom_call" | custom-call | tf_op jit(solution)/shard_map/finish/pallas_call | solution.py:420
  (124 shorter events, 74.5 us)
Async XLA Ops:
  50.2 8.6 %collective-permute-start.1 = (f32[2,256,128]{2,1,0:T(8,128)S(1)}, f32[2,256,128]{2,1,0:T(8,128)S(1)}, u32[]{:S(2)}, u32[]{:S(2)}) collective-permute-start(f32[2,256,128]{2,1,0:T(8,128)S(1)} %get-tuple-element.69.refs_2_), channel_id=1, source_target_pairs={{0,4},{4,0},{8,12},{12,8},{16,20},{20,16},{24,28},{28,24},{1,5},{5... | collective-permute-start | bytes 786440 | tf_op jit(solution)/shard_map/ppermute | solution.py:304
  50.7 8.2 %collective-permute-start = (f32[2,192,128]{2,1,0:T(8,128)S(1)}, f32[2,192,128]{2,1,0:T(8,128)S(1)}, u32[]{:S(2)}, u32[]{:S(2)}) collective-permute-start(f32[2,192,128]{2,1,0:T(8,128)S(1)} %get-tuple-element.68.refs_0_), channel_id=1, source_target_pairs={{0,1},{1,0},{2,3},{3,2},{4,5},{5,4},{6,7},{7,6},{8,9},{9,8},{10,11... | collective-permute-start | bytes 589832 | tf_op jit(solution)/shard_map/ppermute | solution.py:304
  58.9 14.5 %collective-permute-start.5 = (f32[2,256,128]{2,1,0:T(8,128)S(1)}, f32[2,256,128]{2,1,0:T(8,128)S(1)}, u32[]{:S(2)}, u32[]{:S(2)}) collective-permute-start(f32[2,256,128]{2,1,0:T(8,128)S(1)} %get-tuple-element.71.refs_2_), channel_id=1, source_target_pairs={{0,24},{4,28},{8,16},{12,20},{16,8},{20,12},{24,0},{28,4},{1,25},{... | collective-permute-start | bytes 786440 | tf_op jit(solution)/shard_map/ppermute | solution.py:304
  61.6 12.0 %collective-permute-start.4 = (f32[2,256,128]{2,1,0:T(8,128)S(1)}, f32[2,256,128]{2,1,0:T(8,128)S(1)}, u32[]{:S(2)}, u32[]{:S(2)}) collective-permute-start(f32[2,256,128]{2,1,0:T(8,128)S(1)} %get-tuple-element.71.refs_2_), channel_id=1, source_target_pairs={{0,16},{4,20},{8,24},{12,28},{16,0},{20,4},{24,8},{28,12},{1,17},{... | collective-permute-start | bytes 786440 | tf_op jit(solution)/shard_map/ppermute | solution.py:304
  62.0 11.6 %collective-permute-start.3 = (f32[2,256,128]{2,1,0:T(8,128)S(1)}, f32[2,256,128]{2,1,0:T(8,128)S(1)}, u32[]{:S(2)}, u32[]{:S(2)}) collective-permute-start(f32[2,256,128]{2,1,0:T(8,128)S(1)} %get-tuple-element.71.refs_2_), channel_id=1, source_target_pairs={{0,8},{4,12},{8,0},{12,4},{16,24},{20,28},{24,16},{28,20},{1,9},{5... | collective-permute-start | bytes 786440 | tf_op jit(solution)/shard_map/ppermute | solution.py:304
  62.4 10.9 %collective-permute-start.2 = (f32[2,192,128]{2,1,0:T(8,128)S(1)}, f32[2,192,128]{2,1,0:T(8,128)S(1)}, u32[]{:S(2)}, u32[]{:S(2)}) collective-permute-start(f32[2,192,128]{2,1,0:T(8,128)S(1)} %get-tuple-element.70.refs_0_), channel_id=1, source_target_pairs={{0,2},{1,3},{2,0},{3,1},{4,6},{5,7},{6,4},{7,5},{8,10},{9,11},{10,... | collective-permute-start | bytes 589832 | tf_op jit(solution)/shard_map/ppermute | solution.py:304
  83.0 9.1 %collective-permute-start.11 = (f32[256,128]{1,0:T(8,128)S(1)}, f32[256,128]{1,0:T(8,128)S(1)}, u32[]{:S(2)}, u32[]{:S(2)}) collective-permute-start(f32[256,128]{1,0:T(8,128)S(1)} %get-tuple-element.79.refs_2_), channel_id=1, source_target_pairs={{0,24},{4,28},{8,16},{12,20},{16,8},{20,12},{24,0},{28,4},{1,25},{... | collective-permute-start | bytes 393224 | tf_op jit(solution)/shard_map/ppermute | solution.py:304
  85.3 6.8 %collective-permute-start.10 = (f32[256,128]{1,0:T(8,128)S(1)}, f32[256,128]{1,0:T(8,128)S(1)}, u32[]{:S(2)}, u32[]{:S(2)}) collective-permute-start(f32[256,128]{1,0:T(8,128)S(1)} %get-tuple-element.79.refs_2_), channel_id=1, source_target_pairs={{0,16},{4,20},{8,24},{12,28},{16,0},{20,4},{24,8},{28,12},{1,17},{... | collective-permute-start | bytes 393224 | tf_op jit(solution)/shard_map/ppermute | solution.py:304
  101.5 11.0 %collective-permute-start.17 = (f32[256,128]{1,0:T(8,128)S(1)}, f32[256,128]{1,0:T(8,128)S(1)}, u32[]{:S(2)}, u32[]{:S(2)}) collective-permute-start(f32[256,128]{1,0:T(8,128)S(1)} %get-tuple-element.83.refs_2_), channel_id=1, source_target_pairs={{0,24},{4,28},{8,16},{12,20},{16,8},{20,12},{24,0},{28,4},{1,25},{... | collective-permute-start | bytes 393224 | tf_op jit(solution)/shard_map/ppermute | solution.py:304
  104.8 7.6 %collective-permute-start.16 = (f32[256,128]{1,0:T(8,128)S(1)}, f32[256,128]{1,0:T(8,128)S(1)}, u32[]{:S(2)}, u32[]{:S(2)}) collective-permute-start(f32[256,128]{1,0:T(8,128)S(1)} %get-tuple-element.83.refs_2_), channel_id=1, source_target_pairs={{0,16},{4,20},{8,24},{12,28},{16,0},{20,4},{24,8},{28,12},{1,17},{... | collective-permute-start | bytes 393224 | tf_op jit(solution)/shard_map/ppermute | solution.py:304
  104.8 7.6 %collective-permute-start.15 = (f32[256,128]{1,0:T(8,128)S(1)}, f32[256,128]{1,0:T(8,128)S(1)}, u32[]{:S(2)}, u32[]{:S(2)}) collective-permute-start(f32[256,128]{1,0:T(8,128)S(1)} %get-tuple-element.83.refs_2_), channel_id=1, source_target_pairs={{0,8},{4,12},{8,0},{12,4},{16,24},{20,28},{24,16},{28,20},{1,9},{5... | collective-permute-start | bytes 393224 | tf_op jit(solution)/shard_map/ppermute | solution.py:304
  105.5 7.0 %collective-permute-start.14 = (f32[192,128]{1,0:T(8,128)S(1)}, f32[192,128]{1,0:T(8,128)S(1)}, u32[]{:S(2)}, u32[]{:S(2)}) collective-permute-start(f32[192,128]{1,0:T(8,128)S(1)} %get-tuple-element.82.refs_0_), channel_id=1, source_target_pairs={{0,2},{1,3},{2,0},{3,1},{4,6},{5,7},{6,4},{7,5},{8,10},{9,11},{10,... | collective-permute-start | bytes 294920 | tf_op jit(solution)/shard_map/ppermute | solution.py:304
  121.8 10.1 %collective-permute-start.23 = (f32[256,128]{1,0:T(8,128)S(1)}, f32[256,128]{1,0:T(8,128)S(1)}, u32[]{:S(2)}, u32[]{:S(2)}) collective-permute-start(f32[256,128]{1,0:T(8,128)S(1)} %get-tuple-element.87.refs_2_), channel_id=1, source_target_pairs={{0,24},{4,28},{8,16},{12,20},{16,8},{20,12},{24,0},{28,4},{1,25},{... | collective-permute-start | bytes 393224 | tf_op jit(solution)/shard_map/ppermute | solution.py:304
  124.3 7.6 %collective-permute-start.22 = (f32[256,128]{1,0:T(8,128)S(1)}, f32[256,128]{1,0:T(8,128)S(1)}, u32[]{:S(2)}, u32[]{:S(2)}) collective-permute-start(f32[256,128]{1,0:T(8,128)S(1)} %get-tuple-element.87.refs_2_), channel_id=1, source_target_pairs={{0,16},{4,20},{8,24},{12,28},{16,0},{20,4},{24,8},{28,12},{1,17},{... | collective-permute-start | bytes 393224 | tf_op jit(solution)/shard_map/ppermute | solution.py:304
  124.9 7.1 %collective-permute-start.21 = (f32[256,128]{1,0:T(8,128)S(1)}, f32[256,128]{1,0:T(8,128)S(1)}, u32[]{:S(2)}, u32[]{:S(2)}) collective-permute-start(f32[256,128]{1,0:T(8,128)S(1)} %get-tuple-element.87.refs_2_), channel_id=1, source_target_pairs={{0,8},{4,12},{8,0},{12,4},{16,24},{20,28},{24,16},{28,20},{1,9},{5... | collective-permute-start | bytes 393224 | tf_op jit(solution)/shard_map/ppermute | solution.py:304
  141.3 10.1 %collective-permute-start.29 = (f32[256,128]{1,0:T(8,128)S(1)}, f32[256,128]{1,0:T(8,128)S(1)}, u32[]{:S(2)}, u32[]{:S(2)}) collective-permute-start(f32[256,128]{1,0:T(8,128)S(1)} %get-tuple-element.91.refs_2_), channel_id=1, source_target_pairs={{0,24},{4,28},{8,16},{12,20},{16,8},{20,12},{24,0},{28,4},{1,25},{... | collective-permute-start | bytes 393224 | tf_op jit(solution)/shard_map/ppermute | solution.py:304
  143.8 7.6 %collective-permute-start.28 = (f32[256,128]{1,0:T(8,128)S(1)}, f32[256,128]{1,0:T(8,128)S(1)}, u32[]{:S(2)}, u32[]{:S(2)}) collective-permute-start(f32[256,128]{1,0:T(8,128)S(1)} %get-tuple-element.91.refs_2_), channel_id=1, source_target_pairs={{0,16},{4,20},{8,24},{12,28},{16,0},{20,4},{24,8},{28,12},{1,17},{... | collective-permute-start | bytes 393224 | tf_op jit(solution)/shard_map/ppermute | solution.py:304
  144.4 7.1 %collective-permute-start.27 = (f32[256,128]{1,0:T(8,128)S(1)}, f32[256,128]{1,0:T(8,128)S(1)}, u32[]{:S(2)}, u32[]{:S(2)}) collective-permute-start(f32[256,128]{1,0:T(8,128)S(1)} %get-tuple-element.91.refs_2_), channel_id=1, source_target_pairs={{0,8},{4,12},{8,0},{12,4},{16,24},{20,28},{24,16},{28,20},{1,9},{5... | collective-permute-start | bytes 393224 | tf_op jit(solution)/shard_map/ppermute | solution.py:304
  160.9 10.1 %collective-permute-start.35 = (f32[256,128]{1,0:T(8,128)S(1)}, f32[256,128]{1,0:T(8,128)S(1)}, u32[]{:S(2)}, u32[]{:S(2)}) collective-permute-start(f32[256,128]{1,0:T(8,128)S(1)} %get-tuple-element.95.refs_2_), channel_id=1, source_target_pairs={{0,24},{4,28},{8,16},{12,20},{16,8},{20,12},{24,0},{28,4},{1,25},{... | collective-permute-start | bytes 393224 | tf_op jit(solution)/shard_map/ppermute | solution.py:304
  163.4 7.6 %collective-permute-start.34 = (f32[256,128]{1,0:T(8,128)S(1)}, f32[256,128]{1,0:T(8,128)S(1)}, u32[]{:S(2)}, u32[]{:S(2)}) collective-permute-start(f32[256,128]{1,0:T(8,128)S(1)} %get-tuple-element.95.refs_2_), channel_id=1, source_target_pairs={{0,16},{4,20},{8,24},{12,28},{16,0},{20,4},{24,8},{28,12},{1,17},{... | collective-permute-start | bytes 393224 | tf_op jit(solution)/shard_map/ppermute | solution.py:304
  163.9 7.1 %collective-permute-start.33 = (f32[256,128]{1,0:T(8,128)S(1)}, f32[256,128]{1,0:T(8,128)S(1)}, u32[]{:S(2)}, u32[]{:S(2)}) collective-permute-start(f32[256,128]{1,0:T(8,128)S(1)} %get-tuple-element.95.refs_2_), channel_id=1, source_target_pairs={{0,8},{4,12},{8,0},{12,4},{16,24},{20,28},{24,16},{28,20},{1,9},{5... | collective-permute-start | bytes 393224 | tf_op jit(solution)/shard_map/ppermute | solution.py:304
  164.4 6.6 %collective-permute-start.32 = (f32[192,128]{1,0:T(8,128)S(1)}, f32[192,128]{1,0:T(8,128)S(1)}, u32[]{:S(2)}, u32[]{:S(2)}) collective-permute-start(f32[192,128]{1,0:T(8,128)S(1)} %get-tuple-element.94.refs_0_), channel_id=1, source_target_pairs={{0,2},{1,3},{2,0},{3,1},{4,6},{5,7},{6,4},{7,5},{8,10},{9,11},{10,... | collective-permute-start | bytes 294920 | tf_op jit(solution)/shard_map/ppermute | solution.py:304
  180.4 10.1 %collective-permute-start.41 = (f32[256,128]{1,0:T(8,128)S(1)}, f32[256,128]{1,0:T(8,128)S(1)}, u32[]{:S(2)}, u32[]{:S(2)}) collective-permute-start(f32[256,128]{1,0:T(8,128)S(1)} %get-tuple-element.99.refs_2_), channel_id=1, source_target_pairs={{0,24},{4,28},{8,16},{12,20},{16,8},{20,12},{24,0},{28,4},{1,25},{... | collective-permute-start | bytes 393224 | tf_op jit(solution)/shard_map/ppermute | solution.py:304
  182.9 7.6 %collective-permute-start.40 = (f32[256,128]{1,0:T(8,128)S(1)}, f32[256,128]{1,0:T(8,128)S(1)}, u32[]{:S(2)}, u32[]{:S(2)}) collective-permute-start(f32[256,128]{1,0:T(8,128)S(1)} %get-tuple-element.99.refs_2_), channel_id=1, source_target_pairs={{0,16},{4,20},{8,24},{12,28},{16,0},{20,4},{24,8},{28,12},{1,17},{... | collective-permute-start | bytes 393224 | tf_op jit(solution)/shard_map/ppermute | solution.py:304
  183.4 7.1 %collective-permute-start.39 = (f32[256,128]{1,0:T(8,128)S(1)}, f32[256,128]{1,0:T(8,128)S(1)}, u32[]{:S(2)}, u32[]{:S(2)}) collective-permute-start(f32[256,128]{1,0:T(8,128)S(1)} %get-tuple-element.99.refs_2_), channel_id=1, source_target_pairs={{0,8},{4,12},{8,0},{12,4},{16,24},{20,28},{24,16},{28,20},{1,9},{5... | collective-permute-start | bytes 393224 | tf_op jit(solution)/shard_map/ppermute | solution.py:304
  183.9 6.6 %collective-permute-start.38 = (f32[192,128]{1,0:T(8,128)S(1)}, f32[192,128]{1,0:T(8,128)S(1)}, u32[]{:S(2)}, u32[]{:S(2)}) collective-permute-start(f32[192,128]{1,0:T(8,128)S(1)} %get-tuple-element.98.refs_0_), channel_id=1, source_target_pairs={{0,2},{1,3},{2,0},{3,1},{4,6},{5,7},{6,4},{7,5},{8,10},{9,11},{10,... | collective-permute-start | bytes 294920 | tf_op jit(solution)/shard_map/ppermute | solution.py:304
  199.9 10.1 %collective-permute-start.47 = (f32[256,128]{1,0:T(8,128)S(1)}, f32[256,128]{1,0:T(8,128)S(1)}, u32[]{:S(2)}, u32[]{:S(2)}) collective-permute-start(f32[256,128]{1,0:T(8,128)S(1)} %get-tuple-element.103.refs_2_), channel_id=1, source_target_pairs={{0,24},{4,28},{8,16},{12,20},{16,8},{20,12},{24,0},{28,4},{1,25},{... | collective-permute-start | bytes 393224 | tf_op jit(solution)/shard_map/ppermute | solution.py:304
  202.3 7.7 %collective-permute-start.46 = (f32[256,128]{1,0:T(8,128)S(1)}, f32[256,128]{1,0:T(8,128)S(1)}, u32[]{:S(2)}, u32[]{:S(2)}) collective-permute-start(f32[256,128]{1,0:T(8,128)S(1)} %get-tuple-element.103.refs_2_), channel_id=1, source_target_pairs={{0,16},{4,20},{8,24},{12,28},{16,0},{20,4},{24,8},{28,12},{1,17},{... | collective-permute-start | bytes 393224 | tf_op jit(solution)/shard_map/ppermute | solution.py:304
  202.9 7.1 %collective-permute-start.45 = (f32[256,128]{1,0:T(8,128)S(1)}, f32[256,128]{1,0:T(8,128)S(1)}, u32[]{:S(2)}, u32[]{:S(2)}) collective-permute-start(f32[256,128]{1,0:T(8,128)S(1)} %get-tuple-element.103.refs_2_), channel_id=1, source_target_pairs={{0,8},{4,12},{8,0},{12,4},{16,24},{20,28},{24,16},{28,20},{1,9},{5... | collective-permute-start | bytes 393224 | tf_op jit(solution)/shard_map/ppermute | solution.py:304
  219.4 10.1 %collective-permute-start.53 = (f32[256,128]{1,0:T(8,128)S(1)}, f32[256,128]{1,0:T(8,128)S(1)}, u32[]{:S(2)}, u32[]{:S(2)}) collective-permute-start(f32[256,128]{1,0:T(8,128)S(1)} %get-tuple-element.107.rest_2_), channel_id=1, source_target_pairs={{0,24},{4,28},{8,16},{12,20},{16,8},{20,12},{24,0},{28,4},{1,25},{... | collective-permute-start | bytes 393224 | tf_op jit(solution)/shard_map/ppermute | solution.py:304
  221.8 7.7 %collective-permute-start.52 = (f32[256,128]{1,0:T(8,128)S(1)}, f32[256,128]{1,0:T(8,128)S(1)}, u32[]{:S(2)}, u32[]{:S(2)}) collective-permute-start(f32[256,128]{1,0:T(8,128)S(1)} %get-tuple-element.107.rest_2_), channel_id=1, source_target_pairs={{0,16},{4,20},{8,24},{12,28},{16,0},{20,4},{24,8},{28,12},{1,17},{... | collective-permute-start | bytes 393224 | tf_op jit(solution)/shard_map/ppermute | solution.py:304
  222.4 7.0 %collective-permute-start.51 = (f32[256,128]{1,0:T(8,128)S(1)}, f32[256,128]{1,0:T(8,128)S(1)}, u32[]{:S(2)}, u32[]{:S(2)}) collective-permute-start(f32[256,128]{1,0:T(8,128)S(1)} %get-tuple-element.107.rest_2_), channel_id=1, source_target_pairs={{0,8},{4,12},{8,0},{12,4},{16,24},{20,28},{24,16},{28,20},{1,9},{5... | collective-permute-start | bytes 393224 | tf_op jit(solution)/shard_map/ppermute | solution.py:304
  (29 other events, 139.9 us)

commit v3 on v2

v3 whole, which is shorter than its diff:
```python
import functools

import jax
import jax.numpy as jnp
from jax import lax
from jax.experimental import pallas as pl
from jax.experimental.pallas import tpu as pltpu
from jax.sharding import PartitionSpec as P

WEIGHT_ATTACK = 8.0
SHIFT_DIAG = 1.0
BLOCK = 8
LANES = 128
VMEM_MIB = 12
RATIO_IN_VMEM = False
VMEM_SPEC = pl.BlockSpec(memory_space=pltpu.VMEM)
SMEM_SPEC = pl.BlockSpec(memory_space=pltpu.SMEM)
ANY_SPEC = pl.BlockSpec(memory_space=pl.ANY)
F32 = jnp.float32


def shape(*dims):
    return jax.ShapeDtypeStruct(dims, F32)


def params():
    return pltpu.CompilerParams(vmem_limit_bytes=VMEM_MIB * 1024 * 1024)


def inverse(x):
    rough = pl.reciprocal(x, approx=True)
    return rough * (2.0 - x * rough)


def widen(rows):
    return jnp.broadcast_to(rows[:, None, :], (BLOCK, 8, LANES))


def attacked_tile(info_ref, k, row, sizes, inds, nind):
    probs = (info_ref.shape[0] - 2) // 2
    first = info_ref[1] * inds
    column = lax.broadcasted_iota(jnp.int32, (sizes, inds), 0) * (inds * nind)
    column = column + lax.broadcasted_iota(jnp.int32, (sizes, inds), 1) + first
    return column == jnp.where(info_ref[2 + k] == row, info_ref[2 + probs + k], -1)


def any_attack(info_ref, first_row):
    probs = (info_ref.shape[0] - 2) // 2
    hits = jnp.int32(0)
    for k in range(probs):
        offset = info_ref[2 + k] - first_row
        hits = hits + jnp.where((offset >= 0) & (offset < BLOCK), 1, 0)
    return hits


def split_halves(full, keep_ref, send_ref, core):
    half = full.shape[-2] // 2
    for ref, which in ((keep_ref, core), (send_ref, 1 - core)):
        ref[...] = full[..., pl.ds(pl.multiple_of(which * half, 8), half), :]


def prepare_kernel(
    rows, sizes, inds, probs, nind,
    info_ref, pos_hbm, low_hbm, high_hbm, upper_hbm, supp_hbm, drow_ref, dcol_ref,
    scaling_ref, ratio_ref, row_ref, keep_ref, send_ref,
    tile_s, tile_m, up_s, act_s, col_m, col_e, drow_t, dcol_t, col_ref,
):
    blocks = rows // BLOCK
    half = inds // LANES
    first_row = info_ref[0] * rows
    col_m[...] = jnp.zeros_like(col_m)
    col_e[...] = jnp.zeros_like(col_e)
    col_ref[...] = jnp.zeros_like(col_ref)
    drow_t[...] = drow_ref[...].T
    dcol_t[...] = dcol_ref[...].T

    def turn(slot, before, r):
        scaling_ref[before * BLOCK + r] = tile_s[slot, r].T

    def sums(slot, before):
        r0 = pl.multiple_of(before * BLOCK, BLOCK)
        here = pl.ds(r0, BLOCK)
        drow = drow_t[here, :]
        row_wide = widen(drow)
        sum_acc = jnp.zeros((BLOCK, 8, LANES), F32)
        dual_acc = jnp.zeros((BLOCK, 8, LANES), F32)
        for i0 in range(0, inds, 8):
            tile = scaling_ref[here, i0 : i0 + 8, :]
            sum_acc = sum_acc + tile
            dual_acc = dual_acc + tile * dcol_t[i0 : i0 + 8, :][None]
            col_ref[1, i0 : i0 + 8, :] += jnp.sum(tile, axis=0)
            col_e[i0 : i0 + 8, :] += jnp.sum(tile * row_wide, axis=0)
        total = jnp.sum(sum_acc, axis=1)
        margin = lax.dot_general(
            jnp.ones((8, LANES), F32),
            tile_m[slot].reshape(BLOCK * LANES, LANES),
            (((1,), (1,)), ((), ())),
            precision=lax.Precision.HIGHEST,
            preferred_element_type=F32,
        )
        margin = jnp.concatenate([margin[:1, r * LANES : (r + 1) * LANES] for r in range(BLOCK)], axis=0)
        row_ref[1, here, :] = total
        row_ref[0, here, :] = margin - drow * total - jnp.sum(dual_acc, axis=1)

    def body(pos_ref, low_ref, high_ref, upper_ref, supp_ref, *ratio_out):
        block = pl.program_id(0)
        slot = lax.rem(block, 2)
        other = 1 - slot
        before = jnp.maximum(block - 1, 0)
        r0 = block * BLOCK
        up_s[...] = upper_ref[...].astype(F32)
        act_s[...] = supp_ref[...].astype(F32)

        def problem(k, _, attacked):
            turn(other, before, k)
            total = jnp.zeros((sizes, inds), F32)
            place = pl.ds(pl.multiple_of(k * sizes, sizes), sizes)
            for r in range(BLOCK):
                upper = up_s[r]
                active = act_s[r]
                if attacked:
                    hit = attacked_tile(info_ref, k, first_row + r0 + r, sizes, inds, nind)
                    active = jnp.where(hit, jnp.ones_like(active), active)
                value = pos_ref[k, r].astype(F32) * upper
                slack = upper - value
                den = low_ref[k, r].astype(F32) * slack + high_ref[k, r].astype(F32) * value
                ratio = active * inverse(den)
                scaling = value * slack * ratio
                middle = 0.5 * upper - value
                margin = middle * (active + ratio)
                if attacked:
                    margin = margin + jnp.where(hit, WEIGHT_ATTACK * scaling, jnp.zeros_like(scaling))
                if ratio_out:
                    ratio_out[0][k, r] = ratio
                else:
                    ratio_ref[k, r0 + r] = ratio
                tile_s[slot, r, place, :] = scaling
                folded = margin[:, :LANES]
                for part in range(1, half):
                    folded = folded + margin[:, part * LANES : (part + 1) * LANES]
                tile_m[slot, r, place, :] = folded
                total = total + margin
            col_m[place, :] += total
            return 0

        hits = any_attack(info_ref, first_row + r0)

        @pl.when(hits == 0)
        def _():
            lax.fori_loop(0, probs, functools.partial(problem, attacked=False), 0)

        @pl.when(hits != 0)
        def _():
            lax.fori_loop(0, probs, functools.partial(problem, attacked=True), 0)

        @pl.when(block > 0)
        def _():
            sums(other, before)

    cells = pl.BlockSpec((probs, BLOCK, sizes, inds), lambda b: (0, b, 0, 0))
    shared = pl.BlockSpec((BLOCK, sizes, inds), lambda b: (b, 0, 0))
    pltpu.emit_pipeline(
        body,
        grid=(blocks,),
        in_specs=[cells, cells, cells, shared, shared],
        out_specs=[] if RATIO_IN_VMEM else [cells],
    )(pos_hbm, low_hbm, high_hbm, upper_hbm, supp_hbm, *([] if RATIO_IN_VMEM else [ratio_ref]))
    last = blocks - 1
    for r in range(BLOCK):
        turn(last % 2, last, r)
    sums(last % 2, last)
    col_ref[0] = col_m[...].T - dcol_t[...] * col_ref[1] - col_e[...]
    split_halves(col_ref, keep_ref, send_ref, lax.rem(info_ref[0], 2))


def add_up(refs):
    values = [ref[...] for ref in refs]
    while len(values) > 1:
        values = [values[j] + values[j + 1] for j in range(0, len(values), 2)]
    return values[0]


def join_kernel(*refs):
    refs[-1][...] = add_up(refs[:-1])


def begin_kernel(count, info_ref, *refs):
    own, other, row_diag, col_diag, row_now, col_now = refs[count:]
    both = add_up(refs[:count])
    row_diag[...] = both[1] + SHIFT_DIAG
    row_now[...] = both[0] / row_diag[...]
    half = own.shape[1]
    core = lax.rem(info_ref[0], 2)
    for ref, which in ((own, core), (other, 1 - core)):
        here = pl.ds(pl.multiple_of(which * half, 8), half)
        width = ref[1] + SHIFT_DIAG
        col_diag[here, :] = width
        col_now[here, :] = ref[0] / width


def row_end_kernel(*refs):
    refs[-1][...] = add_up(refs[:-2]) / refs[-2][...]


def join_halves(info_ref, own, other, diag, out):
    half = own.shape[0]
    core = lax.rem(info_ref[0], 2)
    for ref, which in ((own, core), (other, 1 - core)):
        here = pl.ds(pl.multiple_of(which * half, 8), half)
        out[here, :] = ref[...] / diag[here, :]


def row_kernel(scaling_ref, col_ref, out_ref):
    rows, inds, _ = scaling_ref.shape

    def step(block, _):
        here = pl.ds(pl.multiple_of(block * BLOCK, BLOCK), BLOCK)
        acc = jnp.zeros((BLOCK, 8, LANES), F32)
        for i0 in range(0, inds, 8):
            acc = acc + scaling_ref[here, i0 : i0 + 8, :] * col_ref[i0 : i0 + 8, :][None]
        out_ref[here, :] = jnp.sum(acc, axis=1)
        return 0

    lax.fori_loop(0, rows // BLOCK, step, 0)


def col_kernel(info_ref, scaling_ref, row_ref, _, keep_ref, send_ref, out_ref):
    rows, inds, _ = scaling_ref.shape
    out_ref[...] = jnp.zeros_like(out_ref)

    def step(block, _):
        here = pl.ds(pl.multiple_of(block * BLOCK, BLOCK), BLOCK)
        row_wide = widen(row_ref[here, :])
        for i0 in range(0, inds, 8):
            out_ref[i0 : i0 + 8, :] += jnp.sum(scaling_ref[here, i0 : i0 + 8, :] * row_wide, axis=0)
        return 0

    lax.fori_loop(0, rows // BLOCK, step, 0)
    split_halves(out_ref, keep_ref, send_ref, lax.rem(info_ref[0], 2))


def products_kernel(iters, nreg, nind, scaling_ref, row_diag_ref, col_diag_ref, *rest):
    count = 3 * iters
    row_p, col_p = [ref[...] for ref in rest[:count]], [ref[...] for ref in rest[count : 2 * count]]
    out_ref, row_z, col_z = rest[2 * count :]
    rows, inds, _ = scaling_ref.shape
    row_zs = [row_p[3 * j] - row_p[3 * j + 1] + row_p[3 * j + 2] for j in range(iters)]
    col_zs = [col_p[3 * j] - col_p[3 * j + 1] + col_p[3 * j + 2] for j in range(iters)]
    row_z[...] = row_zs[-1]
    col_z[...] = col_zs[-1]

    def step(block, acc):
        here = pl.ds(pl.multiple_of(block * BLOCK, BLOCK), BLOCK)
        part = jnp.zeros((BLOCK, 8, LANES), F32)
        for i0 in range(0, inds, 8):
            part = part + scaling_ref[here, i0 : i0 + 8, :] * col_z[i0 : i0 + 8, :][None]
        return acc + jnp.sum(part, axis=1) * row_z[here, :]

    cross = lax.fori_loop(0, rows // BLOCK, step, jnp.zeros((BLOCK, LANES), F32))
    cross = 2.0 * jnp.sum(cross, axis=0, keepdims=True)
    row_diag, col_diag = row_diag_ref[...], col_diag_ref[...]

    def dot(j, row_v, col_v):
        row_sum = jnp.sum(row_zs[j] * row_v, axis=0, keepdims=True)
        col_sum = jnp.sum(col_zs[j] * col_v, axis=0, keepdims=True)
        return row_sum * (1.0 / nind) + col_sum * (1.0 / nreg)

    out_ref[...] = jnp.zeros_like(out_ref)
    slot = 0
    row_n, col_n = row_diag * row_p[0], col_diag * col_p[0]
    for j in range(iters):
        out_ref[slot : slot + 1, :] = dot(j, row_n, col_n)
        slot += 1
    for m in range(iters):
        last = m + 1 == iters
        row_n = row_diag * (row_zs[m] if last else row_p[3 * m] + row_p[3 * m + 3])
        col_n = col_diag * (col_zs[m] if last else col_p[3 * m] + col_p[3 * m + 3])
        for j in range(m, iters):
            product = dot(j, row_n, col_n)
            out_ref[slot : slot + 1, :] = product + cross if last else product
            slot += 1


def finish_kernel(
    rows, sizes, inds, probs, nind, iters, nsum,
    info_ref, pos_hbm, upper_hbm, ratio_ref, drow_ref, dcol_ref, *rest,
):
    count = 3 * iters
    sums, rest = rest[:nsum], rest[nsum:]
    row_p, col_p = rest[:count], rest[count : 2 * count]
    cell_hbm, row_ref, col_ref, row_add, col_add, up_s, row_s = rest[2 * count :]
    first_row = info_ref[0] * rows
    lane = lax.broadcasted_iota(jnp.int32, (LANES, LANES), 0) // sizes
    other = lax.broadcasted_iota(jnp.int32, (LANES, LANES), 1) // sizes
    same = (lane == other).astype(F32)
    total = jnp.dot(add_up(sums), same, preferred_element_type=F32, precision=lax.Precision.HIGHEST)
    g0, g1, g2, h00, h10, h20, h11, h21, h22 = [total[j : j + 1, :] for j in range(9)]
    l1, l2 = h10 / h00, h20 / h00
    d1 = h11 - l1 * h10
    t21 = h21 - l2 * h10
    m21 = t21 / d1
    d2 = h22 - l2 * h20 - m21 * t21
    y1 = g1 - l1 * g0
    y2 = g2 - l2 * g0 - m21 * y1
    c2 = y2 / d2
    c1 = y1 / d1 - m21 * c2
    c0 = g0 / h00 - l1 * c1 - l2 * c2

    def combine(refs):
        acc = None
        for j, coef in enumerate((c0, c1, c2)):
            term = coef * (refs[3 * j][...] - refs[3 * j + 1][...] + refs[3 * j + 2][...])
            acc = term if acc is None else acc + term
        return acc

    row_y = combine(row_p)
    col_turned = combine(col_p).T
    row_ref[...] = row_y.T
    col_ref[...] = col_turned
    row_add[...] = row_y + drow_ref[...].T
    col_add[...] = col_turned + dcol_ref[...]

    def body(pos_ref, upper_ref, *refs):
        cell_ref = refs[-1]
        r0 = pl.multiple_of(pl.program_id(0) * BLOCK, BLOCK)
        up_s[...] = upper_ref[...].astype(F32)
        row_s[...] = row_add[pl.ds(r0, BLOCK), :].T

        def problem(k, _, attacked):
            place = pl.ds(pl.multiple_of(k * sizes, sizes), sizes)
            for r in range(BLOCK):
                upper = up_s[r]
                value = pos_ref[k, r].astype(F32) * upper
                total = row_s[place, r : r + 1] + col_add[place, :]
                if attacked:
                    hit = attacked_tile(info_ref, k, first_row + r0 + r, sizes, inds, nind)
                    total = jnp.where(hit, total - WEIGHT_ATTACK, total)
                ratio = refs[0][k, r] if len(refs) > 1 else ratio_ref[k, r0 + r]
                cell = ratio * (value * (upper - value) * total - (0.5 * upper - value))
                cell_ref[k, r] = cell.astype(jnp.bfloat16)
            return 0

        hits = any_attack(info_ref, first_row + r0)

        @pl.when(hits == 0)
        def _():
            lax.fori_loop(0, probs, functools.partial(problem, attacked=False), 0)

        @pl.when(hits != 0)
        def _():
            lax.fori_loop(0, probs, functools.partial(problem, attacked=True), 0)

    cells = pl.BlockSpec((probs, BLOCK, sizes, inds), lambda b: (0, b, 0, 0))
    shared = pl.BlockSpec((BLOCK, sizes, inds), lambda b: (b, 0, 0))
    more = [] if RATIO_IN_VMEM else [ratio_ref]
    pltpu.emit_pipeline(
        body, grid=(rows // BLOCK,), in_specs=[cells, shared] + [cells] * len(more), out_specs=[cells]
    )(pos_hbm, upper_hbm, *more, cell_hbm)


def bits_of(count):
    return [1 << j for j in range(count.bit_length() - 1)]


def exchange(x, axis, count, bits):
    flips = [0]
    for bit in bits:
        flips = flips + [flip | bit for flip in flips]
    return [x] + [lax.ppermute(x, axis, [(j, j ^ flip) for j in range(count)]) for flip in flips[1:]]


def vmem_call(kernel, outs, name, scratch=(), cost=None, scalars=0):
    def call(*args):
        return pl.pallas_call(
            kernel,
            out_shape=outs,
            in_specs=[SMEM_SPEC] * scalars + [VMEM_SPEC] * (len(args) - scalars),
            out_specs=[VMEM_SPEC] * len(outs),
            scratch_shapes=list(scratch),
            compiler_params=params(),
            cost_estimate=cost,
            name=name,
        )(*args)

    return call


def join(parts):
    return vmem_call(join_kernel, [shape(*parts[0].shape)], "join")(*parts)[0]


def row_sum(x, nind):
    parts = [x]
    for bit in bits_of(nind):
        if len(parts) > 1:
            x = join(parts)
        parts = exchange(x, "industry", nind, [bit])
    return parts


def col_sum(keep, send, nreg):
    (arrived,) = exchange(send, "region", nreg, [1])[1:]
    x = join([keep, arrived])
    bits = bits_of(nreg)[1:]
    for j in range(0, len(bits), 2):
        x = join(exchange(x, "region", nreg, bits[j : j + 2]))
    return exchange(x, "region", nreg, [1])


def local(
    nreg, nind, iters,
    position, dual_lower, dual_upper, upper_bound, suppressed,
    attack_region, attack_column, dual_row, dual_col,
):
    probs, rows, sizes, inds = position.shape
    my_reg, my_ind = lax.axis_index("region"), lax.axis_index("industry")
    info = jnp.concatenate([jnp.stack([my_reg, my_ind]).astype(jnp.int32), attack_region, attack_column])
    drow = dual_row.transpose(0, 2, 1).reshape(LANES, rows)
    dcol = dual_col.reshape(LANES, inds)
    half = inds // 2

    def in_hbm(x):
        return pltpu.with_memory_space_constraint(x, pltpu.HBM)

    def keep(x):
        return pltpu.with_memory_space_constraint(x, pltpu.VMEM)

    position, dual_lower, dual_upper = map(in_hbm, (position, dual_lower, dual_upper))
    upper_bound, suppressed = map(in_hbm, (upper_bound, suppressed))
    whole = (probs, rows, sizes, inds)
    scaling, ratio, row_both, col_keep, col_send = pl.pallas_call(
        functools.partial(prepare_kernel, rows, sizes, inds, probs, nind),
        out_shape=[
            pltpu.VMEM((rows, inds, LANES), F32),
            pltpu.VMEM(whole, F32) if RATIO_IN_VMEM else shape(*whole),
            shape(2, rows, LANES),
            shape(2, half, LANES),
            shape(2, half, LANES),
        ],
        in_specs=[SMEM_SPEC] + [ANY_SPEC] * 5 + [VMEM_SPEC] * 2,
        out_specs=[VMEM_SPEC, VMEM_SPEC if RATIO_IN_VMEM else ANY_SPEC] + [VMEM_SPEC] * 3,
        scratch_shapes=[
            pltpu.VMEM((2, BLOCK, LANES, inds), F32),
            pltpu.VMEM((2, BLOCK, LANES, LANES), F32),
            pltpu.VMEM((BLOCK, sizes, inds), F32),
            pltpu.VMEM((BLOCK, sizes, inds), F32),
            pltpu.VMEM((LANES, inds), F32),
            pltpu.VMEM((inds, LANES), F32),
            pltpu.VMEM((rows, LANES), F32),
            pltpu.VMEM((inds, LANES), F32),
            pltpu.VMEM((2, inds, LANES), F32),
        ],
        compiler_params=params(),
        name="prepare",
    )(info, position, dual_lower, dual_upper, upper_bound, suppressed, drow, dcol)
    scaling = keep(scaling)
    if RATIO_IN_VMEM:
        ratio = keep(ratio)
    cells = rows * inds * LANES
    cost = pl.CostEstimate(flops=2 * cells, bytes_accessed=4 * cells, transcendentals=0)
    margins = [shape(rows, LANES), shape(inds, LANES)]
    row_parts = row_sum(row_both, nind)
    col_halves = col_sum(col_keep, col_send, nreg)
    kernel = functools.partial(begin_kernel, len(row_parts))
    row_diag, col_diag, row_now, col_now = vmem_call(kernel, margins * 2, "begin", scalars=1)(
        info, *row_parts, *col_halves
    )
    row_p, col_p = [row_now], [col_now]
    for _ in range(3 * iters - 1):
        (row_out,) = vmem_call(row_kernel, margins[:1], "row_sweep", cost=cost)(scaling, col_p[-1])
        col_keep, col_send = vmem_call(
            col_kernel, [shape(half, LANES)] * 2, "col_sweep", [pltpu.VMEM((inds, LANES), F32)], cost, 1
        )(info, scaling, row_p[-1], row_out)
        row_parts = row_sum(row_out, nind)
        col_halves = col_sum(col_keep, col_send, nreg)
        row_p += vmem_call(row_end_kernel, margins[:1], "row_end")(*row_parts, row_diag)
        col_p += vmem_call(join_halves, margins[1:], "col_end", scalars=1)(info, *col_halves, col_diag)
    kernel = functools.partial(products_kernel, iters, nreg, nind)
    scratch = [pltpu.VMEM((rows, LANES), F32), pltpu.VMEM((inds, LANES), F32)]
    (part,) = vmem_call(kernel, [shape(16, LANES)], "products", scratch)(
        scaling, row_diag, col_diag, *row_p, *col_p
    )
    bits = bits_of(nreg)
    part = join(exchange(part, "region", nreg, bits[:1]))
    for j in range(1, len(bits), 2):
        part = join(exchange(part, "region", nreg, bits[j : j + 2]))
    bits = bits_of(nind)
    for bit in bits[2:]:
        part = join(exchange(part, "industry", nind, [bit]))
    sums = exchange(part, "industry", nind, bits[:2])
    cell, row_y, col_y = pl.pallas_call(
        functools.partial(finish_kernel, rows, sizes, inds, probs, nind, iters, len(sums)),
        out_shape=[
            jax.ShapeDtypeStruct(whole, jnp.bfloat16),
            shape(LANES, rows),
            shape(LANES, inds),
        ],
        in_specs=[SMEM_SPEC, ANY_SPEC, ANY_SPEC, VMEM_SPEC if RATIO_IN_VMEM else ANY_SPEC]
        + [VMEM_SPEC] * (2 + len(sums) + 6 * iters),
        out_specs=[ANY_SPEC, VMEM_SPEC, VMEM_SPEC],
        scratch_shapes=[
            pltpu.VMEM((rows, LANES), F32),
            pltpu.VMEM((LANES, inds), F32),
            pltpu.VMEM((BLOCK, sizes, inds), F32),
            pltpu.VMEM((LANES, BLOCK), F32),
        ],
        compiler_params=params(),
        name="finish",
    )(info, position, upper_bound, ratio, drow, dcol, *sums, *row_p, *col_p)
    row_step = row_y.reshape(probs, sizes, rows).transpose(0, 2, 1)
    col_step = col_y.reshape(probs, sizes, inds)
    return cell, row_step, col_step


def solution(mesh):
    nreg, nind = mesh.shape["region"], mesh.shape["industry"]
    cells = P(None, "region", None, "industry")
    table = P("region", None, "industry")
    row, col = P(None, "region", None), P(None, None, "industry")
    return jax.shard_map(
        functools.partial(local, nreg, nind, 3),
        mesh=mesh,
        in_specs=(cells, cells, cells, table, table, P(), P(), row, col),
        out_specs=(cells, row, col),
        check_vma=False,
    )
```

time: 275 us -> 253 us (0.920)
  waiting for transfers between devices: 96.6 us -> 47.5 us
  Pallas kernels: 104 us -> 121 us
  starting transfers between devices: 66.5 us -> 71.8 us
  local copies, waits for them, and re-layouts: 4.81 us -> 9.99 us
    ppermute x59 -> x70, waiting for transfers between devices: 96.6 us -> 47.5 us  [exchange(): lax.ppermute(x, axis, [(j, j ^ flip) for j in range(count)])]
    pallas_call x19 -> x63, Pallas kernels: 35.1 us -> 44.2 us  [call(): pl.pallas_call(kernel, out_shape=outs, in_specs=[SMEM_SPEC] * scalars + [...]
    unnamed x4 -> x10, local copies, waits for them, and re-layouts: 1.31 us -> 9.99 us
    pallas_call x1, Pallas kernels: 23.9 us -> 30.6 us  [local(): pl.pallas_call(functools.partial(finish_kernel, rows, sizes, inds, probs,...]
    ppermute x59 -> x70, starting transfers between devices: 66.5 us -> 71.8 us  [exchange(): lax.ppermute(x, axis, [(j, j ^ flip) for j in range(count)])]
  transfers between devices with their start and end apart: 59 -> 70, of which waited for: 24 -> 58; matrix products, arithmetic and copies ran while one was open for 0% -> 0% of each run, Pallas kernels for 0% -> 7%
where the time goes in v3:
time: 253 us; the launch traced here: 252 us
  Pallas kernels  121 us (48%)
  starting transfers between devices  71.8 us (28%)
  waiting for transfers between devices  47.5 us (19%)
  local copies, waits for them, and re-layouts  9.99 us (4%)
    ppermute x70, starting transfers between devices, exchange(): lax.ppermute(x, axis, [(j, j ^ flip) for j in range(count)])  71.8 us
    ppermute x70, waiting for transfers between devices, exchange(): lax.ppermute(x, axis, [(j, j ^ flip) for j in range(count)])  47.5 us
    pallas_call x1, Pallas kernels, local(): pl.pallas_call(functools.partial(prepare_kernel, rows, sizes, inds, probs...  45.7 us
    pallas_call x63, Pallas kernels, call(): pl.pallas_call(kernel, out_shape=outs, in_specs=[SMEM_SPEC] * scalars + [...  44.2 us
    pallas_call x1, Pallas kernels, local(): pl.pallas_call(functools.partial(finish_kernel, rows, sizes, inds, probs,...  30.6 us
    unnamed x10, local copies, waits for them, and re-layouts  9.99 us
  transfers between devices with their start and end apart: 70, of which 58 were waited for; matrix products, arithmetic and copies ran while one was open for 0% of the time, Pallas kernels for 7%

profile of v3, /device:TPU:0, one launch (start us, length us, event | category | flops | bytes accessed | tf_op | source)
XLA Modules:
  0.0 251.8 jit_solution(8491537114098432730)
XLA Ops:
  3.2 45.7 %prepare.1 = (f32[192,256,128]{2,1,0:T(8,128)S(1)}, f32[8,192,16,256]{3,2,1,0:T(8,128)}, f32[2,192,128]{2,1,0:T(8,128)S(1)}, f32[2,128,128]{2,1,0:T(8,128)S(1)}, f32[2,128,128]{2,1,0:T(8,128)S(1)}) custom-call(s32[18]{0:T(128)S(1)} %pad_add_fusion.info_ref, bf16[8,192,16,256]{3,2,1,0:T(8,128)(2,1)} %pos_hbm.3, bf16[8,192,16,256]{3,2,1,0:T(8,128)(2,1)} %low_hbm.1, ...), custom_call_target="tpu_custom_call" | custom-call | tf_op jit(solution)/shard_map/prepare/pallas_call | solution.py:431
  49.4 2.6 %collective-permute-start = (f32[2,192,128]{2,1,0:T(8,128)S(1)}, f32[2,192,128]{2,1,0:T(8,128)S(1)}, u32[]{:S(2)}, u32[]{:S(2)}) collective-permute-start(f32[2,192,128]{2,1,0:T(8,128)S(1)} %get-tuple-element.33.refs_0_), channel_id=1, source_target_pairs={{0,1},{1,0},{2,3},{3,2},{4,5},{5,4},{6,7},{7,6},{8,9},{9,8},{10,11... | collective-permute-start | bytes 589832 | tf_op jit(solution)/shard_map/ppermute | solution.py:369
  52.1 2.6 %collective-permute-start.5 = (f32[2,128,128]{2,1,0:T(8,128)S(1)}, f32[2,128,128]{2,1,0:T(8,128)S(1)}, u32[]{:S(2)}, u32[]{:S(2)}) collective-permute-start(f32[2,128,128]{2,1,0:T(8,128)S(1)} %join.30.refs_0_), channel_id=1, source_target_pairs={{0,24},{4,28},{8,16},{12,20},{16,8},{20,12},{24,0},{28,4},{1,25},{... | collective-permute-start | bytes 393224 | tf_op jit(solution)/shard_map/ppermute | solution.py:369
  57.6 2.8 %collective-permute-start.1 = (f32[2,192,128]{2,1,0:T(8,128)S(1)}, f32[2,192,128]{2,1,0:T(8,128)S(1)}, u32[]{:S(2)}, u32[]{:S(2)}) collective-permute-start(f32[2,192,128]{2,1,0:T(8,128)S(1)} %join.29.refs_0_), channel_id=1, source_target_pairs={{0,2},{1,3},{2,0},{3,1},{4,6},{5,7},{6,4},{7,5},{8,10},{9,11},{10,... | collective-permute-start | bytes 589832 | tf_op jit(solution)/shard_map/ppermute | solution.py:369
  62.9 6.5 %collective-permute-done.1.refs_1_ = f32[2,192,128]{2,1,0:T(8,128)S(1)} collective-permute-done((f32[2,192,128]{2,1,0:T(8,128)S(1)}, f32[2,192,128]{2,1,0:T(8,128)S(1)}, u32[]{:S(2)}, u32[]{:S(2)}) %collective-permute-start.1) | collective-permute-done | bytes 196640 | tf_op jit(solution)/shard_map/ppermute | solution.py:369
  72.0 2.6 %col_sweep.8 = (f32[128,128]{1,0:T(8,128)S(1)}, f32[128,128]{1,0:T(8,128)S(1)}) custom-call(s32[18]{0:T(128)S(1)} %pad_add_fusion.info_ref, f32[192,256,128]{2,1,0:T(8,128)S(1)} %get-tuple-element.32.scaling_ref, f32[192,128]{1,0:T(8,128)S(1)} %get-tuple-element.38.row_ref.rest_0_.rest_4_, f32[192,128]{1,0:T(8,128)S(1)} %row_sweep.8.refs_0_._), custom_call_target="tpu_custom_call" | custom-call | flops 12582912 | bytes 25165824 | tf_op jit(solution)/shard_map/col_sweep/pallas_call | solution.py:374
  75.9 2.5 collective-permute-start.12
  79.9 2.5 collective-permute-start.8
  87.4 2.6 %col_sweep.9 = (f32[128,128]{1,0:T(8,128)S(1)}, f32[128,128]{1,0:T(8,128)S(1)}) custom-call(s32[18]{0:T(128)S(1)} %pad_add_fusion.info_ref, f32[192,256,128]{2,1,0:T(8,128)S(1)} %get-tuple-element.32.scaling_ref, f32[192,128]{1,0:T(8,128)S(1)} %row_end.8.row_ref.rest_1_.rest_5_, f32[192,128]{1,0:T(8,128)S(1)} %row_sweep.9.refs_0_._), custom_call_target="tpu_custom_call" | custom-call | flops 12582912 | bytes 25165824 | tf_op jit(solution)/shard_map/col_sweep/pallas_call | solution.py:374
  91.3 2.5 collective-permute-start.19
  95.3 2.7 %collective-permute-start.15 = (f32[192,128]{1,0:T(8,128)S(1)}, f32[192,128]{1,0:T(8,128)S(1)}, u32[]{:S(2)}, u32[]{:S(2)}) collective-permute-start(f32[192,128]{1,0:T(8,128)S(1)} %join.35.refs_0_), channel_id=1, source_target_pairs={{0,2},{1,3},{2,0},{3,1},{4,6},{5,7},{6,4},{7,5},{8,10},{9,11},{10,... | collective-permute-start | bytes 294920 | tf_op jit(solution)/shard_map/ppermute | solution.py:369
  102.7 2.6 %col_sweep.10 = (f32[128,128]{1,0:T(8,128)S(1)}, f32[128,128]{1,0:T(8,128)S(1)}) custom-call(s32[18]{0:T(128)S(1)} %pad_add_fusion.info_ref, f32[192,256,128]{2,1,0:T(8,128)S(1)} %get-tuple-element.32.scaling_ref, f32[192,128]{1,0:T(8,128)S(1)} %row_end.9.row_ref.rest_2_.rest_6_, f32[192,128]{1,0:T(8,128)S(1)} %row_sweep.10.refs_0_._), custom_call_target="tpu_custom_call" | custom-call | flops 12582912 | bytes 25165824 | tf_op jit(solution)/shard_map/col_sweep/pallas_call | solution.py:374
  106.7 2.5 collective-permute-start.26
  110.7 2.6 %collective-permute-start.22 = (f32[192,128]{1,0:T(8,128)S(1)}, f32[192,128]{1,0:T(8,128)S(1)}, u32[]{:S(2)}, u32[]{:S(2)}) collective-permute-start(f32[192,128]{1,0:T(8,128)S(1)} %join.38.refs_0_), channel_id=1, source_target_pairs={{0,2},{1,3},{2,0},{3,1},{4,6},{5,7},{6,4},{7,5},{8,10},{9,11},{10,... | collective-permute-start | bytes 294920 | tf_op jit(solution)/shard_map/ppermute | solution.py:369
  118.1 2.6 %col_sweep.11 = (f32[128,128]{1,0:T(8,128)S(1)}, f32[128,128]{1,0:T(8,128)S(1)}) custom-call(s32[18]{0:T(128)S(1)} %pad_add_fusion.info_ref, f32[192,256,128]{2,1,0:T(8,128)S(1)} %get-tuple-element.32.scaling_ref, f32[192,128]{1,0:T(8,128)S(1)} %row_end.10.row_ref.rest_3_.rest_7_, f32[192,128]{1,0:T(8,128)S(1)} %row_sweep.11.refs_0_._), custom_call_target="tpu_custom_call" | custom-call | flops 12582912 | bytes 25165824 | tf_op jit(solution)/shard_map/col_sweep/pallas_call | solution.py:374
  122.1 2.5 collective-permute-start.33
  126.0 2.5 collective-permute-start.29
  133.5 2.6 %col_sweep.12 = (f32[128,128]{1,0:T(8,128)S(1)}, f32[128,128]{1,0:T(8,128)S(1)}) custom-call(s32[18]{0:T(128)S(1)} %pad_add_fusion.info_ref, f32[192,256,128]{2,1,0:T(8,128)S(1)} %get-tuple-element.32.scaling_ref, f32[192,128]{1,0:T(8,128)S(1)} %row_end.11.row_ref.rest_4_.rest_8_, f32[192,128]{1,0:T(8,128)S(1)} %row_sweep.12.refs_0_._), custom_call_target="tpu_custom_call" | custom-call | flops 12582912 | bytes 25165824 | tf_op jit(solution)/shard_map/col_sweep/pallas_call | solution.py:374
  137.5 2.5 collective-permute-start.40
  141.4 2.4 collective-permute-start.36
  148.9 2.6 %col_sweep.13 = (f32[128,128]{1,0:T(8,128)S(1)}, f32[128,128]{1,0:T(8,128)S(1)}) custom-call(s32[18]{0:T(128)S(1)} %pad_add_fusion.info_ref, f32[192,256,128]{2,1,0:T(8,128)S(1)} %get-tuple-element.32.scaling_ref, f32[192,128]{1,0:T(8,128)S(1)} %row_end.12.row_ref.rest_5_.rest_9_, f32[192,128]{1,0:T(8,128)S(1)} %row_sweep.13.refs_0_._), custom_call_target="tpu_custom_call" | custom-call | flops 12582912 | bytes 25165824 | tf_op jit(solution)/shard_map/col_sweep/pallas_call | solution.py:374
  152.8 2.5 collective-permute-start.47
  164.3 2.6 %col_sweep.14 = (f32[128,128]{1,0:T(8,128)S(1)}, f32[128,128]{1,0:T(8,128)S(1)}) custom-call(s32[18]{0:T(128)S(1)} %pad_add_fusion.info_ref, f32[192,256,128]{2,1,0:T(8,128)S(1)} %get-tuple-element.32.scaling_ref, f32[192,128]{1,0:T(8,128)S(1)} %row_end.13.row_ref.rest_6_.rest_10_, f32[192,128]{1,0:T(8,128)S(1)} %row_sweep.14.refs_0_._), custom_call_target="tpu_custom_call" | custom-call | flops 12582912 | bytes 25165824 | tf_op jit(solution)/shard_map/col_sweep/pallas_call | solution.py:374
  168.2 2.5 collective-permute-start.54
  179.7 2.6 %col_sweep.15 = (f32[128,128]{1,0:T(8,128)S(1)}, f32[128,128]{1,0:T(8,128)S(1)}) custom-call(s32[18]{0:T(128)S(1)} %pad_add_fusion.info_ref, f32[192,256,128]{2,1,0:T(8,128)S(1)} %get-tuple-element.32.scaling_ref, f32[192,128]{1,0:T(8,128)S(1)} %row_end.14.row_ref.rest_7_.rest_11_, f32[192,128]{1,0:T(8,128)S(1)} %row_sweep.15.refs_0_._), custom_call_target="tpu_custom_call" | custom-call | flops 12582912 | bytes 25165824 | tf_op jit(solution)/shard_map/col_sweep/pallas_call | solution.py:374
  183.6 2.5 collective-permute-start.61
  191.0 4.0 %collective-permute-done.57.refs_1_ = f32[192,128]{1,0:T(8,128)S(1)} collective-permute-done((f32[192,128]{1,0:T(8,128)S(1)}, f32[192,128]{1,0:T(8,128)S(1)}, u32[]{:S(2)}, u32[]{:S(2)}) %collective-permute-start.57) | collective-permute-done | bytes 98336 | tf_op jit(solution)/shard_map/ppermute | solution.py:369
  195.6 2.4 products.1.refs_0_
  199.3 2.4 collective-permute-start.66
  205.9 2.5 collective-permute-start.69
  213.0 8.2 %copy-done = f32[8,192,16,256]{3,2,1,0:T(8,128)S(1)} copy-done((f32[8,192,16,256]{3,2,1,0:T(8,128)S(1)}, f32[8,192,16,256]{3,2,1,0:T(8,128)}, u32[]{:S(2)}) %copy-start) | copy-done | bytes 25165848
  221.1 30.6 %finish.1 = (bf16[8,192,16,256]{3,2,1,0:T(8,128)(2,1)}, f32[128,192]{1,0:T(8,128)}, f32[128,256]{1,0:T(8,128)}) custom-call(s32[18]{0:T(128)S(1)} %pad_add_fusion.info_ref, bf16[8,192,16,256]{3,2,1,0:T(8,128)(2,1)} %pos_hbm.3, s32[192,16,256]{2,1,0:T(8,128)} %upper_hbm.3, f32[8,192,16,256]{3,2,1,0:T(8,128)S(1)} %copy-done, f32[128,192]{1,0:T(8,128)S(1)} %bitcast.11, ...), custom_call_target="tpu_custom_call" | custom-call | tf_op jit(solution)/shard_map/finish/pallas_call | solution.py:491
  (184 shorter events, 86.7 us)
Async XLA Ops:
  49.4 8.1 %collective-permute-start = (f32[2,192,128]{2,1,0:T(8,128)S(1)}, f32[2,192,128]{2,1,0:T(8,128)S(1)}, u32[]{:S(2)}, u32[]{:S(2)}) collective-permute-start(f32[2,192,128]{2,1,0:T(8,128)S(1)} %get-tuple-element.33.refs_0_), channel_id=1, source_target_pairs={{0,1},{1,0},{2,3},{3,2},{4,5},{5,4},{6,7},{7,6},{8,9},{9,8},{10,11... | collective-permute-start | bytes 589832 | tf_op jit(solution)/shard_map/ppermute | solution.py:369
  52.1 8.3 %collective-permute-start.5 = (f32[2,128,128]{2,1,0:T(8,128)S(1)}, f32[2,128,128]{2,1,0:T(8,128)S(1)}, u32[]{:S(2)}, u32[]{:S(2)}) collective-permute-start(f32[2,128,128]{2,1,0:T(8,128)S(1)} %join.30.refs_0_), channel_id=1, source_target_pairs={{0,24},{4,28},{8,16},{12,20},{16,8},{20,12},{24,0},{28,4},{1,25},{... | collective-permute-start | bytes 393224 | tf_op jit(solution)/shard_map/ppermute | solution.py:369
  54.6 6.8 %collective-permute-start.4 = (f32[2,128,128]{2,1,0:T(8,128)S(1)}, f32[2,128,128]{2,1,0:T(8,128)S(1)}, u32[]{:S(2)}, u32[]{:S(2)}) collective-permute-start(f32[2,128,128]{2,1,0:T(8,128)S(1)} %join.30.refs_0_), channel_id=1, source_target_pairs={{0,16},{4,20},{8,24},{12,28},{16,0},{20,4},{24,8},{28,12},{1,17},{... | collective-permute-start | bytes 393224 | tf_op jit(solution)/shard_map/ppermute | solution.py:369
  55.2 6.3 %collective-permute-start.3 = (f32[2,128,128]{2,1,0:T(8,128)S(1)}, f32[2,128,128]{2,1,0:T(8,128)S(1)}, u32[]{:S(2)}, u32[]{:S(2)}) collective-permute-start(f32[2,128,128]{2,1,0:T(8,128)S(1)} %join.30.refs_0_), channel_id=1, source_target_pairs={{0,8},{4,12},{8,0},{12,4},{16,24},{20,28},{24,16},{28,20},{1,9},{5... | collective-permute-start | bytes 393224 | tf_op jit(solution)/shard_map/ppermute | solution.py:369
  57.6 11.8 %collective-permute-start.1 = (f32[2,192,128]{2,1,0:T(8,128)S(1)}, f32[2,192,128]{2,1,0:T(8,128)S(1)}, u32[]{:S(2)}, u32[]{:S(2)}) collective-permute-start(f32[2,192,128]{2,1,0:T(8,128)S(1)} %join.29.refs_0_), channel_id=1, source_target_pairs={{0,2},{1,3},{2,0},{3,1},{4,6},{5,7},{6,4},{7,5},{8,10},{9,11},{10,... | collective-permute-start | bytes 589832 | tf_op jit(solution)/shard_map/ppermute | solution.py:369
  74.7 5.2 %collective-permute-start.7 = (f32[192,128]{1,0:T(8,128)S(1)}, f32[192,128]{1,0:T(8,128)S(1)}, u32[]{:S(2)}, u32[]{:S(2)}) collective-permute-start(f32[192,128]{1,0:T(8,128)S(1)} %row_sweep.8.refs_0_._), channel_id=1, source_target_pairs={{0,1},{1,0},{2,3},{3,2},{4,5},{5,4},{6,7},{7,6},{8,9},{9,8},{10,11... | collective-permute-start | bytes 294920 | tf_op jit(solution)/shard_map/ppermute | solution.py:369
  75.9 6.5 %collective-permute-start.12 = (f32[128,128]{1,0:T(8,128)S(1)}, f32[128,128]{1,0:T(8,128)S(1)}, u32[]{:S(2)}, u32[]{:S(2)}) collective-permute-start(f32[128,128]{1,0:T(8,128)S(1)} %join.33.refs_0_), channel_id=1, source_target_pairs={{0,24},{4,28},{8,16},{12,20},{16,8},{20,12},{24,0},{28,4},{1,25},{... | collective-permute-start | bytes 196616 | tf_op jit(solution)/shard_map/ppermute | solution.py:369
  79.9 7.4 %collective-permute-start.8 = (f32[192,128]{1,0:T(8,128)S(1)}, f32[192,128]{1,0:T(8,128)S(1)}, u32[]{:S(2)}, u32[]{:S(2)}) collective-permute-start(f32[192,128]{1,0:T(8,128)S(1)} %join.32.refs_0_), channel_id=1, source_target_pairs={{0,2},{1,3},{2,0},{3,1},{4,6},{5,7},{6,4},{7,5},{8,10},{9,11},{10,... | collective-permute-start | bytes 294920 | tf_op jit(solution)/shard_map/ppermute | solution.py:369
  90.1 5.2 %collective-permute-start.14 = (f32[192,128]{1,0:T(8,128)S(1)}, f32[192,128]{1,0:T(8,128)S(1)}, u32[]{:S(2)}, u32[]{:S(2)}) collective-permute-start(f32[192,128]{1,0:T(8,128)S(1)} %row_sweep.9.refs_0_._), channel_id=1, source_target_pairs={{0,1},{1,0},{2,3},{3,2},{4,5},{5,4},{6,7},{7,6},{8,9},{9,8},{10,11... | collective-permute-start | bytes 294920 | tf_op jit(solution)/shard_map/ppermute | solution.py:369
  91.3 6.7 %collective-permute-start.19 = (f32[128,128]{1,0:T(8,128)S(1)}, f32[128,128]{1,0:T(8,128)S(1)}, u32[]{:S(2)}, u32[]{:S(2)}) collective-permute-start(f32[128,128]{1,0:T(8,128)S(1)} %join.36.refs_0_), channel_id=1, source_target_pairs={{0,24},{4,28},{8,16},{12,20},{16,8},{20,12},{24,0},{28,4},{1,25},{... | collective-permute-start | bytes 196616 | tf_op jit(solution)/shard_map/ppermute | solution.py:369
  95.3 7.4 %collective-permute-start.15 = (f32[192,128]{1,0:T(8,128)S(1)}, f32[192,128]{1,0:T(8,128)S(1)}, u32[]{:S(2)}, u32[]{:S(2)}) collective-permute-start(f32[192,128]{1,0:T(8,128)S(1)} %join.35.refs_0_), channel_id=1, source_target_pairs={{0,2},{1,3},{2,0},{3,1},{4,6},{5,7},{6,4},{7,5},{8,10},{9,11},{10,... | collective-permute-start | bytes 294920 | tf_op jit(solution)/shard_map/ppermute | solution.py:369
  105.4 5.2 %collective-permute-start.21 = (f32[192,128]{1,0:T(8,128)S(1)}, f32[192,128]{1,0:T(8,128)S(1)}, u32[]{:S(2)}, u32[]{:S(2)}) collective-permute-start(f32[192,128]{1,0:T(8,128)S(1)} %row_sweep.10.refs_0_._), channel_id=1, source_target_pairs={{0,1},{1,0},{2,3},{3,2},{4,5},{5,4},{6,7},{7,6},{8,9},{9,8},{10,11... | collective-permute-start | bytes 294920 | tf_op jit(solution)/shard_map/ppermute | solution.py:369
  106.7 6.6 %collective-permute-start.26 = (f32[128,128]{1,0:T(8,128)S(1)}, f32[128,128]{1,0:T(8,128)S(1)}, u32[]{:S(2)}, u32[]{:S(2)}) collective-permute-start(f32[128,128]{1,0:T(8,128)S(1)} %join.39.refs_0_), channel_id=1, source_target_pairs={{0,24},{4,28},{8,16},{12,20},{16,8},{20,12},{24,0},{28,4},{1,25},{... | collective-permute-start | bytes 196616 | tf_op jit(solution)/shard_map/ppermute | solution.py:369
  110.7 7.4 %collective-permute-start.22 = (f32[192,128]{1,0:T(8,128)S(1)}, f32[192,128]{1,0:T(8,128)S(1)}, u32[]{:S(2)}, u32[]{:S(2)}) collective-permute-start(f32[192,128]{1,0:T(8,128)S(1)} %join.38.refs_0_), channel_id=1, source_target_pairs={{0,2},{1,3},{2,0},{3,1},{4,6},{5,7},{6,4},{7,5},{8,10},{9,11},{10,... | collective-permute-start | bytes 294920 | tf_op jit(solution)/shard_map/ppermute | solution.py:369
  120.8 5.2 %collective-permute-start.28 = (f32[192,128]{1,0:T(8,128)S(1)}, f32[192,128]{1,0:T(8,128)S(1)}, u32[]{:S(2)}, u32[]{:S(2)}) collective-permute-start(f32[192,128]{1,0:T(8,128)S(1)} %row_sweep.11.refs_0_._), channel_id=1, source_target_pairs={{0,1},{1,0},{2,3},{3,2},{4,5},{5,4},{6,7},{7,6},{8,9},{9,8},{10,11... | collective-permute-start | bytes 294920 | tf_op jit(solution)/shard_map/ppermute | solution.py:369
  122.1 6.4 %collective-permute-start.33 = (f32[128,128]{1,0:T(8,128)S(1)}, f32[128,128]{1,0:T(8,128)S(1)}, u32[]{:S(2)}, u32[]{:S(2)}) collective-permute-start(f32[128,128]{1,0:T(8,128)S(1)} %join.42.refs_0_), channel_id=1, source_target_pairs={{0,24},{4,28},{8,16},{12,20},{16,8},{20,12},{24,0},{28,4},{1,25},{... | collective-permute-start | bytes 196616 | tf_op jit(solution)/shard_map/ppermute | solution.py:369
  126.0 7.4 %collective-permute-start.29 = (f32[192,128]{1,0:T(8,128)S(1)}, f32[192,128]{1,0:T(8,128)S(1)}, u32[]{:S(2)}, u32[]{:S(2)}) collective-permute-start(f32[192,128]{1,0:T(8,128)S(1)} %join.41.refs_0_), channel_id=1, source_target_pairs={{0,2},{1,3},{2,0},{3,1},{4,6},{5,7},{6,4},{7,5},{8,10},{9,11},{10,... | collective-permute-start | bytes 294920 | tf_op jit(solution)/shard_map/ppermute | solution.py:369
  136.2 5.2 %collective-permute-start.35 = (f32[192,128]{1,0:T(8,128)S(1)}, f32[192,128]{1,0:T(8,128)S(1)}, u32[]{:S(2)}, u32[]{:S(2)}) collective-permute-start(f32[192,128]{1,0:T(8,128)S(1)} %row_sweep.12.refs_0_._), channel_id=1, source_target_pairs={{0,1},{1,0},{2,3},{3,2},{4,5},{5,4},{6,7},{7,6},{8,9},{9,8},{10,11... | collective-permute-start | bytes 294920 | tf_op jit(solution)/shard_map/ppermute | solution.py:369
  137.5 6.3 %collective-permute-start.40 = (f32[128,128]{1,0:T(8,128)S(1)}, f32[128,128]{1,0:T(8,128)S(1)}, u32[]{:S(2)}, u32[]{:S(2)}) collective-permute-start(f32[128,128]{1,0:T(8,128)S(1)} %join.45.refs_0_), channel_id=1, source_target_pairs={{0,24},{4,28},{8,16},{12,20},{16,8},{20,12},{24,0},{28,4},{1,25},{... | collective-permute-start | bytes 196616 | tf_op jit(solution)/shard_map/ppermute | solution.py:369
  141.4 7.4 %collective-permute-start.36 = (f32[192,128]{1,0:T(8,128)S(1)}, f32[192,128]{1,0:T(8,128)S(1)}, u32[]{:S(2)}, u32[]{:S(2)}) collective-permute-start(f32[192,128]{1,0:T(8,128)S(1)} %join.44.refs_0_), channel_id=1, source_target_pairs={{0,2},{1,3},{2,0},{3,1},{4,6},{5,7},{6,4},{7,5},{8,10},{9,11},{10,... | collective-permute-start | bytes 294920 | tf_op jit(solution)/shard_map/ppermute | solution.py:369
  151.6 5.2 %collective-permute-start.42 = (f32[192,128]{1,0:T(8,128)S(1)}, f32[192,128]{1,0:T(8,128)S(1)}, u32[]{:S(2)}, u32[]{:S(2)}) collective-permute-start(f32[192,128]{1,0:T(8,128)S(1)} %row_sweep.13.refs_0_._), channel_id=1, source_target_pairs={{0,1},{1,0},{2,3},{3,2},{4,5},{5,4},{6,7},{7,6},{8,9},{9,8},{10,11... | collective-permute-start | bytes 294920 | tf_op jit(solution)/shard_map/ppermute | solution.py:369
  152.8 6.2 %collective-permute-start.47 = (f32[128,128]{1,0:T(8,128)S(1)}, f32[128,128]{1,0:T(8,128)S(1)}, u32[]{:S(2)}, u32[]{:S(2)}) collective-permute-start(f32[128,128]{1,0:T(8,128)S(1)} %join.48.refs_0_), channel_id=1, source_target_pairs={{0,24},{4,28},{8,16},{12,20},{16,8},{20,12},{24,0},{28,4},{1,25},{... | collective-permute-start | bytes 196616 | tf_op jit(solution)/shard_map/ppermute | solution.py:369
  156.8 7.4 %collective-permute-start.43 = (f32[192,128]{1,0:T(8,128)S(1)}, f32[192,128]{1,0:T(8,128)S(1)}, u32[]{:S(2)}, u32[]{:S(2)}) collective-permute-start(f32[192,128]{1,0:T(8,128)S(1)} %join.47.refs_0_), channel_id=1, source_target_pairs={{0,2},{1,3},{2,0},{3,1},{4,6},{5,7},{6,4},{7,5},{8,10},{9,11},{10,... | collective-permute-start | bytes 294920 | tf_op jit(solution)/shard_map/ppermute | solution.py:369
  167.0 5.2 %collective-permute-start.49 = (f32[192,128]{1,0:T(8,128)S(1)}, f32[192,128]{1,0:T(8,128)S(1)}, u32[]{:S(2)}, u32[]{:S(2)}) collective-permute-start(f32[192,128]{1,0:T(8,128)S(1)} %row_sweep.14.refs_0_._), channel_id=1, source_target_pairs={{0,1},{1,0},{2,3},{3,2},{4,5},{5,4},{6,7},{7,6},{8,9},{9,8},{10,11... | collective-permute-start | bytes 294920 | tf_op jit(solution)/shard_map/ppermute | solution.py:369
  168.2 6.1 %collective-permute-start.54 = (f32[128,128]{1,0:T(8,128)S(1)}, f32[128,128]{1,0:T(8,128)S(1)}, u32[]{:S(2)}, u32[]{:S(2)}) collective-permute-start(f32[128,128]{1,0:T(8,128)S(1)} %join.51.refs_0_), channel_id=1, source_target_pairs={{0,24},{4,28},{8,16},{12,20},{16,8},{20,12},{24,0},{28,4},{1,25},{... | collective-permute-start | bytes 196616 | tf_op jit(solution)/shard_map/ppermute | solution.py:369
  172.2 7.4 %collective-permute-start.50 = (f32[192,128]{1,0:T(8,128)S(1)}, f32[192,128]{1,0:T(8,128)S(1)}, u32[]{:S(2)}, u32[]{:S(2)}) collective-permute-start(f32[192,128]{1,0:T(8,128)S(1)} %join.50.refs_0_), channel_id=1, source_target_pairs={{0,2},{1,3},{2,0},{3,1},{4,6},{5,7},{6,4},{7,5},{8,10},{9,11},{10,... | collective-permute-start | bytes 294920 | tf_op jit(solution)/shard_map/ppermute | solution.py:369
  182.4 5.2 %collective-permute-start.56 = (f32[192,128]{1,0:T(8,128)S(1)}, f32[192,128]{1,0:T(8,128)S(1)}, u32[]{:S(2)}, u32[]{:S(2)}) collective-permute-start(f32[192,128]{1,0:T(8,128)S(1)} %row_sweep.15.refs_0_._), channel_id=1, source_target_pairs={{0,1},{1,0},{2,3},{3,2},{4,5},{5,4},{6,7},{7,6},{8,9},{9,8},{10,11... | collective-permute-start | bytes 294920 | tf_op jit(solution)/shard_map/ppermute | solution.py:369
  183.6 6.0 %collective-permute-start.61 = (f32[128,128]{1,0:T(8,128)S(1)}, f32[128,128]{1,0:T(8,128)S(1)}, u32[]{:S(2)}, u32[]{:S(2)}) collective-permute-start(f32[128,128]{1,0:T(8,128)S(1)} %join.54.refs_0_), channel_id=1, source_target_pairs={{0,24},{4,28},{8,16},{12,20},{16,8},{20,12},{24,0},{28,4},{1,25},{... | collective-permute-start | bytes 196616 | tf_op jit(solution)/shard_map/ppermute | solution.py:369
  187.6 7.4 %collective-permute-start.57 = (f32[192,128]{1,0:T(8,128)S(1)}, f32[192,128]{1,0:T(8,128)S(1)}, u32[]{:S(2)}, u32[]{:S(2)}) collective-permute-start(f32[192,128]{1,0:T(8,128)S(1)} %join.53.refs_0_), channel_id=1, source_target_pairs={{0,2},{1,3},{2,0},{3,1},{4,6},{5,7},{6,4},{7,5},{8,10},{9,11},{10,... | collective-permute-start | bytes 294920 | tf_op jit(solution)/shard_map/ppermute | solution.py:369
  199.3 4.5 %collective-permute-start.66 = (f32[16,128]{1,0:T(8,128)S(1)}, f32[16,128]{1,0:T(8,128)S(1)}, u32[]{:S(2)}, u32[]{:S(2)}) collective-permute-start(f32[16,128]{1,0:T(8,128)S(1)} %join.56.refs_0_), channel_id=1, source_target_pairs={{0,24},{4,28},{8,16},{12,20},{16,8},{20,12},{24,0},{28,4},{1,25},{... | collective-permute-start | bytes 24584 | tf_op jit(solution)/shard_map/ppermute | solution.py:369
  205.9 5.5 %collective-permute-start.69 = (f32[16,128]{1,0:T(8,128)S(1)}, f32[16,128]{1,0:T(8,128)S(1)}, u32[]{:S(2)}, u32[]{:S(2)}) collective-permute-start(f32[16,128]{1,0:T(8,128)S(1)} %join.57.rest_0_), channel_id=1, source_target_pairs={{0,3},{1,2},{2,1},{3,0},{4,7},{5,6},{6,5},{7,4},{8,11},{9,10},{10,... | collective-permute-start | bytes 24584 | tf_op jit(solution)/shard_map/ppermute | solution.py:369
  208.4 4.5 %collective-permute-start.68 = (f32[16,128]{1,0:T(8,128)S(1)}, f32[16,128]{1,0:T(8,128)S(1)}, u32[]{:S(2)}, u32[]{:S(2)}) collective-permute-start(f32[16,128]{1,0:T(8,128)S(1)} %join.57.rest_0_), channel_id=1, source_target_pairs={{0,2},{1,3},{2,0},{3,1},{4,6},{5,7},{6,4},{7,5},{8,10},{9,11},{10,... | collective-permute-start | bytes 24584 | tf_op jit(solution)/shard_map/ppermute | solution.py:369
  (43 other events, 154.4 us)

commit v4 on v3

--- a/solution.py
+++ b/solution.py
@@ -12,7 +12,6 @@
 BLOCK = 8
 LANES = 128
 VMEM_MIB = 12
-RATIO_IN_VMEM = False
 VMEM_SPEC = pl.BlockSpec(memory_space=pltpu.VMEM)
 SMEM_SPEC = pl.BlockSpec(memory_space=pltpu.SMEM)
 ANY_SPEC = pl.BlockSpec(memory_space=pl.ANY)
@@ -36,18 +35,20 @@
     return jnp.broadcast_to(rows[:, None, :], (BLOCK, 8, LANES))
 
 
-def attacked_tile(info_ref, k, row, sizes, inds, nind):
-    probs = (info_ref.shape[0] - 2) // 2
-    first = info_ref[1] * inds
-    column = lax.broadcasted_iota(jnp.int32, (sizes, inds), 0) * (inds * nind)
-    column = column + lax.broadcasted_iota(jnp.int32, (sizes, inds), 1) + first
-    return column == jnp.where(info_ref[2 + k] == row, info_ref[2 + probs + k], -1)
+def turned(x):
+    return lax.dot_general(
+        identity(x.shape[1]), x, (((1,), (1,)), ((), ())), preferred_element_type=F32
+    )
+
+
+def identity(size):
+    row = lax.broadcasted_iota(jnp.int32, (size, size), 0)
+    return (row == lax.broadcasted_iota(jnp.int32, (size, size), 1)).astype(jnp.bfloat16)
 
 
 def any_attack(info_ref, first_row):
-    probs = (info_ref.shape[0] - 2) // 2
     hits = jnp.int32(0)
-    for k in range(probs):
+    for k in range(info_ref.shape[0] - 2):
         offset = info_ref[2 + k] - first_row
         hits = hits + jnp.where((offset >= 0) & (offset < BLOCK), 1, 0)
     return hits
@@ -61,115 +62,105 @@
 
 def prepare_kernel(
     rows, sizes, inds, probs, nind,
-    info_ref, pos_hbm, low_hbm, high_hbm, upper_hbm, supp_hbm, drow_ref, dcol_ref,
-    scaling_ref, ratio_ref, row_ref, keep_ref, send_ref,
-    tile_s, tile_m, up_s, act_s, col_m, col_e, drow_t, dcol_t, col_ref,
+    info_ref, attack_ref, pos_hbm, low_hbm, high_hbm, upper_hbm, supp_hbm, drow_ref, dcol_ref,
+    scaling_ref, barrier_hbm, row_ref, keep_ref, send_ref,
+    first_s, second_s, drow_t, dcol_t, col_ref,
 ):
     blocks = rows // BLOCK
-    half = inds // LANES
     first_row = info_ref[0] * rows
-    col_m[...] = jnp.zeros_like(col_m)
-    col_e[...] = jnp.zeros_like(col_e)
+    first_ind = info_ref[1] * inds
     col_ref[...] = jnp.zeros_like(col_ref)
     drow_t[...] = drow_ref[...].T
     dcol_t[...] = dcol_ref[...].T
 
-    def turn(slot, before, r):
-        scaling_ref[before * BLOCK + r] = tile_s[slot, r].T
-
-    def sums(slot, before):
-        r0 = pl.multiple_of(before * BLOCK, BLOCK)
-        here = pl.ds(r0, BLOCK)
-        drow = drow_t[here, :]
-        row_wide = widen(drow)
-        sum_acc = jnp.zeros((BLOCK, 8, LANES), F32)
-        dual_acc = jnp.zeros((BLOCK, 8, LANES), F32)
-        for i0 in range(0, inds, 8):
-            tile = scaling_ref[here, i0 : i0 + 8, :]
-            sum_acc = sum_acc + tile
-            dual_acc = dual_acc + tile * dcol_t[i0 : i0 + 8, :][None]
-            col_ref[1, i0 : i0 + 8, :] += jnp.sum(tile, axis=0)
-            col_e[i0 : i0 + 8, :] += jnp.sum(tile * row_wide, axis=0)
-        total = jnp.sum(sum_acc, axis=1)
-        margin = lax.dot_general(
-            jnp.ones((8, LANES), F32),
-            tile_m[slot].reshape(BLOCK * LANES, LANES),
-            (((1,), (1,)), ((), ())),
-            precision=lax.Precision.HIGHEST,
-            preferred_element_type=F32,
-        )
-        margin = jnp.concatenate([margin[:1, r * LANES : (r + 1) * LANES] for r in range(BLOCK)], axis=0)
-        row_ref[1, here, :] = total
-        row_ref[0, here, :] = margin - drow * total - jnp.sum(dual_acc, axis=1)
-
-    def body(pos_ref, low_ref, high_ref, upper_ref, supp_ref, *ratio_out):
-        block = pl.program_id(0)
-        slot = lax.rem(block, 2)
-        other = 1 - slot
-        before = jnp.maximum(block - 1, 0)
-        r0 = block * BLOCK
-        up_s[...] = upper_ref[...].astype(F32)
-        act_s[...] = supp_ref[...].astype(F32)
-
-        def problem(k, _, attacked):
-            turn(other, before, k)
-            total = jnp.zeros((sizes, inds), F32)
-            place = pl.ds(pl.multiple_of(k * sizes, sizes), sizes)
-            for r in range(BLOCK):
-                upper = up_s[r]
-                active = act_s[r]
-                if attacked:
-                    hit = attacked_tile(info_ref, k, first_row + r0 + r, sizes, inds, nind)
-                    active = jnp.where(hit, jnp.ones_like(active), active)
-                value = pos_ref[k, r].astype(F32) * upper
-                slack = upper - value
-                den = low_ref[k, r].astype(F32) * slack + high_ref[k, r].astype(F32) * value
-                ratio = active * inverse(den)
-                scaling = value * slack * ratio
-                middle = 0.5 * upper - value
-                margin = middle * (active + ratio)
-                if attacked:
-                    margin = margin + jnp.where(hit, WEIGHT_ATTACK * scaling, jnp.zeros_like(scaling))
-                if ratio_out:
-                    ratio_out[0][k, r] = ratio
-                else:
-                    ratio_ref[k, r0 + r] = ratio
-                tile_s[slot, r, place, :] = scaling
-                folded = margin[:, :LANES]
-                for part in range(1, half):
-                    folded = folded + margin[:, part * LANES : (part + 1) * LANES]
-                tile_m[slot, r, place, :] = folded
-                total = total + margin
-            col_m[place, :] += total
-            return 0
+    def body(pos_ref, low_ref, high_ref, upper_ref, supp_ref, barrier_ref):
+        r0 = pl.multiple_of(pl.program_id(0) * BLOCK, BLOCK)
+
+        def bring(pair, slot):
+            for j, ref in enumerate((pos_ref, low_ref, high_ref)):
+                both = [ref[:, 2 * pair + r].reshape(LANES, inds) for r in range(2)]
+                slot[j] = turned(jnp.concatenate(both, axis=0))
+            for j, ref in enumerate((upper_ref, supp_ref)):
+                both = []
+                for r in range(2):
+                    one = ref[2 * pair + r].astype(F32).astype(jnp.bfloat16)
+                    both += [one] * probs
+                slot[3 + j] = turned(jnp.concatenate(both, axis=0))
+
+        def work(pair, slot, attacked):
+            rhs_acc = [jnp.zeros((8, LANES), F32)] * 2
+            sum_acc = [jnp.zeros((8, LANES), F32)] * 2
+            drow = [
+                jnp.broadcast_to(drow_t[pl.ds(r0 + 2 * pair + r, 1), :], (8, LANES)) for r in range(2)
+            ]
+            for i0 in range(0, inds, 8):
+                here = slice(i0, i0 + 8)
+                dcol = dcol_t[here, :]
+                col_rhs = col_sum_part = None
+                for r in range(2):
+                    lanes = slice(r * LANES, (r + 1) * LANES)
+                    upper = slot[3, here, lanes]
+                    active = slot[4, here, lanes]
+                    if attacked:
+                        lane = lax.broadcasted_iota(jnp.int32, (8, LANES), 1)
+                        column = lax.rem(lane, sizes) * (inds * nind) + first_ind + i0
+                        column = column + lax.broadcasted_iota(jnp.int32, (8, LANES), 0)
+                        row = first_row + r0 + 2 * pair + r
+                        hit = (attack_ref[1:2, :] == column) & (attack_ref[0:1, :] == row)
+                        active = jnp.where(hit, jnp.ones_like(active), active)
+                    value = slot[0, here, lanes] * upper
+                    slack = upper - value
+                    den = slot[1, here, lanes] * slack + slot[2, here, lanes] * value
+                    ratio = active * inverse(den)
+                    scaling = value * slack * ratio
+                    middle = 0.5 * upper - value
+                    barrier = middle * ratio
+                    if attacked:
+                        barrier = barrier + jnp.where(hit, WEIGHT_ATTACK * scaling, jnp.zeros_like(scaling))
+                    margin = middle * active + barrier - scaling * (drow[r] + dcol)
+                    scaling_ref[r0 + 2 * pair + r, here, :] = scaling
+                    barrier_ref[2 * pair + r, here, :] = barrier
+                    rhs_acc[r] = rhs_acc[r] + margin
+                    sum_acc[r] = sum_acc[r] + scaling
+                    col_rhs = margin if r == 0 else col_rhs + margin
+                    col_sum_part = scaling if r == 0 else col_sum_part + scaling
+                col_ref[0, here, :] += col_rhs
+                col_ref[1, here, :] += col_sum_part
+            for r in range(2):
+                place = pl.ds(r0 + 2 * pair + r, 1)
+                row_ref[0, place, :] = jnp.sum(rhs_acc[r], axis=0, keepdims=True)
+                row_ref[1, place, :] = jnp.sum(sum_acc[r], axis=0, keepdims=True)
 
         hits = any_attack(info_ref, first_row + r0)
+        pairs = BLOCK // 2
 
         @pl.when(hits == 0)
         def _():
-            lax.fori_loop(0, probs, functools.partial(problem, attacked=False), 0)
+            slots = (first_s, second_s)
+            bring(0, slots[0])
+            for pair in range(pairs):
+                if pair + 1 < pairs:
+                    bring(pair + 1, slots[(pair + 1) % 2])
+                work(pair, slots[pair % 2], False)
 
         @pl.when(hits != 0)
         def _():
-            lax.fori_loop(0, probs, functools.partial(problem, attacked=True), 0)
-
-        @pl.when(block > 0)
-        def _():
-            sums(other, before)
+            def step(pair, _):
+                bring(pair, first_s)
+                work(pair, first_s, True)
+                return 0
+
+            lax.fori_loop(0, pairs, step, 0)
 
     cells = pl.BlockSpec((probs, BLOCK, sizes, inds), lambda b: (0, b, 0, 0))
     shared = pl.BlockSpec((BLOCK, sizes, inds), lambda b: (b, 0, 0))
+    turned_cells = pl.BlockSpec((BLOCK, inds, LANES), lambda b: (b, 0, 0))
     pltpu.emit_pipeline(
         body,
         grid=(blocks,),
         in_specs=[cells, cells, cells, shared, shared],
-        out_specs=[] if RATIO_IN_VMEM else [cells],
-    )(pos_hbm, low_hbm, high_hbm, upper_hbm, supp_hbm, *([] if RATIO_IN_VMEM else [ratio_ref]))
-    last = blocks - 1
-    for r in range(BLOCK):
-        turn(last % 2, last, r)
-    sums(last % 2, last)
-    col_ref[0] = col_m[...].T - dcol_t[...] * col_ref[1] - col_e[...]
+        out_specs=[turned_cells],
+    )(pos_hbm, low_hbm, high_hbm, upper_hbm, supp_hbm, barrier_hbm)
     split_halves(col_ref, keep_ref, send_ref, lax.rem(info_ref[0], 2))
 
 
@@ -281,15 +272,11 @@
             slot += 1
 
 
-def finish_kernel(
-    rows, sizes, inds, probs, nind, iters, nsum,
-    info_ref, pos_hbm, upper_hbm, ratio_ref, drow_ref, dcol_ref, *rest,
-):
+def finish_kernel(rows, sizes, inds, probs, iters, nsum, scaling_ref, barrier_hbm, drow_ref, dcol_ref, *rest):
     count = 3 * iters
     sums, rest = rest[:nsum], rest[nsum:]
     row_p, col_p = rest[:count], rest[count : 2 * count]
-    cell_hbm, row_ref, col_ref, row_add, col_add, up_s, row_s = rest[2 * count :]
-    first_row = info_ref[0] * rows
+    cell_hbm, row_ref, col_ref, row_add, col_add = rest[2 * count :]
     lane = lax.broadcasted_iota(jnp.int32, (LANES, LANES), 0) // sizes
     other = lax.broadcasted_iota(jnp.int32, (LANES, LANES), 1) // sizes
     same = (lane == other).astype(F32)
@@ -314,48 +301,24 @@
         return acc
 
     row_y = combine(row_p)
-    col_turned = combine(col_p).T
+    col_y = combine(col_p)
     row_ref[...] = row_y.T
-    col_ref[...] = col_turned
+    col_ref[...] = col_y.T
     row_add[...] = row_y + drow_ref[...].T
-    col_add[...] = col_turned + dcol_ref[...]
-
-    def body(pos_ref, upper_ref, *refs):
-        cell_ref = refs[-1]
-        r0 = pl.multiple_of(pl.program_id(0) * BLOCK, BLOCK)
-        up_s[...] = upper_ref[...].astype(F32)
-        row_s[...] = row_add[pl.ds(r0, BLOCK), :].T
-
-        def problem(k, _, attacked):
-            place = pl.ds(pl.multiple_of(k * sizes, sizes), sizes)
-            for r in range(BLOCK):
-                upper = up_s[r]
-                value = pos_ref[k, r].astype(F32) * upper
-                total = row_s[place, r : r + 1] + col_add[place, :]
-                if attacked:
-                    hit = attacked_tile(info_ref, k, first_row + r0 + r, sizes, inds, nind)
-                    total = jnp.where(hit, total - WEIGHT_ATTACK, total)
-                ratio = refs[0][k, r] if len(refs) > 1 else ratio_ref[k, r0 + r]
-                cell = ratio * (value * (upper - value) * total - (0.5 * upper - value))
-                cell_ref[k, r] = cell.astype(jnp.bfloat16)
-            return 0
-
-        hits = any_attack(info_ref, first_row + r0)
-
-        @pl.when(hits == 0)
-        def _():
-            lax.fori_loop(0, probs, functools.partial(problem, attacked=False), 0)
-
-        @pl.when(hits != 0)
-        def _():
-            lax.fori_loop(0, probs, functools.partial(problem, attacked=True), 0)
+    col_add[...] = col_y + dcol_ref[...].T
+
+    def body(barrier_ref, cell_ref):
+        r0 = pl.program_id(0) * BLOCK
+        for r in range(BLOCK):
+            cell = (col_add[...] + row_add[pl.ds(r0 + r, 1), :]) * scaling_ref[r0 + r] - barrier_ref[r]
+            cell = turned(cell.astype(jnp.bfloat16))
+            cell_ref[:, r] = cell.astype(jnp.bfloat16).reshape(probs, sizes, inds)
 
     cells = pl.BlockSpec((probs, BLOCK, sizes, inds), lambda b: (0, b, 0, 0))
-    shared = pl.BlockSpec((BLOCK, sizes, inds), lambda b: (b, 0, 0))
-    more = [] if RATIO_IN_VMEM else [ratio_ref]
-    pltpu.emit_pipeline(
-        body, grid=(rows // BLOCK,), in_specs=[cells, shared] + [cells] * len(more), out_specs=[cells]
-    )(pos_hbm, upper_hbm, *more, cell_hbm)
+    turned_cells = pl.BlockSpec((BLOCK, inds, LANES), lambda b: (b, 0, 0))
+    pltpu.emit_pipeline(body, grid=(rows // BLOCK,), in_specs=[turned_cells], out_specs=[cells])(
+        barrier_hbm, cell_hbm
+    )
 
 
 def bits_of(count):
@@ -414,7 +377,8 @@
 ):
     probs, rows, sizes, inds = position.shape
     my_reg, my_ind = lax.axis_index("region"), lax.axis_index("industry")
-    info = jnp.concatenate([jnp.stack([my_reg, my_ind]).astype(jnp.int32), attack_region, attack_column])
+    info = jnp.concatenate([jnp.stack([my_reg, my_ind]).astype(jnp.int32), attack_region])
+    attack = jnp.repeat(jnp.stack([attack_region, attack_column]), sizes, axis=1)
     drow = dual_row.transpose(0, 2, 1).reshape(LANES, rows)
     dcol = dual_col.reshape(LANES, inds)
     half = inds // 2
@@ -427,35 +391,29 @@
 
     position, dual_lower, dual_upper = map(in_hbm, (position, dual_lower, dual_upper))
     upper_bound, suppressed = map(in_hbm, (upper_bound, suppressed))
-    whole = (probs, rows, sizes, inds)
-    scaling, ratio, row_both, col_keep, col_send = pl.pallas_call(
+    scaling, barrier, row_both, col_keep, col_send = pl.pallas_call(
         functools.partial(prepare_kernel, rows, sizes, inds, probs, nind),
         out_shape=[
             pltpu.VMEM((rows, inds, LANES), F32),
-            pltpu.VMEM(whole, F32) if RATIO_IN_VMEM else shape(*whole),
+            shape(rows, inds, LANES),
             shape(2, rows, LANES),
             shape(2, half, LANES),
             shape(2, half, LANES),
         ],
-        in_specs=[SMEM_SPEC] + [ANY_SPEC] * 5 + [VMEM_SPEC] * 2,
-        out_specs=[VMEM_SPEC, VMEM_SPEC if RATIO_IN_VMEM else ANY_SPEC] + [VMEM_SPEC] * 3,
+        in_specs=[SMEM_SPEC, VMEM_SPEC] + [ANY_SPEC] * 5 + [VMEM_SPEC] * 2,
+        out_specs=[VMEM_SPEC, ANY_SPEC] + [VMEM_SPEC] * 3,
         scratch_shapes=[
-            pltpu.VMEM((2, BLOCK, LANES, inds), F32),
-            pltpu.VMEM((2, BLOCK, LANES, LANES), F32),
-            pltpu.VMEM((BLOCK, sizes, inds), F32),
-            pltpu.VMEM((BLOCK, sizes, inds), F32),
-            pltpu.VMEM((LANES, inds), F32),
-            pltpu.VMEM((inds, LANES), F32),
+            pltpu.VMEM((5, inds, 2 * LANES), F32),
+            pltpu.VMEM((5, inds, 2 * LANES), F32),
             pltpu.VMEM((rows, LANES), F32),
             pltpu.VMEM((inds, LANES), F32),
             pltpu.VMEM((2, inds, LANES), F32),
         ],
         compiler_params=params(),
         name="prepare",
-    )(info, position, dual_lower, dual_upper, upper_bound, suppressed, drow, dcol)
+    )(info, attack, position, dual_lower, dual_upper, upper_bound, suppressed, drow, dcol)
     scaling = keep(scaling)
-    if RATIO_IN_VMEM:
-        ratio = keep(ratio)
+    barrier = in_hbm(barrier)
     cells = rows * inds * LANES
     cost = pl.CostEstimate(flops=2 * cells, bytes_accessed=4 * cells, transcendentals=0)
     margins = [shape(rows, LANES), shape(inds, LANES)]
@@ -489,24 +447,18 @@
         part = join(exchange(part, "industry", nind, [bit]))
     sums = exchange(part, "industry", nind, bits[:2])
     cell, row_y, col_y = pl.pallas_call(
-        functools.partial(finish_kernel, rows, sizes, inds, probs, nind, iters, len(sums)),
+        functools.partial(finish_kernel, rows, sizes, inds, probs, iters, len(sums)),
         out_shape=[
-            jax.ShapeDtypeStruct(whole, jnp.bfloat16),
+            jax.ShapeDtypeStruct((probs, rows, sizes, inds), jnp.bfloat16),
             shape(LANES, rows),
             shape(LANES, inds),
         ],
-        in_specs=[SMEM_SPEC, ANY_SPEC, ANY_SPEC, VMEM_SPEC if RATIO_IN_VMEM else ANY_SPEC]
-        + [VMEM_SPEC] * (2 + len(sums) + 6 * iters),
+        in_specs=[VMEM_SPEC, ANY_SPEC] + [VMEM_SPEC] * (2 + len(sums) + 6 * iters),
         out_specs=[ANY_SPEC, VMEM_SPEC, VMEM_SPEC],
-        scratch_shapes=[
-            pltpu.VMEM((rows, LANES), F32),
-            pltpu.VMEM((LANES, inds), F32),
-            pltpu.VMEM((BLOCK, sizes, inds), F32),
-            pltpu.VMEM((LANES, BLOCK), F32),
-        ],
+        scratch_shapes=[pltpu.VMEM((rows, LANES), F32), pltpu.VMEM((inds, LANES), F32)],
         compiler_params=params(),
         name="finish",
-    )(info, position, upper_bound, ratio, drow, dcol, *sums, *row_p, *col_p)
+    )(scaling, barrier, drow, dcol, *sums, *row_p, *col_p)
     row_step = row_y.reshape(probs, sizes, rows).transpose(0, 2, 1)
     col_step = col_y.reshape(probs, sizes, inds)
     return cell, row_step, col_step

time: 253 us -> 236 us (0.933)
  Pallas kernels: 121 us -> 112 us
  local copies, waits for them, and re-layouts: 9.99 us -> 1.97 us
  starting transfers between devices: 71.8 us -> 67.2 us
  waiting for transfers between devices: 47.5 us -> 50.3 us
    unnamed x10 -> x6, local copies, waits for them, and re-layouts: 9.99 us -> 1.82 us
    pallas_call x1, Pallas kernels: 30.6 us -> 24.3 us  [local(): pl.pallas_call(functools.partial(finish_kernel, rows, sizes, inds, probs,...]
    ppermute x70, starting transfers between devices: 71.8 us -> 67.2 us  [exchange(): lax.ppermute(x, axis, [(j, j ^ flip) for j in range(count)])]
    pallas_call x1, Pallas kernels: 45.7 us -> 42.6 us  [local(): pl.pallas_call(functools.partial(prepare_kernel, rows, sizes, inds, probs...]
    ppermute x70, waiting for transfers between devices: 47.5 us -> 50.3 us  [exchange(): lax.ppermute(x, axis, [(j, j ^ flip) for j in range(count)])]
  transfers between devices with their start and end apart: 70 -> 70, of which waited for: 58 -> 49; matrix products, arithmetic and copies ran while one was open for 0% -> 0% of each run, Pallas kernels for 7% -> 8%
where the time goes in v4:
time: 236 us; the launch traced here: 234 us
  Pallas kernels  112 us (47%)
  starting transfers between devices  67.2 us (28%)
  waiting for transfers between devices  50.3 us (21%)
    ppermute x70, starting transfers between devices, exchange(): lax.ppermute(x, axis, [(j, j ^ flip) for j in range(count)])  67.2 us
    ppermute x70, waiting for transfers between devices, exchange(): lax.ppermute(x, axis, [(j, j ^ flip) for j in range(count)])  50.3 us
    pallas_call x63, Pallas kernels, call(): pl.pallas_call(kernel, out_shape=outs, in_specs=[SMEM_SPEC] * scalars + [...  45.1 us
    pallas_call x1, Pallas kernels, local(): pl.pallas_call(functools.partial(prepare_kernel, rows, sizes, inds, probs...  42.6 us
    pallas_call x1, Pallas kernels, local(): pl.pallas_call(functools.partial(finish_kernel, rows, sizes, inds, probs,...  24.3 us
  transfers between devices with their start and end apart: 70, of which 49 were waited for; matrix products, arithmetic and copies ran while one was open for 0% of the time, Pallas kernels for 8%

profile of v4, /device:TPU:0, one launch (start us, length us, event | category | flops | bytes accessed | tf_op | source)
XLA Modules:
  0.0 234.0 jit_solution(11912142317859227817)
XLA Ops:
  4.0 42.6 %prepare.1 = (f32[192,256,128]{2,1,0:T(8,128)S(1)}, f32[192,256,128]{2,1,0:T(8,128)}, f32[2,192,128]{2,1,0:T(8,128)S(1)}, f32[2,128,128]{2,1,0:T(8,128)S(1)}, f32[2,128,128]{2,1,0:T(8,128)S(1)}) custom-call(s32[10]{0:T(128)S(1)} %pad_add_fusion.1.info_ref, s32[2,128]{1,0:T(2,128)S(1)} %reshape.21.attack_ref, bf16[8,192,16,256]{3,2,1,0:T(8,128)(2,1)} %pos_hbm.1, ...), custom_call_target="tpu_custom_call" | custom-call | tf_op jit(solution)/shard_map/prepare/pallas_call | solution.py:394
  46.6 2.3 %collective-permute-start.2 = (f32[2,128,128]{2,1,0:T(8,128)S(1)}, f32[2,128,128]{2,1,0:T(8,128)S(1)}, u32[]{:S(2)}, u32[]{:S(2)}) collective-permute-start(f32[2,128,128]{2,1,0:T(8,128)S(1)} %get-tuple-element.35), channel_id=1, source_target_pairs={{0,4},{4,0},{8,12},{12,8},{16,20},{20,16},{24,28},{28,24},{1,5},{5... | collective-permute-start | bytes 393224 | tf_op jit(solution)/shard_map/ppermute | solution.py:332
  49.0 2.4 %collective-permute-start = (f32[2,192,128]{2,1,0:T(8,128)S(1)}, f32[2,192,128]{2,1,0:T(8,128)S(1)}, u32[]{:S(2)}, u32[]{:S(2)}) collective-permute-start(f32[2,192,128]{2,1,0:T(8,128)S(1)} %get-tuple-element.33.refs_0_), channel_id=1, source_target_pairs={{0,1},{1,0},{2,3},{3,2},{4,5},{5,4},{6,7},{7,6},{8,9},{9,8},{10,11... | collective-permute-start | bytes 589832 | tf_op jit(solution)/shard_map/ppermute | solution.py:332
  53.1 1.9 collective-permute-start.3
  56.6 2.8 %collective-permute-start.1 = (f32[2,192,128]{2,1,0:T(8,128)S(1)}, f32[2,192,128]{2,1,0:T(8,128)S(1)}, u32[]{:S(2)}, u32[]{:S(2)}) collective-permute-start(f32[2,192,128]{2,1,0:T(8,128)S(1)} %join.29.refs_0_), channel_id=1, source_target_pairs={{0,2},{1,3},{2,0},{3,1},{4,6},{5,7},{6,4},{7,5},{8,10},{9,11},{10,... | collective-permute-start | bytes 589832 | tf_op jit(solution)/shard_map/ppermute | solution.py:332
  61.8 6.3 %collective-permute-done.1.refs_1_ = f32[2,192,128]{2,1,0:T(8,128)S(1)} collective-permute-done((f32[2,192,128]{2,1,0:T(8,128)S(1)}, f32[2,192,128]{2,1,0:T(8,128)S(1)}, u32[]{:S(2)}, u32[]{:S(2)}) %collective-permute-start.1) | collective-permute-done | bytes 196640 | tf_op jit(solution)/shard_map/ppermute | solution.py:332
  68.7 1.9 row_sweep.8.refs_0_._
  70.6 2.5 %col_sweep.8 = (f32[128,128]{1,0:T(8,128)S(1)}, f32[128,128]{1,0:T(8,128)S(1)}) custom-call(s32[10]{0:T(128)S(1)} %pad_add_fusion.1.info_ref, f32[192,256,128]{2,1,0:T(8,128)S(1)} %get-tuple-element.31.scaling_ref, f32[192,128]{1,0:T(8,128)S(1)} %get-tuple-element.38.row_ref.rest_0_.rest_4_, f32[192,128]{1,0:T(8,128)S(1)} %row_sweep.8.refs_0_._), custom_call_target="tpu_custom_call" | custom-call | flops 12582912 | bytes 25165824 | tf_op jit(solution)/shard_map/col_sweep/pallas_call | solution.py:337
  78.4 2.4 %collective-permute-start.8 = (f32[192,128]{1,0:T(8,128)S(1)}, f32[192,128]{1,0:T(8,128)S(1)}, u32[]{:S(2)}, u32[]{:S(2)}) collective-permute-start(f32[192,128]{1,0:T(8,128)S(1)} %join.32.refs_0_), channel_id=1, source_target_pairs={{0,2},{1,3},{2,0},{3,1},{4,6},{5,7},{6,4},{7,5},{8,10},{9,11},{10,... | collective-permute-start | bytes 294920 | tf_op jit(solution)/shard_map/ppermute | solution.py:332
  82.9 2.1 row_sweep.9.refs_0_._
  85.9 2.5 %col_sweep.9 = (f32[128,128]{1,0:T(8,128)S(1)}, f32[128,128]{1,0:T(8,128)S(1)}) custom-call(s32[10]{0:T(128)S(1)} %pad_add_fusion.1.info_ref, f32[192,256,128]{2,1,0:T(8,128)S(1)} %get-tuple-element.31.scaling_ref, f32[192,128]{1,0:T(8,128)S(1)} %row_end.8.row_ref.rest_1_.rest_5_, f32[192,128]{1,0:T(8,128)S(1)} %row_sweep.9.refs_0_._), custom_call_target="tpu_custom_call" | custom-call | flops 12582912 | bytes 25165824 | tf_op jit(solution)/shard_map/col_sweep/pallas_call | solution.py:337
  93.7 2.3 collective-permute-start.15
  98.2 2.1 row_sweep.10.refs_0_._
  101.2 2.5 %col_sweep.10 = (f32[128,128]{1,0:T(8,128)S(1)}, f32[128,128]{1,0:T(8,128)S(1)}) custom-call(s32[10]{0:T(128)S(1)} %pad_add_fusion.1.info_ref, f32[192,256,128]{2,1,0:T(8,128)S(1)} %get-tuple-element.31.scaling_ref, f32[192,128]{1,0:T(8,128)S(1)} %row_end.9.row_ref.rest_2_.rest_6_, f32[192,128]{1,0:T(8,128)S(1)} %row_sweep.10.refs_0_._), custom_call_target="tpu_custom_call" | custom-call | flops 12582912 | bytes 25165824 | tf_op jit(solution)/shard_map/col_sweep/pallas_call | solution.py:337
  109.0 2.0 collective-permute-start.22
  113.5 2.1 row_sweep.11.refs_0_._
  116.5 2.5 %col_sweep.11 = (f32[128,128]{1,0:T(8,128)S(1)}, f32[128,128]{1,0:T(8,128)S(1)}) custom-call(s32[10]{0:T(128)S(1)} %pad_add_fusion.1.info_ref, f32[192,256,128]{2,1,0:T(8,128)S(1)} %get-tuple-element.31.scaling_ref, f32[192,128]{1,0:T(8,128)S(1)} %row_end.10.row_ref.rest_3_.rest_7_, f32[192,128]{1,0:T(8,128)S(1)} %row_sweep.11.refs_0_._), custom_call_target="tpu_custom_call" | custom-call | flops 12582912 | bytes 25165824 | tf_op jit(solution)/shard_map/col_sweep/pallas_call | solution.py:337
  124.3 1.7 collective-permute-start.29
  128.8 2.1 row_sweep.12.refs_0_._
  131.7 2.5 %col_sweep.12 = (f32[128,128]{1,0:T(8,128)S(1)}, f32[128,128]{1,0:T(8,128)S(1)}) custom-call(s32[10]{0:T(128)S(1)} %pad_add_fusion.1.info_ref, f32[192,256,128]{2,1,0:T(8,128)S(1)} %get-tuple-element.31.scaling_ref, f32[192,128]{1,0:T(8,128)S(1)} %row_end.11.row_ref.rest_4_.rest_8_, f32[192,128]{1,0:T(8,128)S(1)} %row_sweep.12.refs_0_._), custom_call_target="tpu_custom_call" | custom-call | flops 12582912 | bytes 25165824 | tf_op jit(solution)/shard_map/col_sweep/pallas_call | solution.py:337
  144.0 2.1 row_sweep.13.refs_0_._
  146.8 2.5 %col_sweep.13 = (f32[128,128]{1,0:T(8,128)S(1)}, f32[128,128]{1,0:T(8,128)S(1)}) custom-call(s32[10]{0:T(128)S(1)} %pad_add_fusion.1.info_ref, f32[192,256,128]{2,1,0:T(8,128)S(1)} %get-tuple-element.31.scaling_ref, f32[192,128]{1,0:T(8,128)S(1)} %row_end.12.row_ref.rest_5_.rest_9_, f32[192,128]{1,0:T(8,128)S(1)} %row_sweep.13.refs_0_._), custom_call_target="tpu_custom_call" | custom-call | flops 12582912 | bytes 25165824 | tf_op jit(solution)/shard_map/col_sweep/pallas_call | solution.py:337
  159.1 2.1 row_sweep.14.refs_0_._
  161.9 2.5 %col_sweep.14 = (f32[128,128]{1,0:T(8,128)S(1)}, f32[128,128]{1,0:T(8,128)S(1)}) custom-call(s32[10]{0:T(128)S(1)} %pad_add_fusion.1.info_ref, f32[192,256,128]{2,1,0:T(8,128)S(1)} %get-tuple-element.31.scaling_ref, f32[192,128]{1,0:T(8,128)S(1)} %row_end.13.row_ref.rest_6_.rest_10_, f32[192,128]{1,0:T(8,128)S(1)} %row_sweep.14.refs_0_._), custom_call_target="tpu_custom_call" | custom-call | flops 12582912 | bytes 25165824 | tf_op jit(solution)/shard_map/col_sweep/pallas_call | solution.py:337
  174.2 2.1 row_sweep.15.refs_0_._
  177.2 2.5 %col_sweep.15 = (f32[128,128]{1,0:T(8,128)S(1)}, f32[128,128]{1,0:T(8,128)S(1)}) custom-call(s32[10]{0:T(128)S(1)} %pad_add_fusion.1.info_ref, f32[192,256,128]{2,1,0:T(8,128)S(1)} %get-tuple-element.31.scaling_ref, f32[192,128]{1,0:T(8,128)S(1)} %row_end.14.row_ref.rest_7_.rest_11_, f32[192,128]{1,0:T(8,128)S(1)} %row_sweep.15.refs_0_._), custom_call_target="tpu_custom_call" | custom-call | flops 12582912 | bytes 25165824 | tf_op jit(solution)/shard_map/col_sweep/pallas_call | solution.py:337
  187.6 4.5 %collective-permute-done.57.refs_1_ = f32[192,128]{1,0:T(8,128)S(1)} collective-permute-done((f32[192,128]{1,0:T(8,128)S(1)}, f32[192,128]{1,0:T(8,128)S(1)}, u32[]{:S(2)}, u32[]{:S(2)}) %collective-permute-start.57) | collective-permute-done | bytes 98336 | tf_op jit(solution)/shard_map/ppermute | solution.py:332
  192.8 2.4 %products.1.refs_0_ = f32[16,128]{1,0:T(8,128)S(1)} custom-call(f32[192,256,128]{2,1,0:T(8,128)S(1)} %get-tuple-element.31.scaling_ref, f32[192,128]{1,0:T(8,128)S(1)} %get-tuple-element.36.refs_2_.row_diag_ref, f32[256,128]{1,0:T(8,128)S(1)} %get-tuple-element.37.diag.col_diag_ref, f32[192,128]{1,0:T(8,128)S(1)} %get-tuple-element.38.row_ref.rest_0_.rest_4_, ...), custom_call_target="tpu_custom_call" | custom-call | tf_op jit(solution)/shard_map/products/pallas_call | solution.py:337
  202.5 2.7 %collective-permute-start.69 = (f32[16,128]{1,0:T(8,128)S(1)}, f32[16,128]{1,0:T(8,128)S(1)}, u32[]{:S(2)}, u32[]{:S(2)}) collective-permute-start(f32[16,128]{1,0:T(8,128)S(1)} %join.57.rest_0_), channel_id=1, source_target_pairs={{0,3},{1,2},{2,1},{3,0},{4,7},{5,6},{6,5},{7,4},{8,11},{9,10},{10,... | collective-permute-start | bytes 24584 | tf_op jit(solution)/shard_map/ppermute | solution.py:332
  205.1 1.7 collective-permute-start.67
  207.9 1.8 collective-permute-done.68.rest_2_
  209.7 24.3 %finish.1 = (bf16[8,192,16,256]{3,2,1,0:T(8,128)(2,1)}, f32[128,192]{1,0:T(8,128)}, f32[128,256]{1,0:T(8,128)}) custom-call(f32[192,256,128]{2,1,0:T(8,128)S(1)} %get-tuple-element.31.scaling_ref, f32[192,256,128]{2,1,0:T(8,128)} %get-tuple-element.32.barrier_hbm, f32[128,192]{1,0:T(8,128)S(1)} %bitcast.13, f32[128,256]{1,0:T(8,128)S(1)} %bitcast.15, ...), custom_call_target="tpu_custom_call" | custom-call | tf_op jit(solution)/shard_map/finish/pallas_call | solution.py:449
  (183 shorter events, 91.7 us)
Async XLA Ops:
  49.0 7.5 %collective-permute-start = (f32[2,192,128]{2,1,0:T(8,128)S(1)}, f32[2,192,128]{2,1,0:T(8,128)S(1)}, u32[]{:S(2)}, u32[]{:S(2)}) collective-permute-start(f32[2,192,128]{2,1,0:T(8,128)S(1)} %get-tuple-element.33.refs_0_), channel_id=1, source_target_pairs={{0,1},{1,0},{2,3},{3,2},{4,5},{5,4},{6,7},{7,6},{8,9},{9,8},{10,11... | collective-permute-start | bytes 589832 | tf_op jit(solution)/shard_map/ppermute | solution.py:332
  51.4 8.0 %collective-permute-start.5 = (f32[2,128,128]{2,1,0:T(8,128)S(1)}, f32[2,128,128]{2,1,0:T(8,128)S(1)}, u32[]{:S(2)}, u32[]{:S(2)}) collective-permute-start(f32[2,128,128]{2,1,0:T(8,128)S(1)} %join.30.refs_0_), channel_id=1, source_target_pairs={{0,24},{4,28},{8,16},{12,20},{16,8},{20,12},{24,0},{28,4},{1,25},{... | collective-permute-start | bytes 393224 | tf_op jit(solution)/shard_map/ppermute | solution.py:332
  53.1 7.3 %collective-permute-start.4 = (f32[2,128,128]{2,1,0:T(8,128)S(1)}, f32[2,128,128]{2,1,0:T(8,128)S(1)}, u32[]{:S(2)}, u32[]{:S(2)}) collective-permute-start(f32[2,128,128]{2,1,0:T(8,128)S(1)} %join.30.refs_0_), channel_id=1, source_target_pairs={{0,16},{4,20},{8,24},{12,28},{16,0},{20,4},{24,8},{28,12},{1,17},{... | collective-permute-start | bytes 393224 | tf_op jit(solution)/shard_map/ppermute | solution.py:332
  53.1 7.3 %collective-permute-start.3 = (f32[2,128,128]{2,1,0:T(8,128)S(1)}, f32[2,128,128]{2,1,0:T(8,128)S(1)}, u32[]{:S(2)}, u32[]{:S(2)}) collective-permute-start(f32[2,128,128]{2,1,0:T(8,128)S(1)} %join.30.refs_0_), channel_id=1, source_target_pairs={{0,8},{4,12},{8,0},{12,4},{16,24},{20,28},{24,16},{28,20},{1,9},{5... | collective-permute-start | bytes 393224 | tf_op jit(solution)/shard_map/ppermute | solution.py:332
  56.6 11.5 %collective-permute-start.1 = (f32[2,192,128]{2,1,0:T(8,128)S(1)}, f32[2,192,128]{2,1,0:T(8,128)S(1)}, u32[]{:S(2)}, u32[]{:S(2)}) collective-permute-start(f32[2,192,128]{2,1,0:T(8,128)S(1)} %join.29.refs_0_), channel_id=1, source_target_pairs={{0,2},{1,3},{2,0},{3,1},{4,6},{5,7},{6,4},{7,5},{8,10},{9,11},{10,... | collective-permute-start | bytes 589832 | tf_op jit(solution)/shard_map/ppermute | solution.py:332
  73.2 5.2 %collective-permute-start.7 = (f32[192,128]{1,0:T(8,128)S(1)}, f32[192,128]{1,0:T(8,128)S(1)}, u32[]{:S(2)}, u32[]{:S(2)}) collective-permute-start(f32[192,128]{1,0:T(8,128)S(1)} %row_sweep.8.refs_0_._), channel_id=1, source_target_pairs={{0,1},{1,0},{2,3},{3,2},{4,5},{5,4},{6,7},{7,6},{8,9},{9,8},{10,11... | collective-permute-start | bytes 294920 | tf_op jit(solution)/shard_map/ppermute | solution.py:332
  74.5 6.4 %collective-permute-start.12 = (f32[128,128]{1,0:T(8,128)S(1)}, f32[128,128]{1,0:T(8,128)S(1)}, u32[]{:S(2)}, u32[]{:S(2)}) collective-permute-start(f32[128,128]{1,0:T(8,128)S(1)} %join.33.refs_0_), channel_id=1, source_target_pairs={{0,24},{4,28},{8,16},{12,20},{16,8},{20,12},{24,0},{28,4},{1,25},{... | collective-permute-start | bytes 196616 | tf_op jit(solution)/shard_map/ppermute | solution.py:332
  75.9 5.0 %collective-permute-start.11 = (f32[128,128]{1,0:T(8,128)S(1)}, f32[128,128]{1,0:T(8,128)S(1)}, u32[]{:S(2)}, u32[]{:S(2)}) collective-permute-start(f32[128,128]{1,0:T(8,128)S(1)} %join.33.refs_0_), channel_id=1, source_target_pairs={{0,16},{4,20},{8,24},{12,28},{16,0},{20,4},{24,8},{28,12},{1,17},{... | collective-permute-start | bytes 196616 | tf_op jit(solution)/shard_map/ppermute | solution.py:332
  78.4 7.4 %collective-permute-start.8 = (f32[192,128]{1,0:T(8,128)S(1)}, f32[192,128]{1,0:T(8,128)S(1)}, u32[]{:S(2)}, u32[]{:S(2)}) collective-permute-start(f32[192,128]{1,0:T(8,128)S(1)} %join.32.refs_0_), channel_id=1, source_target_pairs={{0,2},{1,3},{2,0},{3,1},{4,6},{5,7},{6,4},{7,5},{8,10},{9,11},{10,... | collective-permute-start | bytes 294920 | tf_op jit(solution)/shard_map/ppermute | solution.py:332
  88.5 5.2 %collective-permute-start.14 = (f32[192,128]{1,0:T(8,128)S(1)}, f32[192,128]{1,0:T(8,128)S(1)}, u32[]{:S(2)}, u32[]{:S(2)}) collective-permute-start(f32[192,128]{1,0:T(8,128)S(1)} %row_sweep.9.refs_0_._), channel_id=1, source_target_pairs={{0,1},{1,0},{2,3},{3,2},{4,5},{5,4},{6,7},{7,6},{8,9},{9,8},{10,11... | collective-permute-start | bytes 294920 | tf_op jit(solution)/shard_map/ppermute | solution.py:332
  89.7 6.3 %collective-permute-start.19 = (f32[128,128]{1,0:T(8,128)S(1)}, f32[128,128]{1,0:T(8,128)S(1)}, u32[]{:S(2)}, u32[]{:S(2)}) collective-permute-start(f32[128,128]{1,0:T(8,128)S(1)} %join.36.refs_0_), channel_id=1, source_target_pairs={{0,24},{4,28},{8,16},{12,20},{16,8},{20,12},{24,0},{28,4},{1,25},{... | collective-permute-start | bytes 196616 | tf_op jit(solution)/shard_map/ppermute | solution.py:332
  91.2 5.0 %collective-permute-start.18 = (f32[128,128]{1,0:T(8,128)S(1)}, f32[128,128]{1,0:T(8,128)S(1)}, u32[]{:S(2)}, u32[]{:S(2)}) collective-permute-start(f32[128,128]{1,0:T(8,128)S(1)} %join.36.refs_0_), channel_id=1, source_target_pairs={{0,16},{4,20},{8,24},{12,28},{16,0},{20,4},{24,8},{28,12},{1,17},{... | collective-permute-start | bytes 196616 | tf_op jit(solution)/shard_map/ppermute | solution.py:332
  93.7 7.4 %collective-permute-start.15 = (f32[192,128]{1,0:T(8,128)S(1)}, f32[192,128]{1,0:T(8,128)S(1)}, u32[]{:S(2)}, u32[]{:S(2)}) collective-permute-start(f32[192,128]{1,0:T(8,128)S(1)} %join.35.refs_0_), channel_id=1, source_target_pairs={{0,2},{1,3},{2,0},{3,1},{4,6},{5,7},{6,4},{7,5},{8,10},{9,11},{10,... | collective-permute-start | bytes 294920 | tf_op jit(solution)/shard_map/ppermute | solution.py:332
  103.8 5.2 %collective-permute-start.21 = (f32[192,128]{1,0:T(8,128)S(1)}, f32[192,128]{1,0:T(8,128)S(1)}, u32[]{:S(2)}, u32[]{:S(2)}) collective-permute-start(f32[192,128]{1,0:T(8,128)S(1)} %row_sweep.10.refs_0_._), channel_id=1, source_target_pairs={{0,1},{1,0},{2,3},{3,2},{4,5},{5,4},{6,7},{7,6},{8,9},{9,8},{10,11... | collective-permute-start | bytes 294920 | tf_op jit(solution)/shard_map/ppermute | solution.py:332
  105.0 6.0 %collective-permute-start.26 = (f32[128,128]{1,0:T(8,128)S(1)}, f32[128,128]{1,0:T(8,128)S(1)}, u32[]{:S(2)}, u32[]{:S(2)}) collective-permute-start(f32[128,128]{1,0:T(8,128)S(1)} %join.39.refs_0_), channel_id=1, source_target_pairs={{0,24},{4,28},{8,16},{12,20},{16,8},{20,12},{24,0},{28,4},{1,25},{... | collective-permute-start | bytes 196616 | tf_op jit(solution)/shard_map/ppermute | solution.py:332
  109.0 7.4 %collective-permute-start.22 = (f32[192,128]{1,0:T(8,128)S(1)}, f32[192,128]{1,0:T(8,128)S(1)}, u32[]{:S(2)}, u32[]{:S(2)}) collective-permute-start(f32[192,128]{1,0:T(8,128)S(1)} %join.38.refs_0_), channel_id=1, source_target_pairs={{0,2},{1,3},{2,0},{3,1},{4,6},{5,7},{6,4},{7,5},{8,10},{9,11},{10,... | collective-permute-start | bytes 294920 | tf_op jit(solution)/shard_map/ppermute | solution.py:332
  119.1 5.2 %collective-permute-start.28 = (f32[192,128]{1,0:T(8,128)S(1)}, f32[192,128]{1,0:T(8,128)S(1)}, u32[]{:S(2)}, u32[]{:S(2)}) collective-permute-start(f32[192,128]{1,0:T(8,128)S(1)} %row_sweep.11.refs_0_._), channel_id=1, source_target_pairs={{0,1},{1,0},{2,3},{3,2},{4,5},{5,4},{6,7},{7,6},{8,9},{9,8},{10,11... | collective-permute-start | bytes 294920 | tf_op jit(solution)/shard_map/ppermute | solution.py:332
  120.3 5.7 %collective-permute-start.33 = (f32[128,128]{1,0:T(8,128)S(1)}, f32[128,128]{1,0:T(8,128)S(1)}, u32[]{:S(2)}, u32[]{:S(2)}) collective-permute-start(f32[128,128]{1,0:T(8,128)S(1)} %join.42.refs_0_), channel_id=1, source_target_pairs={{0,24},{4,28},{8,16},{12,20},{16,8},{20,12},{24,0},{28,4},{1,25},{... | collective-permute-start | bytes 196616 | tf_op jit(solution)/shard_map/ppermute | solution.py:332
  124.3 7.4 %collective-permute-start.29 = (f32[192,128]{1,0:T(8,128)S(1)}, f32[192,128]{1,0:T(8,128)S(1)}, u32[]{:S(2)}, u32[]{:S(2)}) collective-permute-start(f32[192,128]{1,0:T(8,128)S(1)} %join.41.refs_0_), channel_id=1, source_target_pairs={{0,2},{1,3},{2,0},{3,1},{4,6},{5,7},{6,4},{7,5},{8,10},{9,11},{10,... | collective-permute-start | bytes 294920 | tf_op jit(solution)/shard_map/ppermute | solution.py:332
  134.3 5.2 %collective-permute-start.35 = (f32[192,128]{1,0:T(8,128)S(1)}, f32[192,128]{1,0:T(8,128)S(1)}, u32[]{:S(2)}, u32[]{:S(2)}) collective-permute-start(f32[192,128]{1,0:T(8,128)S(1)} %row_sweep.12.refs_0_._), channel_id=1, source_target_pairs={{0,1},{1,0},{2,3},{3,2},{4,5},{5,4},{6,7},{7,6},{8,9},{9,8},{10,11... | collective-permute-start | bytes 294920 | tf_op jit(solution)/shard_map/ppermute | solution.py:332
  135.6 5.5 %collective-permute-start.40 = (f32[128,128]{1,0:T(8,128)S(1)}, f32[128,128]{1,0:T(8,128)S(1)}, u32[]{:S(2)}, u32[]{:S(2)}) collective-permute-start(f32[128,128]{1,0:T(8,128)S(1)} %join.45.refs_0_), channel_id=1, source_target_pairs={{0,24},{4,28},{8,16},{12,20},{16,8},{20,12},{24,0},{28,4},{1,25},{... | collective-permute-start | bytes 196616 | tf_op jit(solution)/shard_map/ppermute | solution.py:332
  139.5 7.3 %collective-permute-start.36 = (f32[192,128]{1,0:T(8,128)S(1)}, f32[192,128]{1,0:T(8,128)S(1)}, u32[]{:S(2)}, u32[]{:S(2)}) collective-permute-start(f32[192,128]{1,0:T(8,128)S(1)} %join.44.refs_0_), channel_id=1, source_target_pairs={{0,2},{1,3},{2,0},{3,1},{4,6},{5,7},{6,4},{7,5},{8,10},{9,11},{10,... | collective-permute-start | bytes 294920 | tf_op jit(solution)/shard_map/ppermute | solution.py:332
  149.4 5.2 %collective-permute-start.42 = (f32[192,128]{1,0:T(8,128)S(1)}, f32[192,128]{1,0:T(8,128)S(1)}, u32[]{:S(2)}, u32[]{:S(2)}) collective-permute-start(f32[192,128]{1,0:T(8,128)S(1)} %row_sweep.13.refs_0_._), channel_id=1, source_target_pairs={{0,1},{1,0},{2,3},{3,2},{4,5},{5,4},{6,7},{7,6},{8,9},{9,8},{10,11... | collective-permute-start | bytes 294920 | tf_op jit(solution)/shard_map/ppermute | solution.py:332
  150.7 5.7 %collective-permute-start.47 = (f32[128,128]{1,0:T(8,128)S(1)}, f32[128,128]{1,0:T(8,128)S(1)}, u32[]{:S(2)}, u32[]{:S(2)}) collective-permute-start(f32[128,128]{1,0:T(8,128)S(1)} %join.48.refs_0_), channel_id=1, source_target_pairs={{0,24},{4,28},{8,16},{12,20},{16,8},{20,12},{24,0},{28,4},{1,25},{... | collective-permute-start | bytes 196616 | tf_op jit(solution)/shard_map/ppermute | solution.py:332
  154.6 7.2 %collective-permute-start.43 = (f32[192,128]{1,0:T(8,128)S(1)}, f32[192,128]{1,0:T(8,128)S(1)}, u32[]{:S(2)}, u32[]{:S(2)}) collective-permute-start(f32[192,128]{1,0:T(8,128)S(1)} %join.47.refs_0_), channel_id=1, source_target_pairs={{0,2},{1,3},{2,0},{3,1},{4,6},{5,7},{6,4},{7,5},{8,10},{9,11},{10,... | collective-permute-start | bytes 294920 | tf_op jit(solution)/shard_map/ppermute | solution.py:332
  164.5 5.2 %collective-permute-start.49 = (f32[192,128]{1,0:T(8,128)S(1)}, f32[192,128]{1,0:T(8,128)S(1)}, u32[]{:S(2)}, u32[]{:S(2)}) collective-permute-start(f32[192,128]{1,0:T(8,128)S(1)} %row_sweep.14.refs_0_._), channel_id=1, source_target_pairs={{0,1},{1,0},{2,3},{3,2},{4,5},{5,4},{6,7},{7,6},{8,9},{9,8},{10,11... | collective-permute-start | bytes 294920 | tf_op jit(solution)/shard_map/ppermute | solution.py:332
  165.7 5.7 %collective-permute-start.54 = (f32[128,128]{1,0:T(8,128)S(1)}, f32[128,128]{1,0:T(8,128)S(1)}, u32[]{:S(2)}, u32[]{:S(2)}) collective-permute-start(f32[128,128]{1,0:T(8,128)S(1)} %join.51.refs_0_), channel_id=1, source_target_pairs={{0,24},{4,28},{8,16},{12,20},{16,8},{20,12},{24,0},{28,4},{1,25},{... | collective-permute-start | bytes 196616 | tf_op jit(solution)/shard_map/ppermute | solution.py:332
  169.7 7.4 %collective-permute-start.50 = (f32[192,128]{1,0:T(8,128)S(1)}, f32[192,128]{1,0:T(8,128)S(1)}, u32[]{:S(2)}, u32[]{:S(2)}) collective-permute-start(f32[192,128]{1,0:T(8,128)S(1)} %join.50.refs_0_), channel_id=1, source_target_pairs={{0,2},{1,3},{2,0},{3,1},{4,6},{5,7},{6,4},{7,5},{8,10},{9,11},{10,... | collective-permute-start | bytes 294920 | tf_op jit(solution)/shard_map/ppermute | solution.py:332
  179.7 5.2 %collective-permute-start.56 = (f32[192,128]{1,0:T(8,128)S(1)}, f32[192,128]{1,0:T(8,128)S(1)}, u32[]{:S(2)}, u32[]{:S(2)}) collective-permute-start(f32[192,128]{1,0:T(8,128)S(1)} %row_sweep.15.refs_0_._), channel_id=1, source_target_pairs={{0,1},{1,0},{2,3},{3,2},{4,5},{5,4},{6,7},{7,6},{8,9},{9,8},{10,11... | collective-permute-start | bytes 294920 | tf_op jit(solution)/shard_map/ppermute | solution.py:332
  181.0 5.4 %collective-permute-start.61 = (f32[128,128]{1,0:T(8,128)S(1)}, f32[128,128]{1,0:T(8,128)S(1)}, u32[]{:S(2)}, u32[]{:S(2)}) collective-permute-start(f32[128,128]{1,0:T(8,128)S(1)} %join.54.refs_0_), channel_id=1, source_target_pairs={{0,24},{4,28},{8,16},{12,20},{16,8},{20,12},{24,0},{28,4},{1,25},{... | collective-permute-start | bytes 196616 | tf_op jit(solution)/shard_map/ppermute | solution.py:332
  185.0 7.2 %collective-permute-start.57 = (f32[192,128]{1,0:T(8,128)S(1)}, f32[192,128]{1,0:T(8,128)S(1)}, u32[]{:S(2)}, u32[]{:S(2)}) collective-permute-start(f32[192,128]{1,0:T(8,128)S(1)} %join.53.refs_0_), channel_id=1, source_target_pairs={{0,2},{1,3},{2,0},{3,1},{4,6},{5,7},{6,4},{7,5},{8,10},{9,11},{10,... | collective-permute-start | bytes 294920 | tf_op jit(solution)/shard_map/ppermute | solution.py:332
  202.5 5.4 %collective-permute-start.69 = (f32[16,128]{1,0:T(8,128)S(1)}, f32[16,128]{1,0:T(8,128)S(1)}, u32[]{:S(2)}, u32[]{:S(2)}) collective-permute-start(f32[16,128]{1,0:T(8,128)S(1)} %join.57.rest_0_), channel_id=1, source_target_pairs={{0,3},{1,2},{2,1},{3,0},{4,7},{5,6},{6,5},{7,4},{8,11},{9,10},{10,... | collective-permute-start | bytes 24584 | tf_op jit(solution)/shard_map/ppermute | solution.py:332
  (41 other events, 136.8 us)

commit v5 on v4

--- a/solution.py
+++ b/solution.py
@@ -48,21 +48,23 @@
 
 def any_attack(info_ref, first_row):
     hits = jnp.int32(0)
-    for k in range(info_ref.shape[0] - 2):
+    for k in range((info_ref.shape[0] - 2) // 2):
         offset = info_ref[2 + k] - first_row
         hits = hits + jnp.where((offset >= 0) & (offset < BLOCK), 1, 0)
     return hits
 
 
-def split_halves(full, keep_ref, send_ref, core):
+def split_halves(full, keep_ref, send_ref, odd_ref):
     half = full.shape[-2] // 2
-    for ref, which in ((keep_ref, core), (send_ref, 1 - core)):
-        ref[...] = full[..., pl.ds(pl.multiple_of(which * half, 8), half), :]
+    odd = jnp.broadcast_to(odd_ref[0:1, :] > 0, keep_ref.shape)
+    first, second = full[..., :half, :], full[..., half:, :]
+    keep_ref[...] = jnp.where(odd, second, first)
+    send_ref[...] = jnp.where(odd, first, second)
 
 
 def prepare_kernel(
     rows, sizes, inds, probs, nind,
-    info_ref, attack_ref, pos_hbm, low_hbm, high_hbm, upper_hbm, supp_hbm, drow_ref, dcol_ref,
+    info_ref, odd_ref, pos_hbm, low_hbm, high_hbm, upper_hbm, supp_hbm, drow_ref, dcol_ref,
     scaling_ref, barrier_hbm, row_ref, keep_ref, send_ref,
     first_s, second_s, drow_t, dcol_t, col_ref,
 ):
@@ -106,7 +108,11 @@
                         column = lax.rem(lane, sizes) * (inds * nind) + first_ind + i0
                         column = column + lax.broadcasted_iota(jnp.int32, (8, LANES), 0)
                         row = first_row + r0 + 2 * pair + r
-                        hit = (attack_ref[1:2, :] == column) & (attack_ref[0:1, :] == row)
+                        goal = jnp.full((8, LANES), -1, jnp.int32)
+                        for k in range(probs):
+                            mine = jnp.where(info_ref[2 + k] == row, info_ref[2 + probs + k], -1)
+                            goal = jnp.where(lane // sizes == k, mine, goal)
+                        hit = goal == column
                         active = jnp.where(hit, jnp.ones_like(active), active)
                     value = slot[0, here, lanes] * upper
                     slack = upper - value
@@ -152,8 +158,9 @@
 
             lax.fori_loop(0, pairs, step, 0)
 
-    cells = pl.BlockSpec((probs, BLOCK, sizes, inds), lambda b: (0, b, 0, 0))
-    shared = pl.BlockSpec((BLOCK, sizes, inds), lambda b: (b, 0, 0))
+    deep = pl.Buffered(3)
+    cells = pl.BlockSpec((probs, BLOCK, sizes, inds), lambda b: (0, b, 0, 0), pipeline_mode=deep)
+    shared = pl.BlockSpec((BLOCK, sizes, inds), lambda b: (b, 0, 0), pipeline_mode=deep)
     turned_cells = pl.BlockSpec((BLOCK, inds, LANES), lambda b: (b, 0, 0))
     pltpu.emit_pipeline(
         body,
@@ -161,7 +168,7 @@
         in_specs=[cells, cells, cells, shared, shared],
         out_specs=[turned_cells],
     )(pos_hbm, low_hbm, high_hbm, upper_hbm, supp_hbm, barrier_hbm)
-    split_halves(col_ref, keep_ref, send_ref, lax.rem(info_ref[0], 2))
+    split_halves(col_ref, keep_ref, send_ref, odd_ref)
 
 
 def add_up(refs):
@@ -175,30 +182,30 @@
     refs[-1][...] = add_up(refs[:-1])
 
 
-def begin_kernel(count, info_ref, *refs):
+def begin_kernel(count, odd_ref, *refs):
     own, other, row_diag, col_diag, row_now, col_now = refs[count:]
     both = add_up(refs[:count])
     row_diag[...] = both[1] + SHIFT_DIAG
     row_now[...] = both[0] / row_diag[...]
     half = own.shape[1]
-    core = lax.rem(info_ref[0], 2)
-    for ref, which in ((own, core), (other, 1 - core)):
-        here = pl.ds(pl.multiple_of(which * half, 8), half)
-        width = ref[1] + SHIFT_DIAG
+    odd = jnp.broadcast_to(odd_ref[0:1, :] > 0, own.shape)
+    halves = jnp.where(odd, other[...], own[...]), jnp.where(odd, own[...], other[...])
+    for j, part in enumerate(halves):
+        here = slice(j * half, (j + 1) * half)
+        width = part[1] + SHIFT_DIAG
         col_diag[here, :] = width
-        col_now[here, :] = ref[0] / width
+        col_now[here, :] = part[0] / width
 
 
 def row_end_kernel(*refs):
     refs[-1][...] = add_up(refs[:-2]) / refs[-2][...]
 
 
-def join_halves(info_ref, own, other, diag, out):
+def join_halves(odd_ref, own, other, diag, out):
     half = own.shape[0]
-    core = lax.rem(info_ref[0], 2)
-    for ref, which in ((own, core), (other, 1 - core)):
-        here = pl.ds(pl.multiple_of(which * half, 8), half)
-        out[here, :] = ref[...] / diag[here, :]
+    odd = jnp.broadcast_to(odd_ref[0:1, :] > 0, own.shape)
+    out[:half, :] = jnp.where(odd, other[...], own[...]) / diag[:half, :]
+    out[half:, :] = jnp.where(odd, own[...], other[...]) / diag[half:, :]
 
 
 def row_kernel(scaling_ref, col_ref, out_ref):
@@ -215,7 +222,7 @@
     lax.fori_loop(0, rows // BLOCK, step, 0)
 
 
-def col_kernel(info_ref, scaling_ref, row_ref, _, keep_ref, send_ref, out_ref):
+def col_kernel(odd_ref, scaling_ref, row_ref, _, keep_ref, send_ref, out_ref):
     rows, inds, _ = scaling_ref.shape
     out_ref[...] = jnp.zeros_like(out_ref)
 
@@ -227,7 +234,7 @@
         return 0
 
     lax.fori_loop(0, rows // BLOCK, step, 0)
-    split_halves(out_ref, keep_ref, send_ref, lax.rem(info_ref[0], 2))
+    split_halves(out_ref, keep_ref, send_ref, odd_ref)
 
 
 def products_kernel(iters, nreg, nind, scaling_ref, row_diag_ref, col_diag_ref, *rest):
@@ -314,8 +321,9 @@
             cell = turned(cell.astype(jnp.bfloat16))
             cell_ref[:, r] = cell.astype(jnp.bfloat16).reshape(probs, sizes, inds)
 
+    deep = pl.Buffered(4)
     cells = pl.BlockSpec((probs, BLOCK, sizes, inds), lambda b: (0, b, 0, 0))
-    turned_cells = pl.BlockSpec((BLOCK, inds, LANES), lambda b: (b, 0, 0))
+    turned_cells = pl.BlockSpec((BLOCK, inds, LANES), lambda b: (b, 0, 0), pipeline_mode=deep)
     pltpu.emit_pipeline(body, grid=(rows // BLOCK,), in_specs=[turned_cells], out_specs=[cells])(
         barrier_hbm, cell_hbm
     )
@@ -332,12 +340,12 @@
     return [x] + [lax.ppermute(x, axis, [(j, j ^ flip) for j in range(count)]) for flip in flips[1:]]
 
 
-def vmem_call(kernel, outs, name, scratch=(), cost=None, scalars=0):
+def vmem_call(kernel, outs, name, scratch=(), cost=None):
     def call(*args):
         return pl.pallas_call(
             kernel,
             out_shape=outs,
-            in_specs=[SMEM_SPEC] * scalars + [VMEM_SPEC] * (len(args) - scalars),
+            in_specs=[VMEM_SPEC] * len(args),
             out_specs=[VMEM_SPEC] * len(outs),
             scratch_shapes=list(scratch),
             compiler_params=params(),
@@ -377,8 +385,8 @@
 ):
     probs, rows, sizes, inds = position.shape
     my_reg, my_ind = lax.axis_index("region"), lax.axis_index("industry")
-    info = jnp.concatenate([jnp.stack([my_reg, my_ind]).astype(jnp.int32), attack_region])
-    attack = jnp.repeat(jnp.stack([attack_region, attack_column]), sizes, axis=1)
+    info = jnp.concatenate([jnp.stack([my_reg, my_ind]).astype(jnp.int32), attack_region, attack_column])
+    odd = jnp.broadcast_to(lax.rem(my_reg, 2).astype(F32), (8, LANES))
     drow = dual_row.transpose(0, 2, 1).reshape(LANES, rows)
     dcol = dual_col.reshape(LANES, inds)
     half = inds // 2
@@ -411,7 +419,7 @@
         ],
         compiler_params=params(),
         name="prepare",
-    )(info, attack, position, dual_lower, dual_upper, upper_bound, suppressed, drow, dcol)
+    )(info, odd, position, dual_lower, dual_upper, upper_bound, suppressed, drow, dcol)
     scaling = keep(scaling)
     barrier = in_hbm(barrier)
     cells = rows * inds * LANES
@@ -420,19 +428,19 @@
     row_parts = row_sum(row_both, nind)
     col_halves = col_sum(col_keep, col_send, nreg)
     kernel = functools.partial(begin_kernel, len(row_parts))
-    row_diag, col_diag, row_now, col_now = vmem_call(kernel, margins * 2, "begin", scalars=1)(
-        info, *row_parts, *col_halves
+    row_diag, col_diag, row_now, col_now = vmem_call(kernel, margins * 2, "begin")(
+        odd, *row_parts, *col_halves
     )
     row_p, col_p = [row_now], [col_now]
     for _ in range(3 * iters - 1):
         (row_out,) = vmem_call(row_kernel, margins[:1], "row_sweep", cost=cost)(scaling, col_p[-1])
         col_keep, col_send = vmem_call(
-            col_kernel, [shape(half, LANES)] * 2, "col_sweep", [pltpu.VMEM((inds, LANES), F32)], cost, 1
-        )(info, scaling, row_p[-1], row_out)
+            col_kernel, [shape(half, LANES)] * 2, "col_sweep", [pltpu.VMEM((inds, LANES), F32)], cost
+        )(odd, scaling, row_p[-1], row_out)
         row_parts = row_sum(row_out, nind)
         col_halves = col_sum(col_keep, col_send, nreg)
         row_p += vmem_call(row_end_kernel, margins[:1], "row_end")(*row_parts, row_diag)
-        col_p += vmem_call(join_halves, margins[1:], "col_end", scalars=1)(info, *col_halves, col_diag)
+        col_p += vmem_call(join_halves, margins[1:], "col_end")(odd, *col_halves, col_diag)
     kernel = functools.partial(products_kernel, iters, nreg, nind)
     scratch = [pltpu.VMEM((rows, LANES), F32), pltpu.VMEM((inds, LANES), F32)]
     (part,) = vmem_call(kernel, [shape(16, LANES)], "products", scratch)(

time: 236 us -> 219 us (0.928)
  Pallas kernels: 112 us -> 93.8 us
  waiting for transfers between devices: 50.3 us -> 53 us
    pallas_call x63, Pallas kernels: 45.1 us -> 35.9 us  [call(): pl.pallas_call(kernel, out_shape=outs, in_specs=[VMEM_SPEC] * len(args),...]
    pallas_call x1, Pallas kernels: 24.3 us -> 16.3 us  [local(): pl.pallas_call(functools.partial(finish_kernel, rows, sizes, inds, probs,...]
    ppermute x70, waiting for transfers between devices: 50.3 us -> 53 us  [exchange(): lax.ppermute(x, axis, [(j, j ^ flip) for j in range(count)])]
  transfers between devices with their start and end apart: 70 -> 70, of which waited for: 49 -> 57; matrix products, arithmetic and copies ran while one was open for 0% -> 0% of each run, Pallas kernels for 8% -> 7%
where the time goes in v5:
time: 219 us; the launch traced here: 218 us
  Pallas kernels  93.8 us (43%)
  starting transfers between devices  67.4 us (31%)
  waiting for transfers between devices  53 us (24%)
    ppermute x70, starting transfers between devices, exchange(): lax.ppermute(x, axis, [(j, j ^ flip) for j in range(count)])  67.4 us
    ppermute x70, waiting for transfers between devices, exchange(): lax.ppermute(x, axis, [(j, j ^ flip) for j in range(count)])  53 us
    pallas_call x1, Pallas kernels, local(): pl.pallas_call(functools.partial(prepare_kernel, rows, sizes, inds, probs...  41.6 us
    pallas_call x63, Pallas kernels, call(): pl.pallas_call(kernel, out_shape=outs, in_specs=[VMEM_SPEC] * len(args),...  35.9 us
    pallas_call x1, Pallas kernels, local(): pl.pallas_call(functools.partial(finish_kernel, rows, sizes, inds, probs,...  16.3 us
  transfers between devices with their start and end apart: 70, of which 57 were waited for; matrix products, arithmetic and copies ran while one was open for 0% of the time, Pallas kernels for 7%

profile of v5, /device:TPU:0, one launch (start us, length us, event | category | flops | bytes accessed | tf_op | source)
XLA Modules:
  0.0 217.8 jit_solution(15075754249836934250)
XLA Ops:
  3.2 41.6 %prepare.1 = (f32[192,256,128]{2,1,0:T(8,128)S(1)}, f32[192,256,128]{2,1,0:T(8,128)}, f32[2,192,128]{2,1,0:T(8,128)S(1)}, f32[2,128,128]{2,1,0:T(8,128)S(1)}, f32[2,128,128]{2,1,0:T(8,128)S(1)}) custom-call(s32[18]{0:T(128)S(1)} %pad_add_fusion.info_ref, f32[8,128]{1,0:T(8,128)S(1)} %broadcast_in_dim.3.odd_ref, bf16[8,192,16,256]{3,2,1,0:T(8,128)(2,1)} %pos_hbm.1, ...), custom_call_target="tpu_custom_call" | custom-call | tf_op jit(solution)/shard_map/prepare/pallas_call | solution.py:402
  44.9 3.1 %collective-permute-start = (f32[2,192,128]{2,1,0:T(8,128)S(1)}, f32[2,192,128]{2,1,0:T(8,128)S(1)}, u32[]{:S(2)}, u32[]{:S(2)}) collective-permute-start(f32[2,192,128]{2,1,0:T(8,128)S(1)} %get-tuple-element.33.refs_0_), channel_id=1, source_target_pairs={{0,1},{1,0},{2,3},{3,2},{4,5},{5,4},{6,7},{7,6},{8,9},{9,8},{10,11... | collective-permute-start | bytes 589832 | tf_op jit(solution)/shard_map/ppermute | solution.py:340
  51.6 1.9 collective-permute-done.refs_1_
  53.5 2.8 %collective-permute-start.1 = (f32[2,192,128]{2,1,0:T(8,128)S(1)}, f32[2,192,128]{2,1,0:T(8,128)S(1)}, u32[]{:S(2)}, u32[]{:S(2)}) collective-permute-start(f32[2,192,128]{2,1,0:T(8,128)S(1)} %join.29.refs_0_), channel_id=1, source_target_pairs={{0,2},{1,3},{2,0},{3,1},{4,6},{5,7},{6,4},{7,5},{8,10},{9,11},{10,... | collective-permute-start | bytes 589832 | tf_op jit(solution)/shard_map/ppermute | solution.py:340
  58.9 6.4 %collective-permute-done.1.refs_1_ = f32[2,192,128]{2,1,0:T(8,128)S(1)} collective-permute-done((f32[2,192,128]{2,1,0:T(8,128)S(1)}, f32[2,192,128]{2,1,0:T(8,128)S(1)}, u32[]{:S(2)}, u32[]{:S(2)}) %collective-permute-start.1) | collective-permute-done | bytes 196640 | tf_op jit(solution)/shard_map/ppermute | solution.py:340
  65.4 1.9 row_sweep.8.refs_0_._
  67.3 2.0 col_sweep.8
  74.6 2.5 %collective-permute-start.8 = (f32[192,128]{1,0:T(8,128)S(1)}, f32[192,128]{1,0:T(8,128)S(1)}, u32[]{:S(2)}, u32[]{:S(2)}) collective-permute-start(f32[192,128]{1,0:T(8,128)S(1)} %join.32.refs_0_), channel_id=1, source_target_pairs={{0,2},{1,3},{2,0},{3,1},{4,6},{5,7},{6,4},{7,5},{8,10},{9,11},{10,... | collective-permute-start | bytes 294920 | tf_op jit(solution)/shard_map/ppermute | solution.py:340
  78.6 2.1 row_sweep.9.refs_0_._
  82.0 2.0 col_sweep.9
  89.3 2.4 %collective-permute-start.15 = (f32[192,128]{1,0:T(8,128)S(1)}, f32[192,128]{1,0:T(8,128)S(1)}, u32[]{:S(2)}, u32[]{:S(2)}) collective-permute-start(f32[192,128]{1,0:T(8,128)S(1)} %join.35.refs_0_), channel_id=1, source_target_pairs={{0,2},{1,3},{2,0},{3,1},{4,6},{5,7},{6,4},{7,5},{8,10},{9,11},{10,... | collective-permute-start | bytes 294920 | tf_op jit(solution)/shard_map/ppermute | solution.py:340
  93.3 2.1 row_sweep.10.refs_0_._
  96.7 2.0 col_sweep.10
  104.0 2.3 %collective-permute-start.22 = (f32[192,128]{1,0:T(8,128)S(1)}, f32[192,128]{1,0:T(8,128)S(1)}, u32[]{:S(2)}, u32[]{:S(2)}) collective-permute-start(f32[192,128]{1,0:T(8,128)S(1)} %join.38.refs_0_), channel_id=1, source_target_pairs={{0,2},{1,3},{2,0},{3,1},{4,6},{5,7},{6,4},{7,5},{8,10},{9,11},{10,... | collective-permute-start | bytes 294920 | tf_op jit(solution)/shard_map/ppermute | solution.py:340
  108.0 2.1 row_sweep.11.refs_0_._
  111.5 2.0 col_sweep.11
  118.7 2.2 %collective-permute-start.29 = (f32[192,128]{1,0:T(8,128)S(1)}, f32[192,128]{1,0:T(8,128)S(1)}, u32[]{:S(2)}, u32[]{:S(2)}) collective-permute-start(f32[192,128]{1,0:T(8,128)S(1)} %join.41.refs_0_), channel_id=1, source_target_pairs={{0,2},{1,3},{2,0},{3,1},{4,6},{5,7},{6,4},{7,5},{8,10},{9,11},{10,... | collective-permute-start | bytes 294920 | tf_op jit(solution)/shard_map/ppermute | solution.py:340
  122.7 2.1 row_sweep.12.refs_0_._
  126.2 2.0 col_sweep.12
  133.5 2.1 collective-permute-start.36
  137.5 2.1 row_sweep.13.refs_0_._
  140.9 2.0 col_sweep.13
  148.2 2.0 collective-permute-start.43
  152.2 2.1 row_sweep.14.refs_0_._
  155.7 2.0 col_sweep.14
  162.9 1.9 collective-permute-start.50
  166.9 2.1 row_sweep.15.refs_0_._
  170.4 2.0 col_sweep.15
  180.4 4.7 %collective-permute-done.57.refs_1_ = f32[192,128]{1,0:T(8,128)S(1)} collective-permute-done((f32[192,128]{1,0:T(8,128)S(1)}, f32[192,128]{1,0:T(8,128)S(1)}, u32[]{:S(2)}, u32[]{:S(2)}) %collective-permute-start.57) | collective-permute-done | bytes 98336 | tf_op jit(solution)/shard_map/ppermute | solution.py:340
  185.2 2.4 %products.1.refs_0_ = f32[16,128]{1,0:T(8,128)S(1)} custom-call(f32[192,256,128]{2,1,0:T(8,128)S(1)} %get-tuple-element.31.scaling_ref, f32[192,128]{1,0:T(8,128)S(1)} %get-tuple-element.36.refs_2_.row_diag_ref, f32[256,128]{1,0:T(8,128)S(1)} %get-tuple-element.37.diag.col_diag_ref, f32[192,128]{1,0:T(8,128)S(1)} %get-tuple-element.38.row_ref.rest_0_.rest_4_, ...), custom_call_target="tpu_custom_call" | custom-call | tf_op jit(solution)/shard_map/products/pallas_call | solution.py:345
  194.3 2.6 %collective-permute-start.69 = (f32[16,128]{1,0:T(8,128)S(1)}, f32[16,128]{1,0:T(8,128)S(1)}, u32[]{:S(2)}, u32[]{:S(2)}) collective-permute-start(f32[16,128]{1,0:T(8,128)S(1)} %join.57.rest_0_), channel_id=1, source_target_pairs={{0,3},{1,2},{2,1},{3,0},{4,7},{5,6},{6,5},{7,4},{8,11},{9,10},{10,... | collective-permute-start | bytes 24584 | tf_op jit(solution)/shard_map/ppermute | solution.py:340
  201.5 16.3 %finish.1 = (bf16[8,192,16,256]{3,2,1,0:T(8,128)(2,1)}, f32[128,192]{1,0:T(8,128)}, f32[128,256]{1,0:T(8,128)}) custom-call(f32[192,256,128]{2,1,0:T(8,128)S(1)} %get-tuple-element.31.scaling_ref, f32[192,256,128]{2,1,0:T(8,128)} %get-tuple-element.32.barrier_hbm, f32[128,192]{1,0:T(8,128)S(1)} %bitcast.11, f32[128,256]{1,0:T(8,128)S(1)} %bitcast.13, ...), custom_call_target="tpu_custom_call" | custom-call | tf_op jit(solution)/shard_map/finish/pallas_call | solution.py:457
  (181 shorter events, 86.7 us)
Async XLA Ops:
  44.9 8.6 %collective-permute-start = (f32[2,192,128]{2,1,0:T(8,128)S(1)}, f32[2,192,128]{2,1,0:T(8,128)S(1)}, u32[]{:S(2)}, u32[]{:S(2)}) collective-permute-start(f32[2,192,128]{2,1,0:T(8,128)S(1)} %get-tuple-element.33.refs_0_), channel_id=1, source_target_pairs={{0,1},{1,0},{2,3},{3,2},{4,5},{5,4},{6,7},{7,6},{8,9},{9,8},{10,11... | collective-permute-start | bytes 589832 | tf_op jit(solution)/shard_map/ppermute | solution.py:340
  48.0 8.3 %collective-permute-start.5 = (f32[2,128,128]{2,1,0:T(8,128)S(1)}, f32[2,128,128]{2,1,0:T(8,128)S(1)}, u32[]{:S(2)}, u32[]{:S(2)}) collective-permute-start(f32[2,128,128]{2,1,0:T(8,128)S(1)} %join.30.refs_0_), channel_id=1, source_target_pairs={{0,24},{4,28},{8,16},{12,20},{16,8},{20,12},{24,0},{28,4},{1,25},{... | collective-permute-start | bytes 393224 | tf_op jit(solution)/shard_map/ppermute | solution.py:340
  49.4 8.0 %collective-permute-start.4 = (f32[2,128,128]{2,1,0:T(8,128)S(1)}, f32[2,128,128]{2,1,0:T(8,128)S(1)}, u32[]{:S(2)}, u32[]{:S(2)}) collective-permute-start(f32[2,128,128]{2,1,0:T(8,128)S(1)} %join.30.refs_0_), channel_id=1, source_target_pairs={{0,16},{4,20},{8,24},{12,28},{16,0},{20,4},{24,8},{28,12},{1,17},{... | collective-permute-start | bytes 393224 | tf_op jit(solution)/shard_map/ppermute | solution.py:340
  49.9 7.6 %collective-permute-start.3 = (f32[2,128,128]{2,1,0:T(8,128)S(1)}, f32[2,128,128]{2,1,0:T(8,128)S(1)}, u32[]{:S(2)}, u32[]{:S(2)}) collective-permute-start(f32[2,128,128]{2,1,0:T(8,128)S(1)} %join.30.refs_0_), channel_id=1, source_target_pairs={{0,8},{4,12},{8,0},{12,4},{16,24},{20,28},{24,16},{28,20},{1,9},{5... | collective-permute-start | bytes 393224 | tf_op jit(solution)/shard_map/ppermute | solution.py:340
  53.5 11.8 %collective-permute-start.1 = (f32[2,192,128]{2,1,0:T(8,128)S(1)}, f32[2,192,128]{2,1,0:T(8,128)S(1)}, u32[]{:S(2)}, u32[]{:S(2)}) collective-permute-start(f32[2,192,128]{2,1,0:T(8,128)S(1)} %join.29.refs_0_), channel_id=1, source_target_pairs={{0,2},{1,3},{2,0},{3,1},{4,6},{5,7},{6,4},{7,5},{8,10},{9,11},{10,... | collective-permute-start | bytes 589832 | tf_op jit(solution)/shard_map/ppermute | solution.py:340
  69.3 5.2 %collective-permute-start.7 = (f32[192,128]{1,0:T(8,128)S(1)}, f32[192,128]{1,0:T(8,128)S(1)}, u32[]{:S(2)}, u32[]{:S(2)}) collective-permute-start(f32[192,128]{1,0:T(8,128)S(1)} %row_sweep.8.refs_0_._), channel_id=1, source_target_pairs={{0,1},{1,0},{2,3},{3,2},{4,5},{5,4},{6,7},{7,6},{8,9},{9,8},{10,11... | collective-permute-start | bytes 294920 | tf_op jit(solution)/shard_map/ppermute | solution.py:340
  70.6 6.5 %collective-permute-start.12 = (f32[128,128]{1,0:T(8,128)S(1)}, f32[128,128]{1,0:T(8,128)S(1)}, u32[]{:S(2)}, u32[]{:S(2)}) collective-permute-start(f32[128,128]{1,0:T(8,128)S(1)} %join.33.refs_0_), channel_id=1, source_target_pairs={{0,24},{4,28},{8,16},{12,20},{16,8},{20,12},{24,0},{28,4},{1,25},{... | collective-permute-start | bytes 196616 | tf_op jit(solution)/shard_map/ppermute | solution.py:340
  74.6 7.4 %collective-permute-start.8 = (f32[192,128]{1,0:T(8,128)S(1)}, f32[192,128]{1,0:T(8,128)S(1)}, u32[]{:S(2)}, u32[]{:S(2)}) collective-permute-start(f32[192,128]{1,0:T(8,128)S(1)} %join.32.refs_0_), channel_id=1, source_target_pairs={{0,2},{1,3},{2,0},{3,1},{4,6},{5,7},{6,4},{7,5},{8,10},{9,11},{10,... | collective-permute-start | bytes 294920 | tf_op jit(solution)/shard_map/ppermute | solution.py:340
  84.1 5.2 %collective-permute-start.14 = (f32[192,128]{1,0:T(8,128)S(1)}, f32[192,128]{1,0:T(8,128)S(1)}, u32[]{:S(2)}, u32[]{:S(2)}) collective-permute-start(f32[192,128]{1,0:T(8,128)S(1)} %row_sweep.9.refs_0_._), channel_id=1, source_target_pairs={{0,1},{1,0},{2,3},{3,2},{4,5},{5,4},{6,7},{7,6},{8,9},{9,8},{10,11... | collective-permute-start | bytes 294920 | tf_op jit(solution)/shard_map/ppermute | solution.py:340
  85.3 6.4 %collective-permute-start.19 = (f32[128,128]{1,0:T(8,128)S(1)}, f32[128,128]{1,0:T(8,128)S(1)}, u32[]{:S(2)}, u32[]{:S(2)}) collective-permute-start(f32[128,128]{1,0:T(8,128)S(1)} %join.36.refs_0_), channel_id=1, source_target_pairs={{0,24},{4,28},{8,16},{12,20},{16,8},{20,12},{24,0},{28,4},{1,25},{... | collective-permute-start | bytes 196616 | tf_op jit(solution)/shard_map/ppermute | solution.py:340
  89.3 7.4 %collective-permute-start.15 = (f32[192,128]{1,0:T(8,128)S(1)}, f32[192,128]{1,0:T(8,128)S(1)}, u32[]{:S(2)}, u32[]{:S(2)}) collective-permute-start(f32[192,128]{1,0:T(8,128)S(1)} %join.35.refs_0_), channel_id=1, source_target_pairs={{0,2},{1,3},{2,0},{3,1},{4,6},{5,7},{6,4},{7,5},{8,10},{9,11},{10,... | collective-permute-start | bytes 294920 | tf_op jit(solution)/shard_map/ppermute | solution.py:340
  98.8 5.2 %collective-permute-start.21 = (f32[192,128]{1,0:T(8,128)S(1)}, f32[192,128]{1,0:T(8,128)S(1)}, u32[]{:S(2)}, u32[]{:S(2)}) collective-permute-start(f32[192,128]{1,0:T(8,128)S(1)} %row_sweep.10.refs_0_._), channel_id=1, source_target_pairs={{0,1},{1,0},{2,3},{3,2},{4,5},{5,4},{6,7},{7,6},{8,9},{9,8},{10,11... | collective-permute-start | bytes 294920 | tf_op jit(solution)/shard_map/ppermute | solution.py:340
  100.0 6.3 %collective-permute-start.26 = (f32[128,128]{1,0:T(8,128)S(1)}, f32[128,128]{1,0:T(8,128)S(1)}, u32[]{:S(2)}, u32[]{:S(2)}) collective-permute-start(f32[128,128]{1,0:T(8,128)S(1)} %join.39.refs_0_), channel_id=1, source_target_pairs={{0,24},{4,28},{8,16},{12,20},{16,8},{20,12},{24,0},{28,4},{1,25},{... | collective-permute-start | bytes 196616 | tf_op jit(solution)/shard_map/ppermute | solution.py:340
  104.0 7.4 %collective-permute-start.22 = (f32[192,128]{1,0:T(8,128)S(1)}, f32[192,128]{1,0:T(8,128)S(1)}, u32[]{:S(2)}, u32[]{:S(2)}) collective-permute-start(f32[192,128]{1,0:T(8,128)S(1)} %join.38.refs_0_), channel_id=1, source_target_pairs={{0,2},{1,3},{2,0},{3,1},{4,6},{5,7},{6,4},{7,5},{8,10},{9,11},{10,... | collective-permute-start | bytes 294920 | tf_op jit(solution)/shard_map/ppermute | solution.py:340
  113.5 5.2 %collective-permute-start.28 = (f32[192,128]{1,0:T(8,128)S(1)}, f32[192,128]{1,0:T(8,128)S(1)}, u32[]{:S(2)}, u32[]{:S(2)}) collective-permute-start(f32[192,128]{1,0:T(8,128)S(1)} %row_sweep.11.refs_0_._), channel_id=1, source_target_pairs={{0,1},{1,0},{2,3},{3,2},{4,5},{5,4},{6,7},{7,6},{8,9},{9,8},{10,11... | collective-permute-start | bytes 294920 | tf_op jit(solution)/shard_map/ppermute | solution.py:340
  114.8 6.2 %collective-permute-start.33 = (f32[128,128]{1,0:T(8,128)S(1)}, f32[128,128]{1,0:T(8,128)S(1)}, u32[]{:S(2)}, u32[]{:S(2)}) collective-permute-start(f32[128,128]{1,0:T(8,128)S(1)} %join.42.refs_0_), channel_id=1, source_target_pairs={{0,24},{4,28},{8,16},{12,20},{16,8},{20,12},{24,0},{28,4},{1,25},{... | collective-permute-start | bytes 196616 | tf_op jit(solution)/shard_map/ppermute | solution.py:340
  116.2 5.1 %collective-permute-start.32 = (f32[128,128]{1,0:T(8,128)S(1)}, f32[128,128]{1,0:T(8,128)S(1)}, u32[]{:S(2)}, u32[]{:S(2)}) collective-permute-start(f32[128,128]{1,0:T(8,128)S(1)} %join.42.refs_0_), channel_id=1, source_target_pairs={{0,16},{4,20},{8,24},{12,28},{16,0},{20,4},{24,8},{28,12},{1,17},{... | collective-permute-start | bytes 196616 | tf_op jit(solution)/shard_map/ppermute | solution.py:340
  118.7 7.4 %collective-permute-start.29 = (f32[192,128]{1,0:T(8,128)S(1)}, f32[192,128]{1,0:T(8,128)S(1)}, u32[]{:S(2)}, u32[]{:S(2)}) collective-permute-start(f32[192,128]{1,0:T(8,128)S(1)} %join.41.refs_0_), channel_id=1, source_target_pairs={{0,2},{1,3},{2,0},{3,1},{4,6},{5,7},{6,4},{7,5},{8,10},{9,11},{10,... | collective-permute-start | bytes 294920 | tf_op jit(solution)/shard_map/ppermute | solution.py:340
  128.2 5.2 %collective-permute-start.35 = (f32[192,128]{1,0:T(8,128)S(1)}, f32[192,128]{1,0:T(8,128)S(1)}, u32[]{:S(2)}, u32[]{:S(2)}) collective-permute-start(f32[192,128]{1,0:T(8,128)S(1)} %row_sweep.12.refs_0_._), channel_id=1, source_target_pairs={{0,1},{1,0},{2,3},{3,2},{4,5},{5,4},{6,7},{7,6},{8,9},{9,8},{10,11... | collective-permute-start | bytes 294920 | tf_op jit(solution)/shard_map/ppermute | solution.py:340
  129.5 6.1 %collective-permute-start.40 = (f32[128,128]{1,0:T(8,128)S(1)}, f32[128,128]{1,0:T(8,128)S(1)}, u32[]{:S(2)}, u32[]{:S(2)}) collective-permute-start(f32[128,128]{1,0:T(8,128)S(1)} %join.45.refs_0_), channel_id=1, source_target_pairs={{0,24},{4,28},{8,16},{12,20},{16,8},{20,12},{24,0},{28,4},{1,25},{... | collective-permute-start | bytes 196616 | tf_op jit(solution)/shard_map/ppermute | solution.py:340
  130.9 5.1 %collective-permute-start.39 = (f32[128,128]{1,0:T(8,128)S(1)}, f32[128,128]{1,0:T(8,128)S(1)}, u32[]{:S(2)}, u32[]{:S(2)}) collective-permute-start(f32[128,128]{1,0:T(8,128)S(1)} %join.45.refs_0_), channel_id=1, source_target_pairs={{0,16},{4,20},{8,24},{12,28},{16,0},{20,4},{24,8},{28,12},{1,17},{... | collective-permute-start | bytes 196616 | tf_op jit(solution)/shard_map/ppermute | solution.py:340
  133.5 7.4 %collective-permute-start.36 = (f32[192,128]{1,0:T(8,128)S(1)}, f32[192,128]{1,0:T(8,128)S(1)}, u32[]{:S(2)}, u32[]{:S(2)}) collective-permute-start(f32[192,128]{1,0:T(8,128)S(1)} %join.44.refs_0_), channel_id=1, source_target_pairs={{0,2},{1,3},{2,0},{3,1},{4,6},{5,7},{6,4},{7,5},{8,10},{9,11},{10,... | collective-permute-start | bytes 294920 | tf_op jit(solution)/shard_map/ppermute | solution.py:340
  143.0 5.2 %collective-permute-start.42 = (f32[192,128]{1,0:T(8,128)S(1)}, f32[192,128]{1,0:T(8,128)S(1)}, u32[]{:S(2)}, u32[]{:S(2)}) collective-permute-start(f32[192,128]{1,0:T(8,128)S(1)} %row_sweep.13.refs_0_._), channel_id=1, source_target_pairs={{0,1},{1,0},{2,3},{3,2},{4,5},{5,4},{6,7},{7,6},{8,9},{9,8},{10,11... | collective-permute-start | bytes 294920 | tf_op jit(solution)/shard_map/ppermute | solution.py:340
  144.2 6.0 %collective-permute-start.47 = (f32[128,128]{1,0:T(8,128)S(1)}, f32[128,128]{1,0:T(8,128)S(1)}, u32[]{:S(2)}, u32[]{:S(2)}) collective-permute-start(f32[128,128]{1,0:T(8,128)S(1)} %join.48.refs_0_), channel_id=1, source_target_pairs={{0,24},{4,28},{8,16},{12,20},{16,8},{20,12},{24,0},{28,4},{1,25},{... | collective-permute-start | bytes 196616 | tf_op jit(solution)/shard_map/ppermute | solution.py:340
  148.2 7.4 %collective-permute-start.43 = (f32[192,128]{1,0:T(8,128)S(1)}, f32[192,128]{1,0:T(8,128)S(1)}, u32[]{:S(2)}, u32[]{:S(2)}) collective-permute-start(f32[192,128]{1,0:T(8,128)S(1)} %join.47.refs_0_), channel_id=1, source_target_pairs={{0,2},{1,3},{2,0},{3,1},{4,6},{5,7},{6,4},{7,5},{8,10},{9,11},{10,... | collective-permute-start | bytes 294920 | tf_op jit(solution)/shard_map/ppermute | solution.py:340
  157.7 5.2 %collective-permute-start.49 = (f32[192,128]{1,0:T(8,128)S(1)}, f32[192,128]{1,0:T(8,128)S(1)}, u32[]{:S(2)}, u32[]{:S(2)}) collective-permute-start(f32[192,128]{1,0:T(8,128)S(1)} %row_sweep.14.refs_0_._), channel_id=1, source_target_pairs={{0,1},{1,0},{2,3},{3,2},{4,5},{5,4},{6,7},{7,6},{8,9},{9,8},{10,11... | collective-permute-start | bytes 294920 | tf_op jit(solution)/shard_map/ppermute | solution.py:340
  158.9 5.9 %collective-permute-start.54 = (f32[128,128]{1,0:T(8,128)S(1)}, f32[128,128]{1,0:T(8,128)S(1)}, u32[]{:S(2)}, u32[]{:S(2)}) collective-permute-start(f32[128,128]{1,0:T(8,128)S(1)} %join.51.refs_0_), channel_id=1, source_target_pairs={{0,24},{4,28},{8,16},{12,20},{16,8},{20,12},{24,0},{28,4},{1,25},{... | collective-permute-start | bytes 196616 | tf_op jit(solution)/shard_map/ppermute | solution.py:340
  162.9 7.4 %collective-permute-start.50 = (f32[192,128]{1,0:T(8,128)S(1)}, f32[192,128]{1,0:T(8,128)S(1)}, u32[]{:S(2)}, u32[]{:S(2)}) collective-permute-start(f32[192,128]{1,0:T(8,128)S(1)} %join.50.refs_0_), channel_id=1, source_target_pairs={{0,2},{1,3},{2,0},{3,1},{4,6},{5,7},{6,4},{7,5},{8,10},{9,11},{10,... | collective-permute-start | bytes 294920 | tf_op jit(solution)/shard_map/ppermute | solution.py:340
  172.4 5.2 %collective-permute-start.56 = (f32[192,128]{1,0:T(8,128)S(1)}, f32[192,128]{1,0:T(8,128)S(1)}, u32[]{:S(2)}, u32[]{:S(2)}) collective-permute-start(f32[192,128]{1,0:T(8,128)S(1)} %row_sweep.15.refs_0_._), channel_id=1, source_target_pairs={{0,1},{1,0},{2,3},{3,2},{4,5},{5,4},{6,7},{7,6},{8,9},{9,8},{10,11... | collective-permute-start | bytes 294920 | tf_op jit(solution)/shard_map/ppermute | solution.py:340
  173.7 5.8 %collective-permute-start.61 = (f32[128,128]{1,0:T(8,128)S(1)}, f32[128,128]{1,0:T(8,128)S(1)}, u32[]{:S(2)}, u32[]{:S(2)}) collective-permute-start(f32[128,128]{1,0:T(8,128)S(1)} %join.54.refs_0_), channel_id=1, source_target_pairs={{0,24},{4,28},{8,16},{12,20},{16,8},{20,12},{24,0},{28,4},{1,25},{... | collective-permute-start | bytes 196616 | tf_op jit(solution)/shard_map/ppermute | solution.py:340
  177.6 7.4 %collective-permute-start.57 = (f32[192,128]{1,0:T(8,128)S(1)}, f32[192,128]{1,0:T(8,128)S(1)}, u32[]{:S(2)}, u32[]{:S(2)}) collective-permute-start(f32[192,128]{1,0:T(8,128)S(1)} %join.53.refs_0_), channel_id=1, source_target_pairs={{0,2},{1,3},{2,0},{3,1},{4,6},{5,7},{6,4},{7,5},{8,10},{9,11},{10,... | collective-permute-start | bytes 294920 | tf_op jit(solution)/shard_map/ppermute | solution.py:340
  194.3 5.4 %collective-permute-start.69 = (f32[16,128]{1,0:T(8,128)S(1)}, f32[16,128]{1,0:T(8,128)S(1)}, u32[]{:S(2)}, u32[]{:S(2)}) collective-permute-start(f32[16,128]{1,0:T(8,128)S(1)} %join.57.rest_0_), channel_id=1, source_target_pairs={{0,3},{1,2},{2,1},{3,0},{4,7},{5,6},{6,5},{7,4},{8,11},{9,10},{10,... | collective-permute-start | bytes 24584 | tf_op jit(solution)/shard_map/ppermute | solution.py:340
  (41 other events, 138.1 us)

commit v6 on v5

--- a/solution.py
+++ b/solution.py
@@ -9,7 +9,9 @@
 
 WEIGHT_ATTACK = 8.0
 SHIFT_DIAG = 1.0
+SUPPRESSED = 64
 BLOCK = 8
+ARRAYS = 4
 LANES = 128
 VMEM_MIB = 12
 VMEM_SPEC = pl.BlockSpec(memory_space=pltpu.VMEM)
@@ -78,18 +80,17 @@
     def body(pos_ref, low_ref, high_ref, upper_ref, supp_ref, barrier_ref):
         r0 = pl.multiple_of(pl.program_id(0) * BLOCK, BLOCK)
 
-        def bring(pair, slot):
-            for j, ref in enumerate((pos_ref, low_ref, high_ref)):
-                both = [ref[:, 2 * pair + r].reshape(LANES, inds) for r in range(2)]
-                slot[j] = turned(jnp.concatenate(both, axis=0))
-            for j, ref in enumerate((upper_ref, supp_ref)):
-                both = []
-                for r in range(2):
-                    one = ref[2 * pair + r].astype(F32).astype(jnp.bfloat16)
-                    both += [one] * probs
-                slot[3 + j] = turned(jnp.concatenate(both, axis=0))
-
-        def work(pair, slot, attacked):
+        def bring(pair, slot, j):
+            both = []
+            for r in range(2):
+                if j < 3:
+                    both += [(pos_ref, low_ref, high_ref)[j][:, 2 * pair + r].reshape(LANES, inds)]
+                else:
+                    coded = upper_ref[2 * pair + r] + SUPPRESSED * supp_ref[2 * pair + r]
+                    both += [coded.astype(F32).astype(jnp.bfloat16)] * probs
+            slot[j] = turned(jnp.concatenate(both, axis=0))
+
+        def work(pair, slot, attacked, next_slot=None):
             rhs_acc = [jnp.zeros((8, LANES), F32)] * 2
             sum_acc = [jnp.zeros((8, LANES), F32)] * 2
             drow = [
@@ -97,12 +98,16 @@
             ]
             for i0 in range(0, inds, 8):
                 here = slice(i0, i0 + 8)
+                if next_slot is not None and i0 * ARRAYS // inds != (i0 - 8) * ARRAYS // inds:
+                    bring(pair + 1, next_slot, i0 * ARRAYS // inds)
                 dcol = dcol_t[here, :]
                 col_rhs = col_sum_part = None
                 for r in range(2):
                     lanes = slice(r * LANES, (r + 1) * LANES)
-                    upper = slot[3, here, lanes]
-                    active = slot[4, here, lanes]
+                    coded = slot[3, here, lanes]
+                    suppressed = coded >= SUPPRESSED
+                    upper = jnp.where(suppressed, coded - SUPPRESSED, coded)
+                    active = jnp.where(suppressed, jnp.ones_like(coded), jnp.zeros_like(coded))
                     if attacked:
                         lane = lax.broadcasted_iota(jnp.int32, (8, LANES), 1)
                         column = lax.rem(lane, sizes) * (inds * nind) + first_ind + i0
@@ -143,16 +148,16 @@
         @pl.when(hits == 0)
         def _():
             slots = (first_s, second_s)
-            bring(0, slots[0])
+            for j in range(ARRAYS):
+                bring(0, slots[0], j)
             for pair in range(pairs):
-                if pair + 1 < pairs:
-                    bring(pair + 1, slots[(pair + 1) % 2])
-                work(pair, slots[pair % 2], False)
+                work(pair, slots[pair % 2], False, slots[(pair + 1) % 2] if pair + 1 < pairs else None)
 
         @pl.when(hits != 0)
         def _():
             def step(pair, _):
-                bring(pair, first_s)
+                for j in range(ARRAYS):
+                    bring(pair, first_s, j)
                 work(pair, first_s, True)
                 return 0
 
@@ -316,10 +321,14 @@
 
     def body(barrier_ref, cell_ref):
         r0 = pl.program_id(0) * BLOCK
-        for r in range(BLOCK):
-            cell = (col_add[...] + row_add[pl.ds(r0 + r, 1), :]) * scaling_ref[r0 + r] - barrier_ref[r]
-            cell = turned(cell.astype(jnp.bfloat16))
-            cell_ref[:, r] = cell.astype(jnp.bfloat16).reshape(probs, sizes, inds)
+        ready = None
+        for r in range(BLOCK + 1):
+            last = ready
+            if r < BLOCK:
+                ready = (col_add[...] + row_add[pl.ds(r0 + r, 1), :]) * scaling_ref[r0 + r] - barrier_ref[r]
+                ready = ready.astype(jnp.bfloat16)
+            if r:
+                cell_ref[:, r - 1] = turned(last).astype(jnp.bfloat16).reshape(probs, sizes, inds)
 
     deep = pl.Buffered(4)
     cells = pl.BlockSpec((probs, BLOCK, sizes, inds), lambda b: (0, b, 0, 0))
@@ -411,8 +420,8 @@
         in_specs=[SMEM_SPEC, VMEM_SPEC] + [ANY_SPEC] * 5 + [VMEM_SPEC] * 2,
         out_specs=[VMEM_SPEC, ANY_SPEC] + [VMEM_SPEC] * 3,
         scratch_shapes=[
-            pltpu.VMEM((5, inds, 2 * LANES), F32),
-            pltpu.VMEM((5, inds, 2 * LANES), F32),
+            pltpu.VMEM((ARRAYS, inds, 2 * LANES), F32),
+            pltpu.VMEM((ARRAYS, inds, 2 * LANES), F32),
             pltpu.VMEM((rows, LANES), F32),
             pltpu.VMEM((inds, LANES), F32),
             pltpu.VMEM((2, inds, LANES), F32),

time: 219 us -> 222 us (1.014)
  Pallas kernels: 93.8 us -> 97.7 us
    pallas_call x1, Pallas kernels: 41.6 us -> 45.5 us  [local(): pl.pallas_call(functools.partial(prepare_kernel, rows, sizes, inds, probs...]
  transfers between devices with their start and end apart: 70 -> 70, of which waited for: 57 -> 40; matrix products, arithmetic and copies ran while one was open for 0% -> 0% of each run, Pallas kernels for 7% -> 7%
where the time goes in v6:
time: 222 us; the launch traced here: 221 us
  Pallas kernels  97.7 us (44%)
  starting transfers between devices  67.6 us (30%)
  waiting for transfers between devices  52.5 us (24%)
    ppermute x70, starting transfers between devices, exchange(): lax.ppermute(x, axis, [(j, j ^ flip) for j in range(count)])  67.6 us
    ppermute x70, waiting for transfers between devices, exchange(): lax.ppermute(x, axis, [(j, j ^ flip) for j in range(count)])  52.5 us
    pallas_call x1, Pallas kernels, local(): pl.pallas_call(functools.partial(prepare_kernel, rows, sizes, inds, probs...  45.5 us
    pallas_call x63, Pallas kernels, call(): pl.pallas_call(kernel, out_shape=outs, in_specs=[VMEM_SPEC] * len(args),...  35.9 us
    pallas_call x1, Pallas kernels, local(): pl.pallas_call(functools.partial(finish_kernel, rows, sizes, inds, probs,...  16.3 us
  transfers between devices with their start and end apart: 70, of which 40 were waited for; matrix products, arithmetic and copies ran while one was open for 0% of the time, Pallas kernels for 7%

profile of v6, /device:TPU:0, one launch (start us, length us, event | category | flops | bytes accessed | tf_op | source)
XLA Modules:
  0.0 221.5 jit_solution(17074601159326320571)
XLA Ops:
  3.2 45.5 %prepare.1 = (f32[192,256,128]{2,1,0:T(8,128)S(1)}, f32[192,256,128]{2,1,0:T(8,128)}, f32[2,192,128]{2,1,0:T(8,128)S(1)}, f32[2,128,128]{2,1,0:T(8,128)S(1)}, f32[2,128,128]{2,1,0:T(8,128)S(1)}) custom-call(s32[18]{0:T(128)S(1)} %pad_add_fusion.info_ref, f32[8,128]{1,0:T(8,128)S(1)} %broadcast_in_dim.3.odd_ref, bf16[8,192,16,256]{3,2,1,0:T(8,128)(2,1)} %pos_hbm.1, ...), custom_call_target="tpu_custom_call" | custom-call | tf_op jit(solution)/shard_map/prepare/pallas_call | solution.py:411
  48.8 3.1 %collective-permute-start = (f32[2,192,128]{2,1,0:T(8,128)S(1)}, f32[2,192,128]{2,1,0:T(8,128)S(1)}, u32[]{:S(2)}, u32[]{:S(2)}) collective-permute-start(f32[2,192,128]{2,1,0:T(8,128)S(1)} %get-tuple-element.33.refs_0_), channel_id=1, source_target_pairs={{0,1},{1,0},{2,3},{3,2},{4,5},{5,4},{6,7},{7,6},{8,9},{9,8},{10,11... | collective-permute-start | bytes 589832 | tf_op jit(solution)/shard_map/ppermute | solution.py:349
  53.4 2.2 collective-permute-start.3
  57.5 2.8 %collective-permute-start.1 = (f32[2,192,128]{2,1,0:T(8,128)S(1)}, f32[2,192,128]{2,1,0:T(8,128)S(1)}, u32[]{:S(2)}, u32[]{:S(2)}) collective-permute-start(f32[2,192,128]{2,1,0:T(8,128)S(1)} %join.29.refs_0_), channel_id=1, source_target_pairs={{0,2},{1,3},{2,0},{3,1},{4,6},{5,7},{6,4},{7,5},{8,10},{9,11},{10,... | collective-permute-start | bytes 589832 | tf_op jit(solution)/shard_map/ppermute | solution.py:349
  62.5 6.8 %collective-permute-done.1.refs_1_ = f32[2,192,128]{2,1,0:T(8,128)S(1)} collective-permute-done((f32[2,192,128]{2,1,0:T(8,128)S(1)}, f32[2,192,128]{2,1,0:T(8,128)S(1)}, u32[]{:S(2)}, u32[]{:S(2)}) %collective-permute-start.1) | collective-permute-done | bytes 196640 | tf_op jit(solution)/shard_map/ppermute | solution.py:349
  75.7 2.4 %collective-permute-start.10 = (f32[128,128]{1,0:T(8,128)S(1)}, f32[128,128]{1,0:T(8,128)S(1)}, u32[]{:S(2)}, u32[]{:S(2)}) collective-permute-start(f32[128,128]{1,0:T(8,128)S(1)} %join.33.refs_0_), channel_id=1, source_target_pairs={{0,8},{4,12},{8,0},{12,4},{16,24},{20,28},{24,16},{28,20},{1,9},{5... | collective-permute-start | bytes 196616 | tf_op jit(solution)/shard_map/ppermute | solution.py:349
  78.5 2.5 %collective-permute-start.8 = (f32[192,128]{1,0:T(8,128)S(1)}, f32[192,128]{1,0:T(8,128)S(1)}, u32[]{:S(2)}, u32[]{:S(2)}) collective-permute-start(f32[192,128]{1,0:T(8,128)S(1)} %join.32.refs_0_), channel_id=1, source_target_pairs={{0,2},{1,3},{2,0},{3,1},{4,6},{5,7},{6,4},{7,5},{8,10},{9,11},{10,... | collective-permute-start | bytes 294920 | tf_op jit(solution)/shard_map/ppermute | solution.py:349
  82.5 2.1 row_sweep.9.refs_0_._
  90.8 2.1 collective-permute-start.17
  93.2 2.4 %collective-permute-start.15 = (f32[192,128]{1,0:T(8,128)S(1)}, f32[192,128]{1,0:T(8,128)S(1)}, u32[]{:S(2)}, u32[]{:S(2)}) collective-permute-start(f32[192,128]{1,0:T(8,128)S(1)} %join.35.refs_0_), channel_id=1, source_target_pairs={{0,2},{1,3},{2,0},{3,1},{4,6},{5,7},{6,4},{7,5},{8,10},{9,11},{10,... | collective-permute-start | bytes 294920 | tf_op jit(solution)/shard_map/ppermute | solution.py:349
  97.1 2.1 row_sweep.10.refs_0_._
  105.6 2.0 collective-permute-start.24
  108.0 2.3 %collective-permute-start.22 = (f32[192,128]{1,0:T(8,128)S(1)}, f32[192,128]{1,0:T(8,128)S(1)}, u32[]{:S(2)}, u32[]{:S(2)}) collective-permute-start(f32[192,128]{1,0:T(8,128)S(1)} %join.38.refs_0_), channel_id=1, source_target_pairs={{0,2},{1,3},{2,0},{3,1},{4,6},{5,7},{6,4},{7,5},{8,10},{9,11},{10,... | collective-permute-start | bytes 294920 | tf_op jit(solution)/shard_map/ppermute | solution.py:349
  111.7 2.1 row_sweep.11.refs_0_._
  120.3 2.0 collective-permute-start.31
  122.7 2.2 %collective-permute-start.29 = (f32[192,128]{1,0:T(8,128)S(1)}, f32[192,128]{1,0:T(8,128)S(1)}, u32[]{:S(2)}, u32[]{:S(2)}) collective-permute-start(f32[192,128]{1,0:T(8,128)S(1)} %join.41.refs_0_), channel_id=1, source_target_pairs={{0,2},{1,3},{2,0},{3,1},{4,6},{5,7},{6,4},{7,5},{8,10},{9,11},{10,... | collective-permute-start | bytes 294920 | tf_op jit(solution)/shard_map/ppermute | solution.py:349
  126.3 2.1 row_sweep.12.refs_0_._
  135.0 2.0 collective-permute-start.38
  137.4 2.1 collective-permute-start.36
  140.9 2.1 row_sweep.13.refs_0_._
  149.8 2.0 collective-permute-start.45
  152.2 2.0 collective-permute-start.43
  155.6 2.1 row_sweep.14.refs_0_._
  164.5 2.0 collective-permute-start.52
  170.2 2.1 row_sweep.15.refs_0_._
  172.3 2.0 collective-permute-done.50.refs_1_
  179.2 2.0 collective-permute-start.59
  183.6 5.4 %collective-permute-done.57.refs_1_ = f32[192,128]{1,0:T(8,128)S(1)} collective-permute-done((f32[192,128]{1,0:T(8,128)S(1)}, f32[192,128]{1,0:T(8,128)S(1)}, u32[]{:S(2)}, u32[]{:S(2)}) %collective-permute-start.57) | collective-permute-done | bytes 98336 | tf_op jit(solution)/shard_map/ppermute | solution.py:349
  189.1 2.4 %products.1.refs_0_ = f32[16,128]{1,0:T(8,128)S(1)} custom-call(f32[192,256,128]{2,1,0:T(8,128)S(1)} %get-tuple-element.31.scaling_ref, f32[192,128]{1,0:T(8,128)S(1)} %get-tuple-element.36.refs_2_.row_diag_ref, f32[256,128]{1,0:T(8,128)S(1)} %get-tuple-element.37.diag.col_diag_ref, f32[192,128]{1,0:T(8,128)S(1)} %get-tuple-element.38.row_ref.rest_0_.rest_4_, ...), custom_call_target="tpu_custom_call" | custom-call | tf_op jit(solution)/shard_map/products/pallas_call | solution.py:354
  194.3 2.0 collective-permute-start.64
  198.0 2.6 %collective-permute-start.69 = (f32[16,128]{1,0:T(8,128)S(1)}, f32[16,128]{1,0:T(8,128)S(1)}, u32[]{:S(2)}, u32[]{:S(2)}) collective-permute-start(f32[16,128]{1,0:T(8,128)S(1)} %join.57.rest_0_), channel_id=1, source_target_pairs={{0,3},{1,2},{2,1},{3,0},{4,7},{5,6},{6,5},{7,4},{8,11},{9,10},{10,... | collective-permute-start | bytes 24584 | tf_op jit(solution)/shard_map/ppermute | solution.py:349
  205.2 16.3 %finish.1 = (bf16[8,192,16,256]{3,2,1,0:T(8,128)(2,1)}, f32[128,192]{1,0:T(8,128)}, f32[128,256]{1,0:T(8,128)}) custom-call(f32[192,256,128]{2,1,0:T(8,128)S(1)} %get-tuple-element.31.scaling_ref, f32[192,256,128]{2,1,0:T(8,128)} %get-tuple-element.32.barrier_hbm, f32[128,192]{1,0:T(8,128)S(1)} %bitcast.11, f32[128,256]{1,0:T(8,128)S(1)} %bitcast.13, ...), custom_call_target="tpu_custom_call" | custom-call | tf_op jit(solution)/shard_map/finish/pallas_call | solution.py:466
  (181 shorter events, 84.3 us)
Async XLA Ops:
  48.8 8.6 %collective-permute-start = (f32[2,192,128]{2,1,0:T(8,128)S(1)}, f32[2,192,128]{2,1,0:T(8,128)S(1)}, u32[]{:S(2)}, u32[]{:S(2)}) collective-permute-start(f32[2,192,128]{2,1,0:T(8,128)S(1)} %get-tuple-element.33.refs_0_), channel_id=1, source_target_pairs={{0,1},{1,0},{2,3},{3,2},{4,5},{5,4},{6,7},{7,6},{8,9},{9,8},{10,11... | collective-permute-start | bytes 589832 | tf_op jit(solution)/shard_map/ppermute | solution.py:349
  52.0 8.3 %collective-permute-start.5 = (f32[2,128,128]{2,1,0:T(8,128)S(1)}, f32[2,128,128]{2,1,0:T(8,128)S(1)}, u32[]{:S(2)}, u32[]{:S(2)}) collective-permute-start(f32[2,128,128]{2,1,0:T(8,128)S(1)} %join.30.refs_0_), channel_id=1, source_target_pairs={{0,24},{4,28},{8,16},{12,20},{16,8},{20,12},{24,0},{28,4},{1,25},{... | collective-permute-start | bytes 393224 | tf_op jit(solution)/shard_map/ppermute | solution.py:349
  53.4 7.7 %collective-permute-start.4 = (f32[2,128,128]{2,1,0:T(8,128)S(1)}, f32[2,128,128]{2,1,0:T(8,128)S(1)}, u32[]{:S(2)}, u32[]{:S(2)}) collective-permute-start(f32[2,128,128]{2,1,0:T(8,128)S(1)} %join.30.refs_0_), channel_id=1, source_target_pairs={{0,16},{4,20},{8,24},{12,28},{16,0},{20,4},{24,8},{28,12},{1,17},{... | collective-permute-start | bytes 393224 | tf_op jit(solution)/shard_map/ppermute | solution.py:349
  53.4 7.7 %collective-permute-start.3 = (f32[2,128,128]{2,1,0:T(8,128)S(1)}, f32[2,128,128]{2,1,0:T(8,128)S(1)}, u32[]{:S(2)}, u32[]{:S(2)}) collective-permute-start(f32[2,128,128]{2,1,0:T(8,128)S(1)} %join.30.refs_0_), channel_id=1, source_target_pairs={{0,8},{4,12},{8,0},{12,4},{16,24},{20,28},{24,16},{28,20},{1,9},{5... | collective-permute-start | bytes 393224 | tf_op jit(solution)/shard_map/ppermute | solution.py:349
  57.5 11.8 %collective-permute-start.1 = (f32[2,192,128]{2,1,0:T(8,128)S(1)}, f32[2,192,128]{2,1,0:T(8,128)S(1)}, u32[]{:S(2)}, u32[]{:S(2)}) collective-permute-start(f32[2,192,128]{2,1,0:T(8,128)S(1)} %join.29.refs_0_), channel_id=1, source_target_pairs={{0,2},{1,3},{2,0},{3,1},{4,6},{5,7},{6,4},{7,5},{8,10},{9,11},{10,... | collective-permute-start | bytes 589832 | tf_op jit(solution)/shard_map/ppermute | solution.py:349
  74.6 6.5 %collective-permute-start.12 = (f32[128,128]{1,0:T(8,128)S(1)}, f32[128,128]{1,0:T(8,128)S(1)}, u32[]{:S(2)}, u32[]{:S(2)}) collective-permute-start(f32[128,128]{1,0:T(8,128)S(1)} %join.33.refs_0_), channel_id=1, source_target_pairs={{0,24},{4,28},{8,16},{12,20},{16,8},{20,12},{24,0},{28,4},{1,25},{... | collective-permute-start | bytes 196616 | tf_op jit(solution)/shard_map/ppermute | solution.py:349
  75.1 5.9 %collective-permute-start.11 = (f32[128,128]{1,0:T(8,128)S(1)}, f32[128,128]{1,0:T(8,128)S(1)}, u32[]{:S(2)}, u32[]{:S(2)}) collective-permute-start(f32[128,128]{1,0:T(8,128)S(1)} %join.33.refs_0_), channel_id=1, source_target_pairs={{0,16},{4,20},{8,24},{12,28},{16,0},{20,4},{24,8},{28,12},{1,17},{... | collective-permute-start | bytes 196616 | tf_op jit(solution)/shard_map/ppermute | solution.py:349
  75.7 5.3 %collective-permute-start.10 = (f32[128,128]{1,0:T(8,128)S(1)}, f32[128,128]{1,0:T(8,128)S(1)}, u32[]{:S(2)}, u32[]{:S(2)}) collective-permute-start(f32[128,128]{1,0:T(8,128)S(1)} %join.33.refs_0_), channel_id=1, source_target_pairs={{0,8},{4,12},{8,0},{12,4},{16,24},{20,28},{24,16},{28,20},{1,9},{5... | collective-permute-start | bytes 196616 | tf_op jit(solution)/shard_map/ppermute | solution.py:349
  78.5 7.4 %collective-permute-start.8 = (f32[192,128]{1,0:T(8,128)S(1)}, f32[192,128]{1,0:T(8,128)S(1)}, u32[]{:S(2)}, u32[]{:S(2)}) collective-permute-start(f32[192,128]{1,0:T(8,128)S(1)} %join.32.refs_0_), channel_id=1, source_target_pairs={{0,2},{1,3},{2,0},{3,1},{4,6},{5,7},{6,4},{7,5},{8,10},{9,11},{10,... | collective-permute-start | bytes 294920 | tf_op jit(solution)/shard_map/ppermute | solution.py:349
  89.3 6.4 %collective-permute-start.19 = (f32[128,128]{1,0:T(8,128)S(1)}, f32[128,128]{1,0:T(8,128)S(1)}, u32[]{:S(2)}, u32[]{:S(2)}) collective-permute-start(f32[128,128]{1,0:T(8,128)S(1)} %join.36.refs_0_), channel_id=1, source_target_pairs={{0,24},{4,28},{8,16},{12,20},{16,8},{20,12},{24,0},{28,4},{1,25},{... | collective-permute-start | bytes 196616 | tf_op jit(solution)/shard_map/ppermute | solution.py:349
  89.9 5.8 %collective-permute-start.18 = (f32[128,128]{1,0:T(8,128)S(1)}, f32[128,128]{1,0:T(8,128)S(1)}, u32[]{:S(2)}, u32[]{:S(2)}) collective-permute-start(f32[128,128]{1,0:T(8,128)S(1)} %join.36.refs_0_), channel_id=1, source_target_pairs={{0,16},{4,20},{8,24},{12,28},{16,0},{20,4},{24,8},{28,12},{1,17},{... | collective-permute-start | bytes 196616 | tf_op jit(solution)/shard_map/ppermute | solution.py:349
  93.2 7.4 %collective-permute-start.15 = (f32[192,128]{1,0:T(8,128)S(1)}, f32[192,128]{1,0:T(8,128)S(1)}, u32[]{:S(2)}, u32[]{:S(2)}) collective-permute-start(f32[192,128]{1,0:T(8,128)S(1)} %join.35.refs_0_), channel_id=1, source_target_pairs={{0,2},{1,3},{2,0},{3,1},{4,6},{5,7},{6,4},{7,5},{8,10},{9,11},{10,... | collective-permute-start | bytes 294920 | tf_op jit(solution)/shard_map/ppermute | solution.py:349
  104.0 6.3 %collective-permute-start.26 = (f32[128,128]{1,0:T(8,128)S(1)}, f32[128,128]{1,0:T(8,128)S(1)}, u32[]{:S(2)}, u32[]{:S(2)}) collective-permute-start(f32[128,128]{1,0:T(8,128)S(1)} %join.39.refs_0_), channel_id=1, source_target_pairs={{0,24},{4,28},{8,16},{12,20},{16,8},{20,12},{24,0},{28,4},{1,25},{... | collective-permute-start | bytes 196616 | tf_op jit(solution)/shard_map/ppermute | solution.py:349
  104.6 5.7 %collective-permute-start.25 = (f32[128,128]{1,0:T(8,128)S(1)}, f32[128,128]{1,0:T(8,128)S(1)}, u32[]{:S(2)}, u32[]{:S(2)}) collective-permute-start(f32[128,128]{1,0:T(8,128)S(1)} %join.39.refs_0_), channel_id=1, source_target_pairs={{0,16},{4,20},{8,24},{12,28},{16,0},{20,4},{24,8},{28,12},{1,17},{... | collective-permute-start | bytes 196616 | tf_op jit(solution)/shard_map/ppermute | solution.py:349
  108.0 7.4 %collective-permute-start.22 = (f32[192,128]{1,0:T(8,128)S(1)}, f32[192,128]{1,0:T(8,128)S(1)}, u32[]{:S(2)}, u32[]{:S(2)}) collective-permute-start(f32[192,128]{1,0:T(8,128)S(1)} %join.38.refs_0_), channel_id=1, source_target_pairs={{0,2},{1,3},{2,0},{3,1},{4,6},{5,7},{6,4},{7,5},{8,10},{9,11},{10,... | collective-permute-start | bytes 294920 | tf_op jit(solution)/shard_map/ppermute | solution.py:349
  118.7 6.2 %collective-permute-start.33 = (f32[128,128]{1,0:T(8,128)S(1)}, f32[128,128]{1,0:T(8,128)S(1)}, u32[]{:S(2)}, u32[]{:S(2)}) collective-permute-start(f32[128,128]{1,0:T(8,128)S(1)} %join.42.refs_0_), channel_id=1, source_target_pairs={{0,24},{4,28},{8,16},{12,20},{16,8},{20,12},{24,0},{28,4},{1,25},{... | collective-permute-start | bytes 196616 | tf_op jit(solution)/shard_map/ppermute | solution.py:349
  119.3 5.6 %collective-permute-start.32 = (f32[128,128]{1,0:T(8,128)S(1)}, f32[128,128]{1,0:T(8,128)S(1)}, u32[]{:S(2)}, u32[]{:S(2)}) collective-permute-start(f32[128,128]{1,0:T(8,128)S(1)} %join.42.refs_0_), channel_id=1, source_target_pairs={{0,16},{4,20},{8,24},{12,28},{16,0},{20,4},{24,8},{28,12},{1,17},{... | collective-permute-start | bytes 196616 | tf_op jit(solution)/shard_map/ppermute | solution.py:349
  122.7 7.4 %collective-permute-start.29 = (f32[192,128]{1,0:T(8,128)S(1)}, f32[192,128]{1,0:T(8,128)S(1)}, u32[]{:S(2)}, u32[]{:S(2)}) collective-permute-start(f32[192,128]{1,0:T(8,128)S(1)} %join.41.refs_0_), channel_id=1, source_target_pairs={{0,2},{1,3},{2,0},{3,1},{4,6},{5,7},{6,4},{7,5},{8,10},{9,11},{10,... | collective-permute-start | bytes 294920 | tf_op jit(solution)/shard_map/ppermute | solution.py:349
  133.5 6.1 %collective-permute-start.40 = (f32[128,128]{1,0:T(8,128)S(1)}, f32[128,128]{1,0:T(8,128)S(1)}, u32[]{:S(2)}, u32[]{:S(2)}) collective-permute-start(f32[128,128]{1,0:T(8,128)S(1)} %join.45.refs_0_), channel_id=1, source_target_pairs={{0,24},{4,28},{8,16},{12,20},{16,8},{20,12},{24,0},{28,4},{1,25},{... | collective-permute-start | bytes 196616 | tf_op jit(solution)/shard_map/ppermute | solution.py:349
  134.0 5.5 %collective-permute-start.39 = (f32[128,128]{1,0:T(8,128)S(1)}, f32[128,128]{1,0:T(8,128)S(1)}, u32[]{:S(2)}, u32[]{:S(2)}) collective-permute-start(f32[128,128]{1,0:T(8,128)S(1)} %join.45.refs_0_), channel_id=1, source_target_pairs={{0,16},{4,20},{8,24},{12,28},{16,0},{20,4},{24,8},{28,12},{1,17},{... | collective-permute-start | bytes 196616 | tf_op jit(solution)/shard_map/ppermute | solution.py:349
  137.4 7.4 %collective-permute-start.36 = (f32[192,128]{1,0:T(8,128)S(1)}, f32[192,128]{1,0:T(8,128)S(1)}, u32[]{:S(2)}, u32[]{:S(2)}) collective-permute-start(f32[192,128]{1,0:T(8,128)S(1)} %join.44.refs_0_), channel_id=1, source_target_pairs={{0,2},{1,3},{2,0},{3,1},{4,6},{5,7},{6,4},{7,5},{8,10},{9,11},{10,... | collective-permute-start | bytes 294920 | tf_op jit(solution)/shard_map/ppermute | solution.py:349
  148.2 6.0 %collective-permute-start.47 = (f32[128,128]{1,0:T(8,128)S(1)}, f32[128,128]{1,0:T(8,128)S(1)}, u32[]{:S(2)}, u32[]{:S(2)}) collective-permute-start(f32[128,128]{1,0:T(8,128)S(1)} %join.48.refs_0_), channel_id=1, source_target_pairs={{0,24},{4,28},{8,16},{12,20},{16,8},{20,12},{24,0},{28,4},{1,25},{... | collective-permute-start | bytes 196616 | tf_op jit(solution)/shard_map/ppermute | solution.py:349
  148.8 5.4 %collective-permute-start.46 = (f32[128,128]{1,0:T(8,128)S(1)}, f32[128,128]{1,0:T(8,128)S(1)}, u32[]{:S(2)}, u32[]{:S(2)}) collective-permute-start(f32[128,128]{1,0:T(8,128)S(1)} %join.48.refs_0_), channel_id=1, source_target_pairs={{0,16},{4,20},{8,24},{12,28},{16,0},{20,4},{24,8},{28,12},{1,17},{... | collective-permute-start | bytes 196616 | tf_op jit(solution)/shard_map/ppermute | solution.py:349
  152.2 7.4 %collective-permute-start.43 = (f32[192,128]{1,0:T(8,128)S(1)}, f32[192,128]{1,0:T(8,128)S(1)}, u32[]{:S(2)}, u32[]{:S(2)}) collective-permute-start(f32[192,128]{1,0:T(8,128)S(1)} %join.47.refs_0_), channel_id=1, source_target_pairs={{0,2},{1,3},{2,0},{3,1},{4,6},{5,7},{6,4},{7,5},{8,10},{9,11},{10,... | collective-permute-start | bytes 294920 | tf_op jit(solution)/shard_map/ppermute | solution.py:349
  162.9 5.9 %collective-permute-start.54 = (f32[128,128]{1,0:T(8,128)S(1)}, f32[128,128]{1,0:T(8,128)S(1)}, u32[]{:S(2)}, u32[]{:S(2)}) collective-permute-start(f32[128,128]{1,0:T(8,128)S(1)} %join.51.refs_0_), channel_id=1, source_target_pairs={{0,24},{4,28},{8,16},{12,20},{16,8},{20,12},{24,0},{28,4},{1,25},{... | collective-permute-start | bytes 196616 | tf_op jit(solution)/shard_map/ppermute | solution.py:349
  163.5 5.3 %collective-permute-start.53 = (f32[128,128]{1,0:T(8,128)S(1)}, f32[128,128]{1,0:T(8,128)S(1)}, u32[]{:S(2)}, u32[]{:S(2)}) collective-permute-start(f32[128,128]{1,0:T(8,128)S(1)} %join.51.refs_0_), channel_id=1, source_target_pairs={{0,16},{4,20},{8,24},{12,28},{16,0},{20,4},{24,8},{28,12},{1,17},{... | collective-permute-start | bytes 196616 | tf_op jit(solution)/shard_map/ppermute | solution.py:349
  166.9 7.4 %collective-permute-start.50 = (f32[192,128]{1,0:T(8,128)S(1)}, f32[192,128]{1,0:T(8,128)S(1)}, u32[]{:S(2)}, u32[]{:S(2)}) collective-permute-start(f32[192,128]{1,0:T(8,128)S(1)} %join.50.refs_0_), channel_id=1, source_target_pairs={{0,2},{1,3},{2,0},{3,1},{4,6},{5,7},{6,4},{7,5},{8,10},{9,11},{10,... | collective-permute-start | bytes 294920 | tf_op jit(solution)/shard_map/ppermute | solution.py:349
  177.6 5.8 %collective-permute-start.61 = (f32[128,128]{1,0:T(8,128)S(1)}, f32[128,128]{1,0:T(8,128)S(1)}, u32[]{:S(2)}, u32[]{:S(2)}) collective-permute-start(f32[128,128]{1,0:T(8,128)S(1)} %join.54.refs_0_), channel_id=1, source_target_pairs={{0,24},{4,28},{8,16},{12,20},{16,8},{20,12},{24,0},{28,4},{1,25},{... | collective-permute-start | bytes 196616 | tf_op jit(solution)/shard_map/ppermute | solution.py:349
  178.2 5.3 %collective-permute-start.60 = (f32[128,128]{1,0:T(8,128)S(1)}, f32[128,128]{1,0:T(8,128)S(1)}, u32[]{:S(2)}, u32[]{:S(2)}) collective-permute-start(f32[128,128]{1,0:T(8,128)S(1)} %join.54.refs_0_), channel_id=1, source_target_pairs={{0,16},{4,20},{8,24},{12,28},{16,0},{20,4},{24,8},{28,12},{1,17},{... | collective-permute-start | bytes 196616 | tf_op jit(solution)/shard_map/ppermute | solution.py:349
  181.6 7.4 %collective-permute-start.57 = (f32[192,128]{1,0:T(8,128)S(1)}, f32[192,128]{1,0:T(8,128)S(1)}, u32[]{:S(2)}, u32[]{:S(2)}) collective-permute-start(f32[192,128]{1,0:T(8,128)S(1)} %join.53.refs_0_), channel_id=1, source_target_pairs={{0,2},{1,3},{2,0},{3,1},{4,6},{5,7},{6,4},{7,5},{8,10},{9,11},{10,... | collective-permute-start | bytes 294920 | tf_op jit(solution)/shard_map/ppermute | solution.py:349
  183.5 5.5 %collective-permute-start.62 = (f32[128,128]{1,0:T(8,128)S(1)}, f32[128,128]{1,0:T(8,128)S(1)}, u32[]{:S(2)}, u32[]{:S(2)}) collective-permute-start(f32[128,128]{1,0:T(8,128)S(1)} %join.55.own), channel_id=1, source_target_pairs={{0,4},{4,0},{8,12},{12,8},{16,20},{20,16},{24,28},{28,24},{1,5},{5... | collective-permute-start | bytes 196616 | tf_op jit(solution)/shard_map/ppermute | solution.py:349
  198.0 5.4 %collective-permute-start.69 = (f32[16,128]{1,0:T(8,128)S(1)}, f32[16,128]{1,0:T(8,128)S(1)}, u32[]{:S(2)}, u32[]{:S(2)}) collective-permute-start(f32[16,128]{1,0:T(8,128)S(1)} %join.57.rest_0_), channel_id=1, source_target_pairs={{0,3},{1,2},{2,1},{3,0},{4,7},{5,6},{6,5},{7,4},{8,11},{9,10},{10,... | collective-permute-start | bytes 24584 | tf_op jit(solution)/shard_map/ppermute | solution.py:349
  (41 other events, 138.4 us)

commit v7 on v5

--- a/solution.py
+++ b/solution.py
@@ -35,15 +35,13 @@
     return jnp.broadcast_to(rows[:, None, :], (BLOCK, 8, LANES))
 
 
-def turned(x):
-    return lax.dot_general(
-        identity(x.shape[1]), x, (((1,), (1,)), ((), ())), preferred_element_type=F32
-    )
+def turned(x, eye_ref):
+    return lax.dot_general(eye_ref[...], x, (((1,), (1,)), ((), ())), preferred_element_type=F32)
 
 
 def identity(size):
     row = lax.broadcasted_iota(jnp.int32, (size, size), 0)
-    return (row == lax.broadcasted_iota(jnp.int32, (size, size), 1)).astype(jnp.bfloat16)
+    return (row == lax.broadcasted_iota(jnp.int32, (size, size), 1)).astype(F32).astype(jnp.bfloat16)
 
 
 def any_attack(info_ref, first_row):
@@ -66,12 +64,13 @@
     rows, sizes, inds, probs, nind,
     info_ref, odd_ref, pos_hbm, low_hbm, high_hbm, upper_hbm, supp_hbm, drow_ref, dcol_ref,
     scaling_ref, barrier_hbm, row_ref, keep_ref, send_ref,
-    first_s, second_s, drow_t, dcol_t, col_ref,
+    first_s, second_s, drow_t, dcol_t, col_ref, eye_ref,
 ):
     blocks = rows // BLOCK
     first_row = info_ref[0] * rows
     first_ind = info_ref[1] * inds
     col_ref[...] = jnp.zeros_like(col_ref)
+    eye_ref[...] = identity(inds)
     drow_t[...] = drow_ref[...].T
     dcol_t[...] = dcol_ref[...].T
 
@@ -81,13 +80,13 @@
         def bring(pair, slot):
             for j, ref in enumerate((pos_ref, low_ref, high_ref)):
                 both = [ref[:, 2 * pair + r].reshape(LANES, inds) for r in range(2)]
-                slot[j] = turned(jnp.concatenate(both, axis=0))
+                slot[j] = turned(jnp.concatenate(both, axis=0), eye_ref)
             for j, ref in enumerate((upper_ref, supp_ref)):
                 both = []
                 for r in range(2):
                     one = ref[2 * pair + r].astype(F32).astype(jnp.bfloat16)
                     both += [one] * probs
-                slot[3 + j] = turned(jnp.concatenate(both, axis=0))
+                slot[3 + j] = turned(jnp.concatenate(both, axis=0), eye_ref)
 
         def work(pair, slot, attacked):
             rhs_acc = [jnp.zeros((8, LANES), F32)] * 2
@@ -283,7 +282,8 @@
     count = 3 * iters
     sums, rest = rest[:nsum], rest[nsum:]
     row_p, col_p = rest[:count], rest[count : 2 * count]
-    cell_hbm, row_ref, col_ref, row_add, col_add = rest[2 * count :]
+    cell_hbm, row_ref, col_ref, row_add, col_add, eye_ref = rest[2 * count :]
+    eye_ref[...] = identity(LANES)
     lane = lax.broadcasted_iota(jnp.int32, (LANES, LANES), 0) // sizes
     other = lax.broadcasted_iota(jnp.int32, (LANES, LANES), 1) // sizes
     same = (lane == other).astype(F32)
@@ -318,7 +318,7 @@
         r0 = pl.program_id(0) * BLOCK
         for r in range(BLOCK):
             cell = (col_add[...] + row_add[pl.ds(r0 + r, 1), :]) * scaling_ref[r0 + r] - barrier_ref[r]
-            cell = turned(cell.astype(jnp.bfloat16))
+            cell = turned(cell.astype(jnp.bfloat16), eye_ref)
             cell_ref[:, r] = cell.astype(jnp.bfloat16).reshape(probs, sizes, inds)
 
     deep = pl.Buffered(4)
@@ -416,6 +416,7 @@
             pltpu.VMEM((rows, LANES), F32),
             pltpu.VMEM((inds, LANES), F32),
             pltpu.VMEM((2, inds, LANES), F32),
+            pltpu.VMEM((inds, inds), jnp.bfloat16),
         ],
         compiler_params=params(),
         name="prepare",
@@ -463,7 +464,11 @@
         ],
         in_specs=[VMEM_SPEC, ANY_SPEC] + [VMEM_SPEC] * (2 + len(sums) + 6 * iters),
         out_specs=[ANY_SPEC, VMEM_SPEC, VMEM_SPEC],
-        scratch_shapes=[pltpu.VMEM((rows, LANES), F32), pltpu.VMEM((inds, LANES), F32)],
+        scratch_shapes=[
+            pltpu.VMEM((rows, LANES), F32),
+            pltpu.VMEM((inds, LANES), F32),
+            pltpu.VMEM((LANES, LANES), jnp.bfloat16),
+        ],
         compiler_params=params(),
         name="finish",
     )(scaling, barrier, drow, dcol, *sums, *row_p, *col_p)

time: 219 us -> 220 us (level)
  Pallas kernels: 93.8 us -> 96 us
  transfers between devices with their start and end apart: 70 -> 70, of which waited for: 57 -> 48; matrix products, arithmetic and copies ran while one was open for 0% -> 0% of each run, Pallas kernels for 7% -> 7%
where the time goes in v7:
time: 220 us
  Pallas kernels  96 us (44%)
  starting transfers between devices  67.1 us (30%)
  waiting for transfers between devices  53 us (24%)
    ppermute x70, starting transfers between devices, exchange(): lax.ppermute(x, axis, [(j, j ^ flip) for j in range(count)])  67.1 us
    ppermute x70, waiting for transfers between devices, exchange(): lax.ppermute(x, axis, [(j, j ^ flip) for j in range(count)])  53 us
    pallas_call x1, Pallas kernels, local(): pl.pallas_call(functools.partial(prepare_kernel, rows, sizes, inds, probs...  43.6 us
    pallas_call x63, Pallas kernels, call(): pl.pallas_call(kernel, out_shape=outs, in_specs=[VMEM_SPEC] * len(args),...  35.9 us
    pallas_call x1, Pallas kernels, local(): pl.pallas_call(functools.partial(finish_kernel, rows, sizes, inds, probs,...  16.5 us
  transfers between devices with their start and end apart: 70, of which 48 were waited for; matrix products, arithmetic and copies ran while one was open for 0% of the time, Pallas kernels for 7%

profile of v7, /device:TPU:0, one launch (start us, length us, event | category | flops | bytes accessed | tf_op | source)
XLA Modules:
  0.0 219.7 jit_solution(11233366407156568037)
XLA Ops:
  3.2 43.6 %prepare.1 = (f32[192,256,128]{2,1,0:T(8,128)S(1)}, f32[192,256,128]{2,1,0:T(8,128)}, f32[2,192,128]{2,1,0:T(8,128)S(1)}, f32[2,128,128]{2,1,0:T(8,128)S(1)}, f32[2,128,128]{2,1,0:T(8,128)S(1)}) custom-call(s32[18]{0:T(128)S(1)} %pad_add_fusion.info_ref, f32[8,128]{1,0:T(8,128)S(1)} %broadcast_in_dim.3.odd_ref, bf16[8,192,16,256]{3,2,1,0:T(8,128)(2,1)} %pos_hbm.1, ...), custom_call_target="tpu_custom_call" | custom-call | tf_op jit(solution)/shard_map/prepare/pallas_call | solution.py:402
  46.9 3.1 %collective-permute-start = (f32[2,192,128]{2,1,0:T(8,128)S(1)}, f32[2,192,128]{2,1,0:T(8,128)S(1)}, u32[]{:S(2)}, u32[]{:S(2)}) collective-permute-start(f32[2,192,128]{2,1,0:T(8,128)S(1)} %get-tuple-element.33.refs_0_), channel_id=1, source_target_pairs={{0,1},{1,0},{2,3},{3,2},{4,5},{5,4},{6,7},{7,6},{8,9},{9,8},{10,11... | collective-permute-start | bytes 589832 | tf_op jit(solution)/shard_map/ppermute | solution.py:340
  50.1 2.3 %collective-permute-start.5 = (f32[2,128,128]{2,1,0:T(8,128)S(1)}, f32[2,128,128]{2,1,0:T(8,128)S(1)}, u32[]{:S(2)}, u32[]{:S(2)}) collective-permute-start(f32[2,128,128]{2,1,0:T(8,128)S(1)} %join.30.refs_0_), channel_id=1, source_target_pairs={{0,24},{4,28},{8,16},{12,20},{16,8},{20,12},{24,0},{28,4},{1,25},{... | collective-permute-start | bytes 393224 | tf_op jit(solution)/shard_map/ppermute | solution.py:340
  55.6 2.8 %collective-permute-start.1 = (f32[2,192,128]{2,1,0:T(8,128)S(1)}, f32[2,192,128]{2,1,0:T(8,128)S(1)}, u32[]{:S(2)}, u32[]{:S(2)}) collective-permute-start(f32[2,192,128]{2,1,0:T(8,128)S(1)} %join.29.refs_0_), channel_id=1, source_target_pairs={{0,2},{1,3},{2,0},{3,1},{4,6},{5,7},{6,4},{7,5},{8,10},{9,11},{10,... | collective-permute-start | bytes 589832 | tf_op jit(solution)/shard_map/ppermute | solution.py:340
  60.9 6.5 %collective-permute-done.1.refs_1_ = f32[2,192,128]{2,1,0:T(8,128)S(1)} collective-permute-done((f32[2,192,128]{2,1,0:T(8,128)S(1)}, f32[2,192,128]{2,1,0:T(8,128)S(1)}, u32[]{:S(2)}, u32[]{:S(2)}) %collective-permute-start.1) | collective-permute-done | bytes 196640 | tf_op jit(solution)/shard_map/ppermute | solution.py:340
  69.4 2.0 col_sweep.8
  74.1 2.1 collective-permute-start.10
  76.6 2.5 %collective-permute-start.8 = (f32[192,128]{1,0:T(8,128)S(1)}, f32[192,128]{1,0:T(8,128)S(1)}, u32[]{:S(2)}, u32[]{:S(2)}) collective-permute-start(f32[192,128]{1,0:T(8,128)S(1)} %join.32.refs_0_), channel_id=1, source_target_pairs={{0,2},{1,3},{2,0},{3,1},{4,6},{5,7},{6,4},{7,5},{8,10},{9,11},{10,... | collective-permute-start | bytes 294920 | tf_op jit(solution)/shard_map/ppermute | solution.py:340
  80.6 2.1 row_sweep.9.refs_0_._
  88.9 2.1 collective-permute-start.17
  91.3 2.4 %collective-permute-start.15 = (f32[192,128]{1,0:T(8,128)S(1)}, f32[192,128]{1,0:T(8,128)S(1)}, u32[]{:S(2)}, u32[]{:S(2)}) collective-permute-start(f32[192,128]{1,0:T(8,128)S(1)} %join.35.refs_0_), channel_id=1, source_target_pairs={{0,2},{1,3},{2,0},{3,1},{4,6},{5,7},{6,4},{7,5},{8,10},{9,11},{10,... | collective-permute-start | bytes 294920 | tf_op jit(solution)/shard_map/ppermute | solution.py:340
  95.3 2.1 row_sweep.10.refs_0_._
  103.6 2.0 collective-permute-start.24
  106.1 2.3 %collective-permute-start.22 = (f32[192,128]{1,0:T(8,128)S(1)}, f32[192,128]{1,0:T(8,128)S(1)}, u32[]{:S(2)}, u32[]{:S(2)}) collective-permute-start(f32[192,128]{1,0:T(8,128)S(1)} %join.38.refs_0_), channel_id=1, source_target_pairs={{0,2},{1,3},{2,0},{3,1},{4,6},{5,7},{6,4},{7,5},{8,10},{9,11},{10,... | collective-permute-start | bytes 294920 | tf_op jit(solution)/shard_map/ppermute | solution.py:340
  110.0 2.1 row_sweep.11.refs_0_._
  118.4 2.0 collective-permute-start.31
  120.8 2.2 collective-permute-start.29
  124.7 2.1 row_sweep.12.refs_0_._
  133.1 2.0 collective-permute-start.38
  135.5 2.1 collective-permute-start.36
  139.5 2.1 row_sweep.13.refs_0_._
  147.8 2.0 collective-permute-start.45
  150.3 2.0 collective-permute-start.43
  154.2 2.1 row_sweep.14.refs_0_._
  162.5 2.1 collective-permute-start.52
  168.9 2.1 row_sweep.15.refs_0_._
  177.2 2.1 collective-permute-start.59
  182.3 4.8 %collective-permute-done.57.refs_1_ = f32[192,128]{1,0:T(8,128)S(1)} collective-permute-done((f32[192,128]{1,0:T(8,128)S(1)}, f32[192,128]{1,0:T(8,128)S(1)}, u32[]{:S(2)}, u32[]{:S(2)}) %collective-permute-start.57) | collective-permute-done | bytes 98336 | tf_op jit(solution)/shard_map/ppermute | solution.py:340
  187.2 2.4 %products.1.refs_0_ = f32[16,128]{1,0:T(8,128)S(1)} custom-call(f32[192,256,128]{2,1,0:T(8,128)S(1)} %get-tuple-element.31.scaling_ref, f32[192,128]{1,0:T(8,128)S(1)} %get-tuple-element.36.refs_2_.row_diag_ref, f32[256,128]{1,0:T(8,128)S(1)} %get-tuple-element.37.diag.col_diag_ref, f32[192,128]{1,0:T(8,128)S(1)} %get-tuple-element.38.row_ref.rest_0_.rest_4_, ...), custom_call_target="tpu_custom_call" | custom-call | tf_op jit(solution)/shard_map/products/pallas_call | solution.py:345
  192.3 2.1 collective-permute-start.64
  196.0 2.7 %collective-permute-start.69 = (f32[16,128]{1,0:T(8,128)S(1)}, f32[16,128]{1,0:T(8,128)S(1)}, u32[]{:S(2)}, u32[]{:S(2)}) collective-permute-start(f32[16,128]{1,0:T(8,128)S(1)} %join.57.rest_0_), channel_id=1, source_target_pairs={{0,3},{1,2},{2,1},{3,0},{4,7},{5,6},{6,5},{7,4},{8,11},{9,10},{10,... | collective-permute-start | bytes 24584 | tf_op jit(solution)/shard_map/ppermute | solution.py:340
  203.2 16.5 %finish.1 = (bf16[8,192,16,256]{3,2,1,0:T(8,128)(2,1)}, f32[128,192]{1,0:T(8,128)}, f32[128,256]{1,0:T(8,128)}) custom-call(f32[192,256,128]{2,1,0:T(8,128)S(1)} %get-tuple-element.31.scaling_ref, f32[192,256,128]{2,1,0:T(8,128)} %get-tuple-element.32.barrier_hbm, f32[128,192]{1,0:T(8,128)S(1)} %bitcast.11, f32[128,256]{1,0:T(8,128)S(1)} %bitcast.13, ...), custom_call_target="tpu_custom_call" | custom-call | tf_op jit(solution)/shard_map/finish/pallas_call | solution.py:458
  (181 shorter events, 85.0 us)
Async XLA Ops:
  46.9 8.6 %collective-permute-start = (f32[2,192,128]{2,1,0:T(8,128)S(1)}, f32[2,192,128]{2,1,0:T(8,128)S(1)}, u32[]{:S(2)}, u32[]{:S(2)}) collective-permute-start(f32[2,192,128]{2,1,0:T(8,128)S(1)} %get-tuple-element.33.refs_0_), channel_id=1, source_target_pairs={{0,1},{1,0},{2,3},{3,2},{4,5},{5,4},{6,7},{7,6},{8,9},{9,8},{10,11... | collective-permute-start | bytes 589832 | tf_op jit(solution)/shard_map/ppermute | solution.py:340
  50.1 8.3 %collective-permute-start.5 = (f32[2,128,128]{2,1,0:T(8,128)S(1)}, f32[2,128,128]{2,1,0:T(8,128)S(1)}, u32[]{:S(2)}, u32[]{:S(2)}) collective-permute-start(f32[2,128,128]{2,1,0:T(8,128)S(1)} %join.30.refs_0_), channel_id=1, source_target_pairs={{0,24},{4,28},{8,16},{12,20},{16,8},{20,12},{24,0},{28,4},{1,25},{... | collective-permute-start | bytes 393224 | tf_op jit(solution)/shard_map/ppermute | solution.py:340
  52.3 7.1 %collective-permute-start.4 = (f32[2,128,128]{2,1,0:T(8,128)S(1)}, f32[2,128,128]{2,1,0:T(8,128)S(1)}, u32[]{:S(2)}, u32[]{:S(2)}) collective-permute-start(f32[2,128,128]{2,1,0:T(8,128)S(1)} %join.30.refs_0_), channel_id=1, source_target_pairs={{0,16},{4,20},{8,24},{12,28},{16,0},{20,4},{24,8},{28,12},{1,17},{... | collective-permute-start | bytes 393224 | tf_op jit(solution)/shard_map/ppermute | solution.py:340
  52.3 7.1 %collective-permute-start.3 = (f32[2,128,128]{2,1,0:T(8,128)S(1)}, f32[2,128,128]{2,1,0:T(8,128)S(1)}, u32[]{:S(2)}, u32[]{:S(2)}) collective-permute-start(f32[2,128,128]{2,1,0:T(8,128)S(1)} %join.30.refs_0_), channel_id=1, source_target_pairs={{0,8},{4,12},{8,0},{12,4},{16,24},{20,28},{24,16},{28,20},{1,9},{5... | collective-permute-start | bytes 393224 | tf_op jit(solution)/shard_map/ppermute | solution.py:340
  55.6 11.8 %collective-permute-start.1 = (f32[2,192,128]{2,1,0:T(8,128)S(1)}, f32[2,192,128]{2,1,0:T(8,128)S(1)}, u32[]{:S(2)}, u32[]{:S(2)}) collective-permute-start(f32[2,192,128]{2,1,0:T(8,128)S(1)} %join.29.refs_0_), channel_id=1, source_target_pairs={{0,2},{1,3},{2,0},{3,1},{4,6},{5,7},{6,4},{7,5},{8,10},{9,11},{10,... | collective-permute-start | bytes 589832 | tf_op jit(solution)/shard_map/ppermute | solution.py:340
  71.4 5.2 %collective-permute-start.7 = (f32[192,128]{1,0:T(8,128)S(1)}, f32[192,128]{1,0:T(8,128)S(1)}, u32[]{:S(2)}, u32[]{:S(2)}) collective-permute-start(f32[192,128]{1,0:T(8,128)S(1)} %row_sweep.8.refs_0_._), channel_id=1, source_target_pairs={{0,1},{1,0},{2,3},{3,2},{4,5},{5,4},{6,7},{7,6},{8,9},{9,8},{10,11... | collective-permute-start | bytes 294920 | tf_op jit(solution)/shard_map/ppermute | solution.py:340
  72.7 6.5 %collective-permute-start.12 = (f32[128,128]{1,0:T(8,128)S(1)}, f32[128,128]{1,0:T(8,128)S(1)}, u32[]{:S(2)}, u32[]{:S(2)}) collective-permute-start(f32[128,128]{1,0:T(8,128)S(1)} %join.33.refs_0_), channel_id=1, source_target_pairs={{0,24},{4,28},{8,16},{12,20},{16,8},{20,12},{24,0},{28,4},{1,25},{... | collective-permute-start | bytes 196616 | tf_op jit(solution)/shard_map/ppermute | solution.py:340
  74.1 5.1 %collective-permute-start.11 = (f32[128,128]{1,0:T(8,128)S(1)}, f32[128,128]{1,0:T(8,128)S(1)}, u32[]{:S(2)}, u32[]{:S(2)}) collective-permute-start(f32[128,128]{1,0:T(8,128)S(1)} %join.33.refs_0_), channel_id=1, source_target_pairs={{0,16},{4,20},{8,24},{12,28},{16,0},{20,4},{24,8},{28,12},{1,17},{... | collective-permute-start | bytes 196616 | tf_op jit(solution)/shard_map/ppermute | solution.py:340
  76.6 7.4 %collective-permute-start.8 = (f32[192,128]{1,0:T(8,128)S(1)}, f32[192,128]{1,0:T(8,128)S(1)}, u32[]{:S(2)}, u32[]{:S(2)}) collective-permute-start(f32[192,128]{1,0:T(8,128)S(1)} %join.32.refs_0_), channel_id=1, source_target_pairs={{0,2},{1,3},{2,0},{3,1},{4,6},{5,7},{6,4},{7,5},{8,10},{9,11},{10,... | collective-permute-start | bytes 294920 | tf_op jit(solution)/shard_map/ppermute | solution.py:340
  86.1 5.2 %collective-permute-start.14 = (f32[192,128]{1,0:T(8,128)S(1)}, f32[192,128]{1,0:T(8,128)S(1)}, u32[]{:S(2)}, u32[]{:S(2)}) collective-permute-start(f32[192,128]{1,0:T(8,128)S(1)} %row_sweep.9.refs_0_._), channel_id=1, source_target_pairs={{0,1},{1,0},{2,3},{3,2},{4,5},{5,4},{6,7},{7,6},{8,9},{9,8},{10,11... | collective-permute-start | bytes 294920 | tf_op jit(solution)/shard_map/ppermute | solution.py:340
  87.4 6.4 %collective-permute-start.19 = (f32[128,128]{1,0:T(8,128)S(1)}, f32[128,128]{1,0:T(8,128)S(1)}, u32[]{:S(2)}, u32[]{:S(2)}) collective-permute-start(f32[128,128]{1,0:T(8,128)S(1)} %join.36.refs_0_), channel_id=1, source_target_pairs={{0,24},{4,28},{8,16},{12,20},{16,8},{20,12},{24,0},{28,4},{1,25},{... | collective-permute-start | bytes 196616 | tf_op jit(solution)/shard_map/ppermute | solution.py:340
  88.8 5.1 %collective-permute-start.18 = (f32[128,128]{1,0:T(8,128)S(1)}, f32[128,128]{1,0:T(8,128)S(1)}, u32[]{:S(2)}, u32[]{:S(2)}) collective-permute-start(f32[128,128]{1,0:T(8,128)S(1)} %join.36.refs_0_), channel_id=1, source_target_pairs={{0,16},{4,20},{8,24},{12,28},{16,0},{20,4},{24,8},{28,12},{1,17},{... | collective-permute-start | bytes 196616 | tf_op jit(solution)/shard_map/ppermute | solution.py:340
  91.3 7.4 %collective-permute-start.15 = (f32[192,128]{1,0:T(8,128)S(1)}, f32[192,128]{1,0:T(8,128)S(1)}, u32[]{:S(2)}, u32[]{:S(2)}) collective-permute-start(f32[192,128]{1,0:T(8,128)S(1)} %join.35.refs_0_), channel_id=1, source_target_pairs={{0,2},{1,3},{2,0},{3,1},{4,6},{5,7},{6,4},{7,5},{8,10},{9,11},{10,... | collective-permute-start | bytes 294920 | tf_op jit(solution)/shard_map/ppermute | solution.py:340
  100.8 5.2 %collective-permute-start.21 = (f32[192,128]{1,0:T(8,128)S(1)}, f32[192,128]{1,0:T(8,128)S(1)}, u32[]{:S(2)}, u32[]{:S(2)}) collective-permute-start(f32[192,128]{1,0:T(8,128)S(1)} %row_sweep.10.refs_0_._), channel_id=1, source_target_pairs={{0,1},{1,0},{2,3},{3,2},{4,5},{5,4},{6,7},{7,6},{8,9},{9,8},{10,11... | collective-permute-start | bytes 294920 | tf_op jit(solution)/shard_map/ppermute | solution.py:340
  102.1 6.3 %collective-permute-start.26 = (f32[128,128]{1,0:T(8,128)S(1)}, f32[128,128]{1,0:T(8,128)S(1)}, u32[]{:S(2)}, u32[]{:S(2)}) collective-permute-start(f32[128,128]{1,0:T(8,128)S(1)} %join.39.refs_0_), channel_id=1, source_target_pairs={{0,24},{4,28},{8,16},{12,20},{16,8},{20,12},{24,0},{28,4},{1,25},{... | collective-permute-start | bytes 196616 | tf_op jit(solution)/shard_map/ppermute | solution.py:340
  106.1 7.4 %collective-permute-start.22 = (f32[192,128]{1,0:T(8,128)S(1)}, f32[192,128]{1,0:T(8,128)S(1)}, u32[]{:S(2)}, u32[]{:S(2)}) collective-permute-start(f32[192,128]{1,0:T(8,128)S(1)} %join.38.refs_0_), channel_id=1, source_target_pairs={{0,2},{1,3},{2,0},{3,1},{4,6},{5,7},{6,4},{7,5},{8,10},{9,11},{10,... | collective-permute-start | bytes 294920 | tf_op jit(solution)/shard_map/ppermute | solution.py:340
  115.6 5.2 %collective-permute-start.28 = (f32[192,128]{1,0:T(8,128)S(1)}, f32[192,128]{1,0:T(8,128)S(1)}, u32[]{:S(2)}, u32[]{:S(2)}) collective-permute-start(f32[192,128]{1,0:T(8,128)S(1)} %row_sweep.11.refs_0_._), channel_id=1, source_target_pairs={{0,1},{1,0},{2,3},{3,2},{4,5},{5,4},{6,7},{7,6},{8,9},{9,8},{10,11... | collective-permute-start | bytes 294920 | tf_op jit(solution)/shard_map/ppermute | solution.py:340
  116.8 6.2 %collective-permute-start.33 = (f32[128,128]{1,0:T(8,128)S(1)}, f32[128,128]{1,0:T(8,128)S(1)}, u32[]{:S(2)}, u32[]{:S(2)}) collective-permute-start(f32[128,128]{1,0:T(8,128)S(1)} %join.42.refs_0_), channel_id=1, source_target_pairs={{0,24},{4,28},{8,16},{12,20},{16,8},{20,12},{24,0},{28,4},{1,25},{... | collective-permute-start | bytes 196616 | tf_op jit(solution)/shard_map/ppermute | solution.py:340
  120.8 7.4 %collective-permute-start.29 = (f32[192,128]{1,0:T(8,128)S(1)}, f32[192,128]{1,0:T(8,128)S(1)}, u32[]{:S(2)}, u32[]{:S(2)}) collective-permute-start(f32[192,128]{1,0:T(8,128)S(1)} %join.41.refs_0_), channel_id=1, source_target_pairs={{0,2},{1,3},{2,0},{3,1},{4,6},{5,7},{6,4},{7,5},{8,10},{9,11},{10,... | collective-permute-start | bytes 294920 | tf_op jit(solution)/shard_map/ppermute | solution.py:340
  130.3 5.2 %collective-permute-start.35 = (f32[192,128]{1,0:T(8,128)S(1)}, f32[192,128]{1,0:T(8,128)S(1)}, u32[]{:S(2)}, u32[]{:S(2)}) collective-permute-start(f32[192,128]{1,0:T(8,128)S(1)} %row_sweep.12.refs_0_._), channel_id=1, source_target_pairs={{0,1},{1,0},{2,3},{3,2},{4,5},{5,4},{6,7},{7,6},{8,9},{9,8},{10,11... | collective-permute-start | bytes 294920 | tf_op jit(solution)/shard_map/ppermute | solution.py:340
  131.5 6.1 %collective-permute-start.40 = (f32[128,128]{1,0:T(8,128)S(1)}, f32[128,128]{1,0:T(8,128)S(1)}, u32[]{:S(2)}, u32[]{:S(2)}) collective-permute-start(f32[128,128]{1,0:T(8,128)S(1)} %join.45.refs_0_), channel_id=1, source_target_pairs={{0,24},{4,28},{8,16},{12,20},{16,8},{20,12},{24,0},{28,4},{1,25},{... | collective-permute-start | bytes 196616 | tf_op jit(solution)/shard_map/ppermute | solution.py:340
  135.5 7.4 %collective-permute-start.36 = (f32[192,128]{1,0:T(8,128)S(1)}, f32[192,128]{1,0:T(8,128)S(1)}, u32[]{:S(2)}, u32[]{:S(2)}) collective-permute-start(f32[192,128]{1,0:T(8,128)S(1)} %join.44.refs_0_), channel_id=1, source_target_pairs={{0,2},{1,3},{2,0},{3,1},{4,6},{5,7},{6,4},{7,5},{8,10},{9,11},{10,... | collective-permute-start | bytes 294920 | tf_op jit(solution)/shard_map/ppermute | solution.py:340
  145.0 5.2 %collective-permute-start.42 = (f32[192,128]{1,0:T(8,128)S(1)}, f32[192,128]{1,0:T(8,128)S(1)}, u32[]{:S(2)}, u32[]{:S(2)}) collective-permute-start(f32[192,128]{1,0:T(8,128)S(1)} %row_sweep.13.refs_0_._), channel_id=1, source_target_pairs={{0,1},{1,0},{2,3},{3,2},{4,5},{5,4},{6,7},{7,6},{8,9},{9,8},{10,11... | collective-permute-start | bytes 294920 | tf_op jit(solution)/shard_map/ppermute | solution.py:340
  146.3 6.0 %collective-permute-start.47 = (f32[128,128]{1,0:T(8,128)S(1)}, f32[128,128]{1,0:T(8,128)S(1)}, u32[]{:S(2)}, u32[]{:S(2)}) collective-permute-start(f32[128,128]{1,0:T(8,128)S(1)} %join.48.refs_0_), channel_id=1, source_target_pairs={{0,24},{4,28},{8,16},{12,20},{16,8},{20,12},{24,0},{28,4},{1,25},{... | collective-permute-start | bytes 196616 | tf_op jit(solution)/shard_map/ppermute | solution.py:340
  150.3 7.4 %collective-permute-start.43 = (f32[192,128]{1,0:T(8,128)S(1)}, f32[192,128]{1,0:T(8,128)S(1)}, u32[]{:S(2)}, u32[]{:S(2)}) collective-permute-start(f32[192,128]{1,0:T(8,128)S(1)} %join.47.refs_0_), channel_id=1, source_target_pairs={{0,2},{1,3},{2,0},{3,1},{4,6},{5,7},{6,4},{7,5},{8,10},{9,11},{10,... | collective-permute-start | bytes 294920 | tf_op jit(solution)/shard_map/ppermute | solution.py:340
  159.7 5.2 %collective-permute-start.49 = (f32[192,128]{1,0:T(8,128)S(1)}, f32[192,128]{1,0:T(8,128)S(1)}, u32[]{:S(2)}, u32[]{:S(2)}) collective-permute-start(f32[192,128]{1,0:T(8,128)S(1)} %row_sweep.14.refs_0_._), channel_id=1, source_target_pairs={{0,1},{1,0},{2,3},{3,2},{4,5},{5,4},{6,7},{7,6},{8,9},{9,8},{10,11... | collective-permute-start | bytes 294920 | tf_op jit(solution)/shard_map/ppermute | solution.py:340
  161.0 5.9 %collective-permute-start.54 = (f32[128,128]{1,0:T(8,128)S(1)}, f32[128,128]{1,0:T(8,128)S(1)}, u32[]{:S(2)}, u32[]{:S(2)}) collective-permute-start(f32[128,128]{1,0:T(8,128)S(1)} %join.51.refs_0_), channel_id=1, source_target_pairs={{0,24},{4,28},{8,16},{12,20},{16,8},{20,12},{24,0},{28,4},{1,25},{... | collective-permute-start | bytes 196616 | tf_op jit(solution)/shard_map/ppermute | solution.py:340
  165.0 7.4 %collective-permute-start.50 = (f32[192,128]{1,0:T(8,128)S(1)}, f32[192,128]{1,0:T(8,128)S(1)}, u32[]{:S(2)}, u32[]{:S(2)}) collective-permute-start(f32[192,128]{1,0:T(8,128)S(1)} %join.50.refs_0_), channel_id=1, source_target_pairs={{0,2},{1,3},{2,0},{3,1},{4,6},{5,7},{6,4},{7,5},{8,10},{9,11},{10,... | collective-permute-start | bytes 294920 | tf_op jit(solution)/shard_map/ppermute | solution.py:340
  174.5 5.2 %collective-permute-start.56 = (f32[192,128]{1,0:T(8,128)S(1)}, f32[192,128]{1,0:T(8,128)S(1)}, u32[]{:S(2)}, u32[]{:S(2)}) collective-permute-start(f32[192,128]{1,0:T(8,128)S(1)} %row_sweep.15.refs_0_._), channel_id=1, source_target_pairs={{0,1},{1,0},{2,3},{3,2},{4,5},{5,4},{6,7},{7,6},{8,9},{9,8},{10,11... | collective-permute-start | bytes 294920 | tf_op jit(solution)/shard_map/ppermute | solution.py:340
  175.7 5.8 %collective-permute-start.61 = (f32[128,128]{1,0:T(8,128)S(1)}, f32[128,128]{1,0:T(8,128)S(1)}, u32[]{:S(2)}, u32[]{:S(2)}) collective-permute-start(f32[128,128]{1,0:T(8,128)S(1)} %join.54.refs_0_), channel_id=1, source_target_pairs={{0,24},{4,28},{8,16},{12,20},{16,8},{20,12},{24,0},{28,4},{1,25},{... | collective-permute-start | bytes 196616 | tf_op jit(solution)/shard_map/ppermute | solution.py:340
  179.7 7.4 %collective-permute-start.57 = (f32[192,128]{1,0:T(8,128)S(1)}, f32[192,128]{1,0:T(8,128)S(1)}, u32[]{:S(2)}, u32[]{:S(2)}) collective-permute-start(f32[192,128]{1,0:T(8,128)S(1)} %join.53.refs_0_), channel_id=1, source_target_pairs={{0,2},{1,3},{2,0},{3,1},{4,6},{5,7},{6,4},{7,5},{8,10},{9,11},{10,... | collective-permute-start | bytes 294920 | tf_op jit(solution)/shard_map/ppermute | solution.py:340
  196.0 5.5 %collective-permute-start.69 = (f32[16,128]{1,0:T(8,128)S(1)}, f32[16,128]{1,0:T(8,128)S(1)}, u32[]{:S(2)}, u32[]{:S(2)}) collective-permute-start(f32[16,128]{1,0:T(8,128)S(1)} %join.57.rest_0_), channel_id=1, source_target_pairs={{0,3},{1,2},{2,1},{3,0},{4,7},{5,6},{6,5},{7,4},{8,11},{9,10},{10,... | collective-permute-start | bytes 24584 | tf_op jit(solution)/shard_map/ppermute | solution.py:340
  (41 other events, 139.9 us)
